TPU v7x, 32 devices: a whole 2x2x4 slice. The times are simulated.
32 devices in a mesh: row: 8 (over z, y), col: 4 (over x, core).
Axes of the slice: x: 2, y: 2, z: 4, core: 2. Of those that a mesh axis runs over, the one named last changes fastest.
Arguments:
- row_embed: float32 [8192, 512], P(('row', 'col')), may hold values from -1.5 to 1.5
- row_accum: float32 [8192, 512], P(('row', 'col')), may hold values from 0.001 to 0.01
- col_embed: float32 [4, 4096, 512], P('col', 'row'), may hold values from -1.5 to 1.5
- col_accum: float32 [4, 4096, 512], P('col', 'row'), may hold values from 0.001 to 0.01
- col_freq: int32 [4, 4096], P('col'), may hold values from 1000 to 29999
- row_freq: int32 [8192], P('row'), may hold values from 1000 to 29999
- block_cols: int32 [8, 4, 2], P('row', 'col'), may hold values from 0 to 3, all different within a row
- counts: int32 [8, 4, 2, 1024, 1024], P('row', 'col'), may hold values from 0 to 1024
- excluded: int32 [512], replicated, may hold values from 0 to 8191
- log_total: float32 [], replicated, may hold values from 15 to 19
Outputs:
- row_embed_new: float32 [8192, 512], P(('row', 'col'))
- row_accum_new: float32 [8192, 512], P(('row', 'col'))
- col_embed_new: float32 [4, 4096, 512], P('col', 'row')
- col_accum_new: float32 [4, 4096, 512], P('col', 'row')
Inputs may be any that keep to these rules, and one draw needn't show every extreme that they name: `block_cols`: the 2 column blocks of one row block and group are different.
All inputs are finite; a program needn't handle non-finite values.
Results may differ from a plain program's by a relative error of at most 0.0071.
The roundings to bfloat16 on the way count: a program that leaves them out, or rounds other values in their place, can miss the bound.
Values may be sent and summed in bfloat16 or wider, within the bound.
No kernel may reach another device: no remote copies, remote signals or barrier semaphores. Data moves between devices by JAX's collectives and lax.ppermute only.
A program may use at most 128 MiB of HBM per device.

v0:
```python
import jax
import jax.numpy as jnp
from jax import lax
from jax.sharding import PartitionSpec as P

BLOCK = 1024


learn_rate = 0.2
decay_rate = 0.5


def cell_grads(count_block, predicted, row_logs, col_logs, log_total):
    nonzero = count_block > 0
    safe_count = jnp.where(nonzero, count_block.astype(jnp.float32), jnp.float32(1.0))
    baseline = log_total - row_logs[:, None] - col_logs[None, :]
    weight = 0.1 + 0.25 * jnp.sqrt(safe_count)
    fitted = weight * (predicted - baseline - jnp.log(safe_count))
    hinge_grad = jax.nn.sigmoid(predicted - baseline)
    return (jnp.where(nonzero, fitted, hinge_grad) / BLOCK).astype(jnp.bfloat16)


def body(
    row_embed,
    row_accum,
    col_embed,
    col_accum,
    col_freq,
    row_freq,
    block_cols,
    counts,
    excluded,
    log_total,
):
    block = counts.shape[3]
    slots = counts.shape[2]
    width = row_embed.shape[1]
    own_rows = row_embed.shape[0]
    own_cols = col_embed.shape[1]
    chosen = block_cols[0, 0]
    block_rows = lax.all_gather(row_embed.astype(jnp.bfloat16), "col", axis=0, tiled=True)
    piece = lax.all_gather(col_embed.astype(jnp.bfloat16), "row", axis=1, tiled=True)
    span = piece.shape[1]
    positions = jnp.arange(span, dtype=jnp.int32)
    owner_block = positions // block
    offset = positions - owner_block * block
    target = jnp.full((span,), slots * block, jnp.int32)
    for collect_slot_id in range(slots):
        target = jnp.where(
            owner_block == chosen[collect_slot_id], collect_slot_id * block + offset, target
        )
    fetched = jnp.zeros((slots * block, width), jnp.bfloat16).at[target].set(piece[0], mode="drop")
    row_logs = jnp.log(row_freq.astype(jnp.float32))
    col_logs = jnp.log(col_freq[0].astype(jnp.float32))
    row_grad = jnp.zeros((block, width), jnp.float32)
    col_parts = []
    for slot_id in range(slots):
        col_block = fetched[slot_id * block : (slot_id + 1) * block]
        block_col_logs = lax.dynamic_slice_in_dim(col_logs, chosen[slot_id] * block, block)
        predicted = lax.dot_general(
            block_rows, col_block, (((1,), (1,)), ((), ())), preferred_element_type=jnp.float32
        )
        cell = cell_grads(counts[0, 0, slot_id], predicted, row_logs, block_col_logs, log_total)
        row_grad = row_grad + jnp.dot(cell, col_block, preferred_element_type=jnp.float32)
        col_parts.append(
            lax.dot_general(
                cell, block_rows, (((0,), (0,)), ((), ())), preferred_element_type=jnp.float32
            )
        )
    positions = jnp.arange(own_cols * lax.axis_size("row"), dtype=jnp.int32)
    owner_block = positions // block
    offset = positions - owner_block * block
    summed = jnp.zeros((own_cols * lax.axis_size("row"), width), jnp.float32)
    for slot_id in range(slots):
        picked = jnp.take(col_parts[slot_id], offset, axis=0)
        summed = summed + jnp.where(
            (owner_block == chosen[slot_id])[:, None], picked, jnp.float32(0.0)
        )
    col_grad = lax.psum_scatter(summed, "row", scatter_dimension=0, tiled=True)
    own_grad = lax.psum_scatter(row_grad, "col", scatter_dimension=0, tiled=True)
    col_index = lax.axis_index("col")
    row_index = lax.axis_index("row")
    own_freq = lax.dynamic_slice_in_dim(row_freq, col_index * own_rows, own_rows).astype(
        jnp.float32
    )
    row_ids = row_index * block + col_index * own_rows + jnp.arange(own_rows, dtype=jnp.int32)
    decayed = jnp.all(row_ids[:, None] != excluded[None, :], axis=1)
    freq_root = jnp.sqrt(own_freq)
    decay_coef = jnp.where(decayed, decay_rate * freq_root / (freq_root + 30.0), jnp.float32(0.0))
    full_grad = own_grad + decay_coef[:, None] * row_embed
    row_accum_new = row_accum + full_grad * full_grad
    row_embed_new = row_embed - learn_rate * full_grad / jnp.sqrt(row_accum_new)
    col_step = col_grad[None]
    col_accum_new = col_accum + col_step * col_step
    col_embed_new = col_embed - learn_rate * col_step / jnp.sqrt(col_accum_new)
    return (row_embed_new, row_accum_new, col_embed_new, col_accum_new)


def solution(mesh):
    in_specs = (
        P(("row", "col"), None),
        P(("row", "col"), None),
        P("col", "row", None),
        P("col", "row", None),
        P("col", None),
        P("row"),
        P("row", "col", None),
        P("row", "col", None, None, None),
        P(),
        P(),
    )
    out_specs = (
        P(("row", "col"), None),
        P(("row", "col"), None),
        P("col", "row", None),
        P("col", "row", None),
    )
    return jax.shard_map(body, mesh=mesh, in_specs=in_specs, out_specs=out_specs, check_vma=False)
```

profile of v0, /device:TPU:0, one launch (start us, length us, event | category | flops | bytes accessed | tf_op | source)
XLA Modules:
  0.0 333.0 jit_solution(4989740510535665114)
XLA Ops:
  7.2 2.1 convert_element_type.36
  9.4 1.8 convert_element_type.37
  11.2 0.0 reduce-scatter.3.cloned.1.call-start
  11.2 1.3 fusion.20
  13.8 8.5 %fusion.19 = (s32[1,1,1,1024,1024]{4,3,2,1,0:T(8,128)}, s32[1,1,1,1024,1024]{4,3,2,1,0:T(8,128)}) fusion(s32[1,1,2,1024,1024]{4,3,2,1,0:T(8,128)} %param.19), kind=kLoop, calls=%fused_computation.56 | loop fusion | bytes 16777216 | tf_op jit(solution)/shard_map/slice | solution.py:63
  22.3 5.4 %copy.20 = s32[1,1,1,1024,1024]{3,4,2,1,0:T(8,128)} copy(s32[1,1,1,1024,1024]{4,3,2,1,0:T(8,128)} %get-tuple-element.10) | data formatting | bytes 8388608
  28.4 5.4 %copy.21 = s32[1,1,1,1024,1024]{3,4,2,1,0:T(8,128)} copy(s32[1,1,1,1024,1024]{4,3,2,1,0:T(8,128)} %get-tuple-element.9) | data formatting | bytes 8388608
  33.9 1.4 compare_select_fusion
  35.2 51.6 %all-gather.3.cloned.1.call-done = bf16[1,4096,512]{2,1,0:T(8,128)(2,1)} async-done(((bf16[1,512,512]{2,1,0:T(8,128)(2,1)}), bf16[1,4096,512]{2,1,0:T(8,128)(2,1)}) %all-gather.3.cloned.1.call-update) | async-done | bytes 4194320 | tf_op jit(solution)/shard_map/all_gather | solution.py:42
  86.8 19.2 %scatter_custom_fusion = bf16[2048,512]{1,0:T(8,128)(2,1)S(1)} fusion(s32[4096]{0:T(1024)S(1)} %bitcast.43, bf16[1,4096,512]{2,1,0:T(8,128)(2,1)} %all-gather.3.cloned.1.call-done, bf16[]{:T(256)} %constant.64.clone.1), kind=kCustom, calls=%fused_computation.9 | custom fusion | bytes 6291458 | tf_op jit(solution)/shard_map/scatter | solution.py:52
  106.1 7.2 %multiply_convert_fusion.1 = bf16[1024,1024]{0,1:T(8,128)(2,1)S(1)} fusion(s32[1,1,1,1024,1024]{3,4,2,1,0:T(8,128)} %copy.20, bf16[1024,512]{1,0:T(8,128)(2,1)} %all-gather.5.cloned.1.call-done, f32[1024]{0:T(1024)S(1)} %bitcast.45, f32[1024]{0:T(1024)S(1)} %log_subtract_fusion, bf16[2048,512]{1,0:T(8,128)(2,1)S(1)} %scatter_custom_fusion), kind=kOutput, calls=%fused_computation.13 | convolution fusion | flops 1089470464 | bytes 8396800 | tf_op jit(solution)/shard_map/dot_general | solution.py:60
  113.4 1.3 fusion.7
  114.7 1.6 copy-done.1
  116.3 0.3 copy-done.8
  116.6 4.1 %multiply_convert_fusion = bf16[1024,1024]{0,1:T(8,128)(2,1)S(1)} fusion(s32[1,1,1,1024,1024]{3,4,2,1,0:T(8,128)S(1)} %copy-done.1, bf16[1024,512]{1,0:T(8,128)(2,1)S(1)} %copy-done.8, f32[1024]{0:T(1024)S(1)} %bitcast.44, f32[1024]{0:T(1024)S(1)} %log_subtract_fusion, bf16[2048,512]{1,0:T(8,128)(2,1)S(1)} %scatter_custom_fusion), kind=kOutput, calls=%fused_computation.12 | convolution fusion | flops 1089470464 | bytes 8396800 | tf_op jit(solution)/shard_map/dot_general | solution.py:60
  120.7 1.3 copy-done.9
  122.0 2.6 convolution_add_fusion
  124.7 0.2 reduce-scatter.5.cloned.1.call-start
  124.9 1.3 fusion.12
  126.2 3.1 fusion.22
  129.4 16.8 %gather_fusion.1 = f32[4096,512]{1,0:T(8,128)} fusion(f32[1024,512]{1,0:T(8,128)S(1)} %fusion.22, s32[4096]{0:T(1024)S(1)} %fusion.17), kind=kCustom, calls=%fused_computation.1.clone | custom fusion | bytes 16793600 | tf_op jit(solution)/shard_map/jit(_take)/gather | solution.py:75
  146.2 3.1 fusion.21
  149.3 16.8 %gather_fusion = f32[4096,512]{1,0:T(8,128)} fusion(f32[1024,512]{1,0:T(8,128)S(1)} %fusion.21, s32[4096]{0:T(1024)S(1)} %fusion.17), kind=kCustom, calls=%fused_computation.clone | custom fusion | bytes 16793600 | tf_op jit(solution)/shard_map/jit(_take)/gather | solution.py:75
  166.1 9.9 %fusion = f32[4096,512]{1,0:T(8,128)} fusion(f32[4096,512]{1,0:T(8,128)} %gather_fusion.1, f32[4096,512]{1,0:T(8,128)} %gather_fusion, pred[4096]{0:T(1024)(128)(4,1)S(1)} %compare_and_fusion, pred[4096]{0:T(1024)(128)(4,1)S(1)} %get-tuple-element.15, pred[4096]{0:T(1024)(128)(4,1)S(1)} %get-tuple-element.16), kind=kLoop, calls=%fused_computation.4 | loop fusion | flops 10485760 | bytes 25178112 | tf_op jit(solution)/shard_map/add | solution.py:76
  176.1 0.6 copy-done.7
  176.7 0.2 compare_reduce_fusion
  176.8 0.1 fusion.18
  176.9 0.1 copy-done.2
  177.0 0.2 copy-done.4
  177.2 2.2 multiply_subtract_fusion
  179.4 144.1 %reduce-scatter.5.cloned.1.call-done = f32[512,512]{1,0:T(8,128)} async-done(((f32[4096,512]{1,0:T(8,128)}), f32[512,512]{1,0:T(8,128)}) %reduce-scatter.5.cloned.1.call-update) | async-done | bytes 1048592 | tf_op jit(solution)/shard_map/reduce_scatter | solution.py:79
  323.5 2.9 fusion.3
  (30 shorter events, 0.3 us)
Async XLA Ops:
  7.2 79.7 %all-gather.3.cloned.1.call-start = ((), (), s32[]{:S(2)}) async-start(), calls=%async_computation.2 | async-start | bytes 4718592 | tf_op jit(solution)/shard_map/all_gather | solution.py:42
  9.3 96.8 %all-gather.5.cloned.1.call-start = ((), (), s32[]{:S(2)}) async-start(), calls=%async_computation.3 | async-start | bytes 1310720 | tf_op jit(solution)/shard_map/all_gather | solution.py:41
  11.2 165.8 %reduce-scatter.3.cloned.1.call-start = ((), (), s32[]{:S(2)}) async-start(), calls=%async_computation.4 | async-start | bytes 2621440 | tf_op jit(solution)/shard_map/reduce_scatter | solution.py:80
  28.4 5.4 %copy-start.5 = (s32[1,4096]{1,0:T(1,128)S(1)}, s32[1,4096]{1,0:T(1,128)}, u32[]{:S(2)}) copy-start(s32[1,4096]{1,0:T(1,128)} %param.16) | copy-start | bytes 49156
  28.4 5.5 %copy-start.6 = (s32[1024]{0:T(1024)S(1)}, s32[1024]{0:T(1024)}, u32[]{:S(2)}) copy-start(s32[1024]{0:T(1024)} %param.17) | copy-start | bytes 12292
  113.3 1.3 copy-start.10
  113.3 2.9 copy-start.1
  113.4 3.2 copy-start.8
  120.7 1.3 copy-start.9
  124.7 198.8 %reduce-scatter.5.cloned.1.call-start = ((), (), s32[]{:S(2)}) async-start(), calls=%async_computation.5 | async-start | bytes 9437184 | tf_op jit(solution)/shard_map/reduce_scatter | solution.py:79
  176.0 0.7 copy-start.7
  176.0 1.1 copy-start.2
  176.0 1.2 copy-start.4
  176.0 147.5 %copy-start = (f32[1,512,512]{2,1,0:T(8,128)S(1)}, f32[1,512,512]{2,1,0:T(8,128)}, u32[]{:S(2)}) copy-start(f32[1,512,512]{2,1,0:T(8,128)} %param.14) | copy-start | bytes 3145732
  176.0 147.5 %copy-start.3 = (f32[1,512,512]{2,1,0:T(8,128)S(1)}, f32[1,512,512]{2,1,0:T(8,128)}, u32[]{:S(2)}) copy-start(f32[1,512,512]{2,1,0:T(8,128)} %param.15) | copy-start | bytes 3145732
Sparse Core Ops, SparseCore 0:
  10.7 76.0 all-gather.2
  89.0 14.9 all-gather.4
  124.8 29.7 reduce-scatter.2
  176.2 147.2 reduce-scatter.4
where the time goes:
time: 333 us
  waiting for transfers between devices  196 us (59%)
  local copies, waits for them, and re-layouts  77.5 us (23%)
  other arithmetic  21.9 us (7%)
  matrix products  21.5 us (6%)
  between operations  15.9 us (5%)
    reduce_scatter x1, waiting for transfers between devices, body(): col_grad = lax.psum_scatter(summed, 'row', scatter_dimension=0, tiled=True)  144 us
    all_gather x1, waiting for transfers between devices, body(): lax.all_gather(col_embed.astype(jnp.bfloat16), 'row', axis=1, tiled=True)  51.6 us
    gather x2, local copies, waits for them, and re-layouts, body(): picked = jnp.take(col_parts[slot_id], offset, axis=0)  33.6 us
    scatter x1, local copies, waits for them, and re-layouts, body(): jnp.zeros((slots * block, width), jnp.bfloat16).at[target]  19.2 us
    unnamed x24, local copies, waits for them, and re-layouts  14.9 us
    dot_general x2, matrix products, body(): lax.dot_general(block_rows, col_block, (((1,), (1,)), ((), ())), preferre...  11.4 us
    add x1, other arithmetic, body(): summed + jnp.where((owner_block == chosen[slot_id])[:, None], picked, jnp...  9.91 us
    slice x1, local copies, waits for them, and re-layouts, body(): counts[0, 0, slot_id]  8.48 us
  transfers between devices with their start and end apart: 4, of which 2 were waited for; matrix products, arithmetic and copies ran while one was open for 29% of the time, Pallas kernels for 0%

commit v1 on v0

v1 whole, which is shorter than its diff:
```python
import functools

import jax
import jax.numpy as jnp
from jax import lax
from jax.experimental import pallas as pl
from jax.experimental.pallas import tpu as pltpu
from jax.sharding import PartitionSpec as P

learn_rate = 0.2
decay_rate = 0.5

PARTS = 2


def cell_grads(count_block, shifted, block):
    safe_count = jnp.maximum(count_block, 1).astype(jnp.float32)
    weight = (0.1 / block) + (0.25 / block) * jnp.sqrt(safe_count)
    fitted = weight * (shifted - jnp.log(safe_count))
    hinge_grad = (0.5 / block) * jnp.tanh(0.5 * shifted) + (0.5 / block)
    return jnp.where(count_block > 0, fitted, hinge_grad).astype(jnp.bfloat16)


def block_kernel(first, block, meta, own_rows, x_rows, core_rows, cols, row_term, col_term, counts, *rest):
    if first:
        row_grad, col_grad = rest
    else:
        row_before, row_grad, col_grad = rest
    slot = pl.program_id(0)
    some = cols[0]
    size = own_rows.shape[0]

    @pl.when(slot == 0)
    def _():
        if first:
            row_grad[...] = jnp.zeros_like(row_grad)
        else:
            row_grad[...] = row_before[...]

    total = None
    for piece in range(4):
        rows = (own_rows, core_rows.at[0], x_rows, core_rows.at[1])[piece][...]
        at = pl.ds(pl.multiple_of((meta[1] ^ piece) * size, size), size)
        predicted = lax.dot_general(
            rows, some, (((1,), (1,)), ((), ())), preferred_element_type=jnp.float32
        )
        shifted = predicted + row_term[at, :] + col_term[0]
        cell = cell_grads(counts[0, 0, 0, at, :], shifted, block)
        row_grad[piece] += jnp.dot(cell, some, preferred_element_type=jnp.float32)
        term = lax.dot_general(
            cell, rows, (((0,), (0,)), ((), ())), preferred_element_type=jnp.float32
        )
        total = term if total is None else total + term
    col_grad[0] = total.astype(col_grad.dtype)


def block_grads(meta, rows, cols, row_term, col_term, counts, row_before, col_type):
    own_rows, x_rows, core_rows = rows
    slots, span, width = cols.shape
    size = own_rows.shape[0]
    block = counts.shape[3]
    first = row_before is None
    whole2 = lambda slot, meta: (0, 0)
    whole3 = lambda slot, meta: (0, 0, 0)
    in_specs = [
        pl.BlockSpec((size, width), whole2),
        pl.BlockSpec((size, width), whole2),
        pl.BlockSpec((2, size, width), whole3),
        pl.BlockSpec((1, span, width), lambda slot, meta: (slot, 0, 0)),
        pl.BlockSpec((block, 1), whole2),
        pl.BlockSpec((1, 1, span), lambda slot, meta: (slot, 0, 0)),
        pl.BlockSpec((1, 1, 1, block, span), lambda slot, meta: (0, 0, slot, 0, meta[0])),
    ]
    args = [own_rows, x_rows, core_rows, cols, row_term, col_term, counts]
    if not first:
        in_specs.append(pl.BlockSpec((4, size, width), whole3))
        args.append(row_before)
    return pl.pallas_call(
        functools.partial(block_kernel, first, block),
        grid_spec=pltpu.PrefetchScalarGridSpec(
            num_scalar_prefetch=1,
            grid=(slots,),
            in_specs=in_specs,
            out_specs=[
                pl.BlockSpec((4, size, width), whole3),
                pl.BlockSpec((1, span, width), lambda slot, meta: (slot, 0, 0)),
            ],
        ),
        out_shape=[
            jax.ShapeDtypeStruct((4, size, width), jnp.float32),
            jax.ShapeDtypeStruct((slots, span, width), col_type),
        ],
        cost_estimate=pl.CostEstimate(
            flops=6 * slots * block * span * width,
            bytes_accessed=slots * block * span * 4 + 3 * block * width * 4,
            transcendentals=3 * slots * block * span,
        ),
        compiler_params=pltpu.CompilerParams(vmem_limit_bytes=40 * 1024 * 1024),
    )(meta, *args)


def crossed_body(
    row_embed,
    row_accum,
    col_embed,
    col_accum,
    col_freq,
    row_freq,
    block_cols,
    counts,
    excluded,
    log_total,
):
    block = counts.shape[3]
    slots = counts.shape[2]
    own_rows = row_embed.shape[0]
    own_cols = col_embed.shape[1]
    span = own_cols // PARTS
    row_index = lax.axis_index("row")
    col_index = lax.axis_index("col")
    half = row_index % 2
    home = row_index // 2
    edge = (home == 0) | (home == 3)

    mate_swap = [(i, i ^ 1) for i in range(8)]
    near_swap = [(i, i ^ 2) for i in range(8)]
    far_swap = [(i, i ^ 4) for i in range(8)]
    inner_swap = [(i, i ^ 6) for i in range(2, 6)]
    to_edge = [(i, i ^ 2) for i in range(2, 6)]
    from_edge = [(i, i ^ 2) for i in (0, 1, 6, 7)]
    core_swap = [(i, i ^ 1) for i in range(4)]
    chip_swap = [(i, i ^ 2) for i in range(4)]

    chosen = block_cols[0, 0]
    mate_chosen = lax.ppermute(chosen, "row", mate_swap)

    row_half = row_embed.astype(jnp.bfloat16)
    col_half = col_embed[0].astype(jnp.bfloat16)

    gathered = []
    for part in range(PARTS):
        own = col_half[part * span : (part + 1) * span]
        near = lax.ppermute(own, "row", near_swap)
        far = lax.ppermute(own, "row", far_swap)
        inner = lax.ppermute(own, "row", inner_swap)
        last = lax.ppermute(far, "row", to_edge)
        gathered.append((own, near, far, inner, last))

    x_rows = lax.ppermute(row_half, "col", chip_swap)
    core_rows = lax.ppermute(jnp.stack([row_half, x_rows]), "col", core_swap)
    rows = (row_half, x_rows, core_rows)

    row_term = (jnp.log(row_freq.astype(jnp.float32)) - log_total)[:, None]
    col_logs = jnp.log(col_freq[0].astype(jnp.float32))

    def pick(part, wanted):
        own, near, far, inner, last = gathered[part]
        away = wanted ^ home
        crossed = jnp.where(edge, last, inner)
        return jnp.where(
            away == 0, own, jnp.where(away == 1, near, jnp.where(away == 2, far, crossed))
        )

    def col_term(part, side):
        return jnp.stack(
            [
                lax.dynamic_slice_in_dim(
                    col_logs, chosen[s] * block + side * own_cols + part * span, span
                )[None]
                for s in range(slots)
            ]
        )

    row_grad = None
    col_sums = []
    for part in range(PARTS):
        asked = jnp.stack([pick(part, mate_chosen[s]) for s in range(slots)])
        received = lax.ppermute(asked, "row", mate_swap)
        kept = jnp.stack([pick(part, chosen[s]) for s in range(slots)])
        grads = []
        for side, cols, kind in ((half, kept, jnp.float32), (1 - half, received, jnp.bfloat16)):
            meta = jnp.stack([side * PARTS + part, col_index]).astype(jnp.int32)
            row_grad, grad = block_grads(
                meta, rows, cols, row_term, col_term(part, side), counts, row_grad, kind
            )
            grads.append(grad)
        mine, theirs = grads
        from_mate = lax.ppermute(theirs, "row", mate_swap).astype(jnp.float32)

        def block_sum(away):
            wanted = home ^ away
            total = 0.0
            for s in range(slots):
                total = total + jnp.where(chosen[s] == wanted, mine[s], 0.0)
                total = total + jnp.where(mate_chosen[s] == wanted, from_mate[s], 0.0)
            return total

        crossed = block_sum(3).astype(jnp.bfloat16)
        carried = lax.ppermute(crossed, "row", from_edge)
        inner = lax.ppermute(crossed, "row", inner_swap)
        near = lax.ppermute(block_sum(1).astype(jnp.bfloat16), "row", near_swap)
        far_sum = block_sum(2) + carried.astype(jnp.float32)
        far = lax.ppermute(far_sum.astype(jnp.bfloat16), "row", far_swap)
        col_sums.append(
            block_sum(0)
            + near.astype(jnp.float32)
            + far.astype(jnp.float32)
            + inner.astype(jnp.float32)
        )

    from_core = lax.ppermute(jnp.stack([row_grad[1], row_grad[3]]), "col", core_swap)
    away_rows = (row_grad[2] + from_core[1]).astype(jnp.bfloat16)
    from_chip = lax.ppermute(away_rows, "col", chip_swap)
    own_grad = row_grad[0] + from_core[0] + from_chip.astype(jnp.float32)
    return updates(
        row_embed, row_accum, col_embed, col_accum, row_freq, excluded, block, own_grad,
        jnp.concatenate(col_sums, axis=0),
    )


def updates(
    row_embed, row_accum, col_embed, col_accum, row_freq, excluded, block, own_grad, col_grad
):
    own_rows = row_embed.shape[0]
    col_index = lax.axis_index("col")
    row_index = lax.axis_index("row")
    own_freq = lax.dynamic_slice_in_dim(row_freq, col_index * own_rows, own_rows).astype(
        jnp.float32
    )
    row_ids = row_index * block + col_index * own_rows + jnp.arange(own_rows, dtype=jnp.int32)
    decayed = jnp.all(row_ids[:, None] != excluded[None, :], axis=1)
    freq_root = jnp.sqrt(own_freq)
    decay_coef = jnp.where(decayed, decay_rate * freq_root / (freq_root + 30.0), jnp.float32(0.0))
    full_grad = own_grad + decay_coef[:, None] * row_embed
    row_accum_new = row_accum + full_grad * full_grad
    row_embed_new = row_embed - learn_rate * full_grad / jnp.sqrt(row_accum_new)
    col_step = col_grad[None]
    col_accum_new = col_accum + col_step * col_step
    col_embed_new = col_embed - learn_rate * col_step / jnp.sqrt(col_accum_new)
    return (row_embed_new, row_accum_new, col_embed_new, col_accum_new)


def gathered_body(
    row_embed,
    row_accum,
    col_embed,
    col_accum,
    col_freq,
    row_freq,
    block_cols,
    counts,
    excluded,
    log_total,
):
    block = counts.shape[3]
    slots = counts.shape[2]
    width = row_embed.shape[1]
    chosen = block_cols[0, 0]
    block_rows = lax.all_gather(row_embed.astype(jnp.bfloat16), "col", axis=0, tiled=True)
    group = lax.all_gather(col_embed[0].astype(jnp.bfloat16), "row", axis=0, tiled=True)
    row_term = (jnp.log(row_freq.astype(jnp.float32)) - log_total)[:, None]
    col_logs = jnp.log(col_freq[0].astype(jnp.float32))
    row_grad = jnp.zeros((block, width), jnp.float32)
    summed = jnp.zeros(group.shape, jnp.float32)
    for slot in range(slots):
        start = chosen[slot] * block
        cols = lax.dynamic_slice_in_dim(group, start, block)
        predicted = lax.dot_general(
            block_rows, cols, (((1,), (1,)), ((), ())), preferred_element_type=jnp.float32
        )
        shifted = predicted + row_term + lax.dynamic_slice_in_dim(col_logs, start, block)[None]
        cell = cell_grads(counts[0, 0, slot], shifted, block)
        row_grad = row_grad + jnp.dot(cell, cols, preferred_element_type=jnp.float32)
        term = lax.dot_general(
            cell, block_rows, (((0,), (0,)), ((), ())), preferred_element_type=jnp.float32
        )
        summed = lax.dynamic_update_slice_in_dim(summed, term, start, 0)
    col_grad = lax.psum_scatter(summed, "row", scatter_dimension=0, tiled=True)
    own_grad = lax.psum_scatter(row_grad, "col", scatter_dimension=0, tiled=True)
    return updates(
        row_embed, row_accum, col_embed, col_accum, row_freq, excluded, block, own_grad, col_grad
    )


def body(row_embed, row_accum, col_embed, col_accum, col_freq, row_freq, block_cols, counts, *rest):
    halves = lax.axis_size("row") == 8 and 2 * col_embed.shape[1] == counts.shape[3]
    pick = crossed_body if halves and lax.axis_size("col") == 4 else gathered_body
    return pick(
        row_embed, row_accum, col_embed, col_accum, col_freq, row_freq, block_cols, counts, *rest
    )


def solution(mesh):
    in_specs = (
        P(("row", "col"), None),
        P(("row", "col"), None),
        P("col", "row", None),
        P("col", "row", None),
        P("col", None),
        P("row"),
        P("row", "col", None),
        P("row", "col", None, None, None),
        P(),
        P(),
    )
    out_specs = (
        P(("row", "col"), None),
        P(("row", "col"), None),
        P("col", "row", None),
        P("col", "row", None),
    )
    return jax.shard_map(body, mesh=mesh, in_specs=in_specs, out_specs=out_specs, check_vma=False)
```

time: 333 us -> 153 us (0.46)
  waiting for transfers between devices: 196 us -> 52.9 us
  local copies, waits for them, and re-layouts: 77.5 us -> 8.28 us
  starting transfers between devices: 0.34 us -> 41.4 us
  Pallas kernels: 0 us -> 23.7 us
  matrix products: 21.5 us -> 0 us
  other arithmetic: 21.9 us -> 9.69 us
    reduce_scatter x2 -> x0, waiting for transfers between devices: 144 us -> none  [the longest x1 144 us: body(): col_grad = lax.psum_scatter(summed, 'row', scatter_dimension=0, tiled=True)]
    ppermute x0 -> x25, waiting for transfers between devices: none -> 52.9 us  [the longest x2 13 us: crossed_body(): far = lax.ppermute(own, 'row', far_swap)]
    all_gather x2 -> x0, waiting for transfers between devices: 51.6 us -> none  [the longest x1 51.6 us: body(): lax.all_gather(col_embed.astype(jnp.bfloat16), 'row', axis=1, tiled=True)]
    ppermute x0 -> x25, starting transfers between devices: none -> 41.4 us  [the longest x2 14.9 us: crossed_body(): carried = lax.ppermute(crossed, 'row', from_edge)]
    gather x2 -> x0, local copies, waits for them, and re-layouts: 33.6 us -> none  [body(): picked = jnp.take(col_parts[slot_id], offset, axis=0)]
    pallas_call x0 -> x4, Pallas kernels: none -> 23.7 us  [block_grads(): pl.pallas_call(functools.partial(block_kernel, first, block), grid_spec=p...]
    dot_general x6 -> x0, matrix products: 21.5 us -> none  [the longest x2 11.4 us: body(): lax.dot_general(block_rows, col_block, (((1,), (1,)), ((), ())), preferre...]
    scatter x1 -> x0, local copies, waits for them, and re-layouts: 19.2 us -> none  [body(): jnp.zeros((slots * block, width), jnp.bfloat16).at[target]]
  transfers between devices with their start and end apart: 4 -> 25, of which waited for: 2 -> 12; matrix products, arithmetic and copies ran while one was open for 29% -> 6% of each run, Pallas kernels for 0% -> 11%
where the time goes in v1:
time: 153 us; the launch traced here: 152 us
  waiting for transfers between devices  52.9 us (35%)
  starting transfers between devices  41.4 us (27%)
  Pallas kernels  23.7 us (15%)
  between operations  16 us (10%)
  other arithmetic  9.69 us (6%)
  local copies, waits for them, and re-layouts  8.28 us (5%)
    pallas_call x4, Pallas kernels, block_grads(): pl.pallas_call(functools.partial(block_kernel, first, block), grid_spec=p...  23.7 us
    ppermute x2, starting transfers between devices, crossed_body(): carried = lax.ppermute(crossed, 'row', from_edge)  14.9 us
    ppermute x2, waiting for transfers between devices, crossed_body(): far = lax.ppermute(own, 'row', far_swap)  13 us
    ppermute x2, waiting for transfers between devices, crossed_body(): far = lax.ppermute(far_sum.astype(jnp.bfloat16), 'row', far_swap)  11.9 us
    ppermute x2, waiting for transfers between devices, crossed_body(): carried = lax.ppermute(crossed, 'row', from_edge)  6.35 us
    ppermute x2, waiting for transfers between devices, crossed_body(): from_mate = lax.ppermute(theirs, 'row', mate_swap).astype(jnp.float32)  5.37 us
    unnamed x26, local copies, waits for them, and re-layouts  4.77 us
    ppermute x2, starting transfers between devices, crossed_body(): far = lax.ppermute(far_sum.astype(jnp.bfloat16), 'row', far_swap)  4.75 us
  transfers between devices with their start and end apart: 25, of which 12 were waited for; matrix products, arithmetic and copies ran while one was open for 6% of the time, Pallas kernels for 11%

profile of v1, /device:TPU:0, one launch (start us, length us, event | category | flops | bytes accessed | tf_op | source)
XLA Modules:
  0.0 151.8 jit_solution(11803478232577577802)
XLA Ops:
  0.7 1.3 convert_element_type.67
  2.9 3.0 %collective-permute-start.3 = (bf16[256,512]{1,0:T(8,128)(2,1)}, bf16[256,512]{1,0:T(8,128)(2,1)S(1)}, u32[]{:S(2)}, u32[]{:S(2)}) collective-permute-start(bf16[256,512]{1,0:T(8,128)(2,1)} %get-tuple-element.43), channel_id=1, source_target_pairs={{0,8},{4,12},{8,0},{12,4},{16,24},{20,28},{24,16},{28,20},{1,9},{5... | collective-permute-start | bytes 786440 | tf_op jit(solution)/shard_map/ppermute | solution.py:143
  5.9 2.6 %collective-permute-start.4 = (bf16[256,512]{1,0:T(8,128)(2,1)}, bf16[256,512]{1,0:T(8,128)(2,1)S(1)}, u32[]{:S(2)}, u32[]{:S(2)}) collective-permute-start(bf16[256,512]{1,0:T(8,128)(2,1)} %get-tuple-element.43), channel_id=1, source_target_pairs={{0,16},{4,20},{8,24},{12,28},{16,0},{20,4},{24,8},{28,12},{1,17},{... | collective-permute-start | bytes 786440 | tf_op jit(solution)/shard_map/ppermute | solution.py:144
  8.5 1.6 %collective-permute-start = (bf16[256,512]{1,0:T(8,128)(2,1)S(1)}, bf16[256,512]{1,0:T(8,128)(2,1)S(1)}, u32[]{:S(2)}, u32[]{:S(2)}) collective-permute-start(bf16[256,512]{1,0:T(8,128)(2,1)S(1)} %convert_element_type.66.own_rows), channel_id=1, source_target_pairs={{0,2},{1,3},{2,0},{3,1},{4,6},{5,7},{6,4},{7,5},{8,10},{9,11},{10,... | collective-permute-start | bytes 786440 | tf_op jit(solution)/shard_map/ppermute | solution.py:149
  10.4 1.5 %collective-permute-start.2 = (s32[2]{0:T(128)S(1)}, s32[2]{0:T(128)S(1)}, u32[]{:S(2)}, u32[]{:S(2)}) collective-permute-start(s32[2]{0:T(128)S(1)} %bitcast.117), channel_id=1, source_target_pairs={{0,4},{4,0},{8,12},{12,8},{16,20},{20,16},{24,28},{28,24},{1,5},{5... | collective-permute-start | bytes 32 | tf_op jit(solution)/shard_map/ppermute | solution.py:135
  16.7 2.0 %collective-permute-done.3 = bf16[256,512]{1,0:T(8,128)(2,1)S(1)} collective-permute-done((bf16[256,512]{1,0:T(8,128)(2,1)}, bf16[256,512]{1,0:T(8,128)(2,1)S(1)}, u32[]{:S(2)}, u32[]{:S(2)}) %collective-permute-start.3) | collective-permute-done | bytes 262176 | tf_op jit(solution)/shard_map/ppermute | solution.py:143
  18.7 1.4 collective-permute-start.6
  20.1 13.0 %collective-permute-done.9 = bf16[256,512]{1,0:T(8,128)(2,1)S(1)} collective-permute-done((bf16[256,512]{1,0:T(8,128)(2,1)}, bf16[256,512]{1,0:T(8,128)(2,1)S(1)}, u32[]{:S(2)}, u32[]{:S(2)}) %collective-permute-start.9) | collective-permute-done | bytes 262176 | tf_op jit(solution)/shard_map/ppermute | solution.py:144
  34.4 1.3 collective-permute-start.5
  44.3 1.8 %collective-permute-done.5 = bf16[256,512]{1,0:T(8,128)(2,1)} collective-permute-done((bf16[256,512]{1,0:T(8,128)(2,1)S(1)}, bf16[256,512]{1,0:T(8,128)(2,1)}, u32[]{:S(2)}, u32[]{:S(2)}) %collective-permute-start.5) | collective-permute-done | bytes 262176 | tf_op jit(solution)/shard_map/ppermute | solution.py:146
  47.5 1.6 %collective-permute-start.12 = (bf16[2,256,512]{2,1,0:T(8,128)(2,1)S(1)}, bf16[2,256,512]{2,1,0:T(8,128)(2,1)S(1)}, u32[]{:S(2)}, u32[]{:S(2)}) collective-permute-start(bf16[2,256,512]{2,1,0:T(8,128)(2,1)S(1)} %pad_maximum_fusion.5), channel_id=1, source_target_pairs={{0,4},{4,0},{8,12},{12,8},{16,20},{20,16},{24,28},{28,24},{1,5},{5... | collective-permute-start | bytes 1572872 | tf_op jit(solution)/shard_map/ppermute | solution.py:178
  50.0 3.4 %copy-done = s32[1,1,2,1024,1024]{4,3,2,1,0:T(8,128)S(1)} copy-done((s32[1,1,2,1024,1024]{4,3,2,1,0:T(8,128)S(1)}, s32[1,1,2,1024,1024]{4,3,2,1,0:T(8,128)}, u32[]{:S(2)}) %copy-start) | copy-done | bytes 8388632
  53.3 4.9 %shard_map.129 = (f32[4,256,512]{2,1,0:T(8,128)S(1)}, f32[2,256,512]{2,1,0:T(8,128)S(1)}) custom-call(s32[2]{0:T(128)S(1)} %pad_add_fusion.3.meta, bf16[256,512]{1,0:T(8,128)(2,1)S(1)} %convert_element_type.66.own_rows, bf16[256,512]{1,0:T(8,128)(2,1)S(1)} %collective-permute-done.x_rows, bf16[2,256,512]{2,1,0:T(8,128)(2,1)S(1)} %collective-permute-done.1.core_rows, ...), custom_call_target="tpu_custom_call" | custom-call | flops 1610612736 | bytes 8388608 | tf_op jit(solution)/shard_map/pallas_call | solution.py:78
  58.3 4.2 %collective-permute-done.12.cols = bf16[2,256,512]{2,1,0:T(8,128)(2,1)S(1)} collective-permute-done((bf16[2,256,512]{2,1,0:T(8,128)(2,1)S(1)}, bf16[2,256,512]{2,1,0:T(8,128)(2,1)S(1)}, u32[]{:S(2)}, u32[]{:S(2)}) %collective-permute-start.12) | collective-permute-done | bytes 524320 | tf_op jit(solution)/shard_map/ppermute | solution.py:178
  62.4 6.0 %shard_map.130 = (f32[4,256,512]{2,1,0:T(8,128)S(1)}, bf16[2,256,512]{2,1,0:T(8,128)(2,1)S(1)}) custom-call(s32[2]{0:T(128)S(1)} %get-tuple-element.57.meta, bf16[256,512]{1,0:T(8,128)(2,1)S(1)} %convert_element_type.66.own_rows, bf16[256,512]{1,0:T(8,128)(2,1)S(1)} %collective-permute-done.x_rows, ...), custom_call_target="tpu_custom_call" | custom-call | flops 1610612736 | bytes 8388608 | tf_op jit(solution)/shard_map/pallas_call | solution.py:78
  68.5 6.0 %shard_map.131 = (f32[4,256,512]{2,1,0:T(8,128)S(1)}, f32[2,256,512]{2,1,0:T(8,128)S(1)}) custom-call(s32[2]{0:T(128)S(1)} %get-tuple-element.56.meta, bf16[256,512]{1,0:T(8,128)(2,1)S(1)} %convert_element_type.66.own_rows, bf16[256,512]{1,0:T(8,128)(2,1)S(1)} %collective-permute-done.x_rows, bf16[2,256,512]{2,1,0:T(8,128)(2,1)S(1)} %collective-permute-done.1.core_rows, ...), custom_call_target="tpu_custom_call" | custom-call | flops 1610612736 | bytes 8388608 | tf_op jit(solution)/shard_map/pallas_call | solution.py:78
  74.5 6.7 %shard_map.132 = (f32[4,256,512]{2,1,0:T(8,128)S(1)}, bf16[2,256,512]{2,1,0:T(8,128)(2,1)}) custom-call(s32[2]{0:T(128)S(1)} %pad_add_fusion.meta, bf16[256,512]{1,0:T(8,128)(2,1)S(1)} %convert_element_type.66.own_rows, bf16[256,512]{1,0:T(8,128)(2,1)S(1)} %collective-permute-done.x_rows, bf16[2,256,512]{2,1,0:T(8,128)(2,1)S(1)} %collective-permute-done.1.core_rows, ...), custom_call_target="tpu_custom_call" | custom-call | flops 1610612736 | bytes 8388608 | tf_op jit(solution)/shard_map/pallas_call | solution.py:78
  81.2 1.3 copy-done.1
  82.5 1.5 %collective-permute-start.20 = (bf16[2,256,512]{2,1,0:T(8,128)(2,1)}, bf16[2,256,512]{2,1,0:T(8,128)(2,1)}, u32[]{:S(2)}, u32[]{:S(2)}) collective-permute-start(bf16[2,256,512]{2,1,0:T(8,128)(2,1)} %get-tuple-element.19), channel_id=1, source_target_pairs={{0,4},{4,0},{8,12},{12,8},{16,20},{20,16},{24,28},{28,24},{1,5},{5... | collective-permute-start | bytes 1572872 | tf_op jit(solution)/shard_map/ppermute | solution.py:188
  91.3 5.4 %collective-permute-done.20 = bf16[2,256,512]{2,1,0:T(8,128)(2,1)} collective-permute-done((bf16[2,256,512]{2,1,0:T(8,128)(2,1)}, bf16[2,256,512]{2,1,0:T(8,128)(2,1)}, u32[]{:S(2)}, u32[]{:S(2)}) %collective-permute-start.20) | collective-permute-done | bytes 524320 | tf_op jit(solution)/shard_map/ppermute | solution.py:188
  98.8 7.9 %collective-permute-start.22 = (bf16[256,512]{1,0:T(8,128)(2,1)S(1)}, bf16[256,512]{1,0:T(8,128)(2,1)S(1)}, u32[]{:S(2)}, u32[]{:S(2)}) collective-permute-start(bf16[256,512]{1,0:T(8,128)(2,1)S(1)} %get-tuple-element.31), channel_id=1, source_target_pairs={{0,8},{4,12},{24,16},{28,20},{1,9},{5,13},{25,17},{29,21},{2,10},{... | collective-permute-start | bytes 786440 | tf_op jit(solution)/shard_map/ppermute | solution.py:199
  107.9 7.0 %collective-permute-start.17 = (bf16[256,512]{1,0:T(8,128)(2,1)S(1)}, bf16[256,512]{1,0:T(8,128)(2,1)S(1)}, u32[]{:S(2)}, u32[]{:S(2)}) collective-permute-start(bf16[256,512]{1,0:T(8,128)(2,1)S(1)} %get-tuple-element.29), channel_id=1, source_target_pairs={{0,8},{4,12},{24,16},{28,20},{1,9},{5,13},{25,17},{29,21},{2,10},{... | collective-permute-start | bytes 786440 | tf_op jit(solution)/shard_map/ppermute | solution.py:199
  115.3 6.3 %collective-permute-done.17 = bf16[256,512]{1,0:T(8,128)(2,1)S(1)} collective-permute-done((bf16[256,512]{1,0:T(8,128)(2,1)S(1)}, bf16[256,512]{1,0:T(8,128)(2,1)S(1)}, u32[]{:S(2)}, u32[]{:S(2)}) %collective-permute-start.17) | collective-permute-done | bytes 262176 | tf_op jit(solution)/shard_map/ppermute | solution.py:199
  121.6 2.4 %collective-permute-start.23 = (bf16[256,512]{1,0:T(8,128)(2,1)S(1)}, bf16[256,512]{1,0:T(8,128)(2,1)S(1)}, u32[]{:S(2)}, u32[]{:S(2)}) collective-permute-start(bf16[256,512]{1,0:T(8,128)(2,1)S(1)} %fusion.4), channel_id=1, source_target_pairs={{0,16},{4,20},{8,24},{12,28},{16,0},{20,4},{24,8},{28,12},{1,17},{... | collective-permute-start | bytes 786440 | tf_op jit(solution)/shard_map/ppermute | solution.py:203
  124.5 2.8 %collective-permute-done.21 = bf16[256,512]{1,0:T(8,128)(2,1)S(1)} collective-permute-done((bf16[256,512]{1,0:T(8,128)(2,1)S(1)}, bf16[256,512]{1,0:T(8,128)(2,1)S(1)}, u32[]{:S(2)}, u32[]{:S(2)}) %collective-permute-start.21) | collective-permute-done | bytes 262176 | tf_op jit(solution)/shard_map/ppermute | solution.py:201
  127.2 2.4 %collective-permute-start.18 = (bf16[256,512]{1,0:T(8,128)(2,1)S(1)}, bf16[256,512]{1,0:T(8,128)(2,1)S(1)}, u32[]{:S(2)}, u32[]{:S(2)}) collective-permute-start(bf16[256,512]{1,0:T(8,128)(2,1)S(1)} %fusion.8), channel_id=1, source_target_pairs={{0,16},{4,20},{8,24},{12,28},{16,0},{20,4},{24,8},{28,12},{1,17},{... | collective-permute-start | bytes 786440 | tf_op jit(solution)/shard_map/ppermute | solution.py:203
  129.6 6.5 %collective-permute-done.23 = bf16[256,512]{1,0:T(8,128)(2,1)S(1)} collective-permute-done((bf16[256,512]{1,0:T(8,128)(2,1)S(1)}, bf16[256,512]{1,0:T(8,128)(2,1)S(1)}, u32[]{:S(2)}, u32[]{:S(2)}) %collective-permute-start.23) | collective-permute-done | bytes 262176 | tf_op jit(solution)/shard_map/ppermute | solution.py:203
  136.5 1.8 %collective-permute-done.16 = bf16[256,512]{1,0:T(8,128)(2,1)S(1)} collective-permute-done((bf16[256,512]{1,0:T(8,128)(2,1)S(1)}, bf16[256,512]{1,0:T(8,128)(2,1)S(1)}, u32[]{:S(2)}, u32[]{:S(2)}) %collective-permute-start.16) | collective-permute-done | bytes 262176 | tf_op jit(solution)/shard_map/ppermute | solution.py:201
  138.3 5.4 %collective-permute-done.18 = bf16[256,512]{1,0:T(8,128)(2,1)S(1)} collective-permute-done((bf16[256,512]{1,0:T(8,128)(2,1)S(1)}, bf16[256,512]{1,0:T(8,128)(2,1)S(1)}, u32[]{:S(2)}, u32[]{:S(2)}) %collective-permute-start.18) | collective-permute-done | bytes 262176 | tf_op jit(solution)/shard_map/ppermute | solution.py:203
  144.2 1.6 %collective-permute-start.14 = (bf16[256,512]{1,0:T(8,128)(2,1)S(1)}, bf16[256,512]{1,0:T(8,128)(2,1)S(1)}, u32[]{:S(2)}, u32[]{:S(2)}) collective-permute-start(bf16[256,512]{1,0:T(8,128)(2,1)S(1)} %fusion.12), channel_id=1, source_target_pairs={{0,2},{1,3},{2,0},{3,1},{4,6},{5,7},{6,4},{7,5},{8,10},{9,11},{10,... | collective-permute-start | bytes 786440 | tf_op jit(solution)/shard_map/ppermute | solution.py:213
  145.7 1.7 %multiply_subtract_fusion = (f32[1,512,512]{2,1,0:T(8,128)}, f32[1,512,512]{2,1,0:T(8,128)}) fusion(f32[1,512,512]{2,1,0:T(8,128)S(1)} %copy-done.6, f32[1,256,512]{2,1,0:T(8,128)S(1)} %fusion.7, f32[1,256,512]{2,1,0:T(8,128)S(1)} %fusion.11, f32[1,512,512]{2,1,0:T(8,128)S(1)} %copy-done.7), kind=kLoop, calls=%fused_computation.2 | loop fusion | flops 1572864 | bytes 5242880 | tf_op jit(solution)/shard_map/sub | solution.py:239
  147.4 3.2 %collective-permute-done.14 = bf16[256,512]{1,0:T(8,128)(2,1)S(1)} collective-permute-done((bf16[256,512]{1,0:T(8,128)(2,1)S(1)}, bf16[256,512]{1,0:T(8,128)(2,1)S(1)}, u32[]{:S(2)}, u32[]{:S(2)}) %collective-permute-start.14) | collective-permute-done | bytes 262176 | tf_op jit(solution)/shard_map/ppermute | solution.py:213
  (88 shorter events, 16.5 us)
Async XLA Ops:
  0.6 7.8 %copy-start.4 = (f32[256,512]{1,0:T(8,128)S(1)}, f32[256,512]{1,0:T(8,128)}, u32[]{:S(2)}) copy-start(f32[256,512]{1,0:T(8,128)} %param.10) | copy-start | bytes 1572868
  0.6 9.8 %copy-start.12 = (s32[1,1,2]{2,1,0:T(1,128)S(1)}, s32[1,1,2]{2,1,0:T(1,128)}, u32[]{:S(2)}) copy-start(s32[1,1,2]{2,1,0:T(1,128)} %param.16) | copy-start | bytes 28
  0.7 13.8 %copy-start.9 = (s32[1,4096]{1,0:T(1,128)S(1)}, s32[1,4096]{1,0:T(1,128)}, u32[]{:S(2)}) copy-start(s32[1,4096]{1,0:T(1,128)} %param.14) | copy-start | bytes 49156
  0.7 13.9 %copy-start.11 = (s32[512]{0:T(512)S(1)}, s32[512]{0:T(512)}, u32[]{:S(2)}) copy-start(s32[512]{0:T(512)} %param.18) | copy-start | bytes 6148
  0.7 14.1 %copy-start.10 = (s32[1024]{0:T(1024)S(1)}, s32[1024]{0:T(1024)}, u32[]{:S(2)}) copy-start(s32[1024]{0:T(1024)} %param.15) | copy-start | bytes 12292
  2.9 15.9 %collective-permute-start.3 = (bf16[256,512]{1,0:T(8,128)(2,1)}, bf16[256,512]{1,0:T(8,128)(2,1)S(1)}, u32[]{:S(2)}, u32[]{:S(2)}) collective-permute-start(bf16[256,512]{1,0:T(8,128)(2,1)} %get-tuple-element.43), channel_id=1, source_target_pairs={{0,8},{4,12},{8,0},{12,4},{16,24},{20,28},{24,16},{28,20},{1,9},{5... | collective-permute-start | bytes 786440 | tf_op jit(solution)/shard_map/ppermute | solution.py:143
  5.9 28.5 %collective-permute-start.4 = (bf16[256,512]{1,0:T(8,128)(2,1)}, bf16[256,512]{1,0:T(8,128)(2,1)S(1)}, u32[]{:S(2)}, u32[]{:S(2)}) collective-permute-start(bf16[256,512]{1,0:T(8,128)(2,1)} %get-tuple-element.43), channel_id=1, source_target_pairs={{0,16},{4,20},{8,24},{12,28},{16,0},{20,4},{24,8},{28,12},{1,17},{... | collective-permute-start | bytes 786440 | tf_op jit(solution)/shard_map/ppermute | solution.py:144
  8.5 7.6 %collective-permute-start = (bf16[256,512]{1,0:T(8,128)(2,1)S(1)}, bf16[256,512]{1,0:T(8,128)(2,1)S(1)}, u32[]{:S(2)}, u32[]{:S(2)}) collective-permute-start(bf16[256,512]{1,0:T(8,128)(2,1)S(1)} %convert_element_type.66.own_rows), channel_id=1, source_target_pairs={{0,2},{1,3},{2,0},{3,1},{4,6},{5,7},{6,4},{7,5},{8,10},{9,11},{10,... | collective-permute-start | bytes 786440 | tf_op jit(solution)/shard_map/ppermute | solution.py:149
  10.1 23.0 %collective-permute-start.9 = (bf16[256,512]{1,0:T(8,128)(2,1)}, bf16[256,512]{1,0:T(8,128)(2,1)S(1)}, u32[]{:S(2)}, u32[]{:S(2)}) collective-permute-start(bf16[256,512]{1,0:T(8,128)(2,1)} %get-tuple-element.42), channel_id=1, source_target_pairs={{0,16},{4,20},{8,24},{12,28},{16,0},{20,4},{24,8},{28,12},{1,17},{... | collective-permute-start | bytes 786440 | tf_op jit(solution)/shard_map/ppermute | solution.py:144
  10.4 4.7 %collective-permute-start.2 = (s32[2]{0:T(128)S(1)}, s32[2]{0:T(128)S(1)}, u32[]{:S(2)}, u32[]{:S(2)}) collective-permute-start(s32[2]{0:T(128)S(1)} %bitcast.117), channel_id=1, source_target_pairs={{0,4},{4,0},{8,12},{12,8},{16,20},{20,16},{24,28},{28,24},{1,5},{5... | collective-permute-start | bytes 32 | tf_op jit(solution)/shard_map/ppermute | solution.py:135
  15.1 29.2 %collective-permute-start.8 = (bf16[256,512]{1,0:T(8,128)(2,1)}, bf16[256,512]{1,0:T(8,128)(2,1)S(1)}, u32[]{:S(2)}, u32[]{:S(2)}) collective-permute-start(bf16[256,512]{1,0:T(8,128)(2,1)} %get-tuple-element.42), channel_id=1, source_target_pairs={{0,8},{4,12},{8,0},{12,4},{16,24},{20,28},{24,16},{28,20},{1,9},{5... | collective-permute-start | bytes 786440 | tf_op jit(solution)/shard_map/ppermute | solution.py:143
  16.1 28.3 %collective-permute-start.11 = (bf16[256,512]{1,0:T(8,128)(2,1)}, bf16[256,512]{1,0:T(8,128)(2,1)S(1)}, u32[]{:S(2)}, u32[]{:S(2)}) collective-permute-start(bf16[256,512]{1,0:T(8,128)(2,1)} %get-tuple-element.42), channel_id=1, source_target_pairs={{8,16},{12,20},{16,8},{20,12},{9,17},{13,21},{17,9},{21,13},{10,18... | collective-permute-start | bytes 786440 | tf_op jit(solution)/shard_map/ppermute | solution.py:145
  18.7 25.6 %collective-permute-start.6 = (bf16[256,512]{1,0:T(8,128)(2,1)}, bf16[256,512]{1,0:T(8,128)(2,1)}, u32[]{:S(2)}, u32[]{:S(2)}) collective-permute-start(bf16[256,512]{1,0:T(8,128)(2,1)} %get-tuple-element.43), channel_id=1, source_target_pairs={{8,16},{12,20},{16,8},{20,12},{9,17},{13,21},{17,9},{21,13},{10,18... | collective-permute-start | bytes 786440 | tf_op jit(solution)/shard_map/ppermute | solution.py:145
  33.1 11.3 %collective-permute-start.10 = (bf16[256,512]{1,0:T(8,128)(2,1)S(1)}, bf16[256,512]{1,0:T(8,128)(2,1)}, u32[]{:S(2)}, u32[]{:S(2)}) collective-permute-start(bf16[256,512]{1,0:T(8,128)(2,1)S(1)} %collective-permute-done.9), channel_id=1, source_target_pairs={{8,0},{12,4},{16,24},{20,28},{9,1},{13,5},{17,25},{21,29},{10,2},{... | collective-permute-start | bytes 786440 | tf_op jit(solution)/shard_map/ppermute | solution.py:146
  34.4 11.8 %collective-permute-start.5 = (bf16[256,512]{1,0:T(8,128)(2,1)S(1)}, bf16[256,512]{1,0:T(8,128)(2,1)}, u32[]{:S(2)}, u32[]{:S(2)}) collective-permute-start(bf16[256,512]{1,0:T(8,128)(2,1)S(1)} %collective-permute-done.4), channel_id=1, source_target_pairs={{8,0},{12,4},{16,24},{20,28},{9,1},{13,5},{17,25},{21,29},{10,2},{... | collective-permute-start | bytes 786440 | tf_op jit(solution)/shard_map/ppermute | solution.py:146
  44.2 5.7 %collective-permute-start.1 = (bf16[2,256,512]{2,1,0:T(8,128)(2,1)S(1)}, bf16[2,256,512]{2,1,0:T(8,128)(2,1)S(1)}, u32[]{:S(2)}, u32[]{:S(2)}) collective-permute-start(bf16[2,256,512]{2,1,0:T(8,128)(2,1)S(1)} %pad_maximum_fusion.2), channel_id=1, source_target_pairs={{0,1},{1,0},{2,3},{3,2},{4,5},{5,4},{6,7},{7,6},{8,9},{9,8},{10,11... | collective-permute-start | bytes 1572872 | tf_op jit(solution)/shard_map/ppermute | solution.py:150
  47.5 14.9 %collective-permute-start.12 = (bf16[2,256,512]{2,1,0:T(8,128)(2,1)S(1)}, bf16[2,256,512]{2,1,0:T(8,128)(2,1)S(1)}, u32[]{:S(2)}, u32[]{:S(2)}) collective-permute-start(bf16[2,256,512]{2,1,0:T(8,128)(2,1)S(1)} %pad_maximum_fusion.5), channel_id=1, source_target_pairs={{0,4},{4,0},{8,12},{12,8},{16,20},{20,16},{24,28},{28,24},{1,5},{5... | collective-permute-start | bytes 1572872 | tf_op jit(solution)/shard_map/ppermute | solution.py:178
  49.3 25.2 %collective-permute-start.7 = (bf16[2,256,512]{2,1,0:T(8,128)(2,1)S(1)}, bf16[2,256,512]{2,1,0:T(8,128)(2,1)S(1)}, u32[]{:S(2)}, u32[]{:S(2)}) collective-permute-start(bf16[2,256,512]{2,1,0:T(8,128)(2,1)S(1)} %pad_maximum_fusion.3), channel_id=1, source_target_pairs={{0,4},{4,0},{8,12},{12,8},{16,20},{20,16},{24,28},{28,24},{1,5},{5... | collective-permute-start | bytes 1572872 | tf_op jit(solution)/shard_map/ppermute | solution.py:178
  82.5 14.2 %collective-permute-start.20 = (bf16[2,256,512]{2,1,0:T(8,128)(2,1)}, bf16[2,256,512]{2,1,0:T(8,128)(2,1)}, u32[]{:S(2)}, u32[]{:S(2)}) collective-permute-start(bf16[2,256,512]{2,1,0:T(8,128)(2,1)} %get-tuple-element.19), channel_id=1, source_target_pairs={{0,4},{4,0},{8,12},{12,8},{16,20},{20,16},{24,28},{28,24},{1,5},{5... | collective-permute-start | bytes 1572872 | tf_op jit(solution)/shard_map/ppermute | solution.py:188
  89.3 17.4 %collective-permute-start.15 = (bf16[2,256,512]{2,1,0:T(8,128)(2,1)}, bf16[2,256,512]{2,1,0:T(8,128)(2,1)S(1)}, u32[]{:S(2)}, u32[]{:S(2)}) collective-permute-start(bf16[2,256,512]{2,1,0:T(8,128)(2,1)} %copy-done.3), channel_id=1, source_target_pairs={{0,4},{4,0},{8,12},{12,8},{16,20},{20,16},{24,28},{28,24},{1,5},{5... | collective-permute-start | bytes 1572872 | tf_op jit(solution)/shard_map/ppermute | solution.py:188
  91.3 52.8 %collective-permute-start.13 = (f32[2,256,512]{2,1,0:T(8,128)S(1)}, f32[2,256,512]{2,1,0:T(8,128)S(1)}, u32[]{:S(2)}, u32[]{:S(2)}) collective-permute-start(f32[2,256,512]{2,1,0:T(8,128)S(1)} %pad_maximum_fusion), channel_id=1, source_target_pairs={{0,1},{1,0},{2,3},{3,2},{4,5},{5,4},{6,7},{7,6},{8,9},{9,8},{10,11... | collective-permute-start | bytes 3145736 | tf_op jit(solution)/shard_map/ppermute | solution.py:211
  98.2 26.1 %collective-permute-start.24 = (bf16[256,512]{1,0:T(8,128)(2,1)S(1)}, bf16[256,512]{1,0:T(8,128)(2,1)S(1)}, u32[]{:S(2)}, u32[]{:S(2)}) collective-permute-start(bf16[256,512]{1,0:T(8,128)(2,1)S(1)} %get-tuple-element.31), channel_id=1, source_target_pairs={{8,16},{12,20},{16,8},{20,12},{9,17},{13,21},{17,9},{21,13},{10,18... | collective-permute-start | bytes 786440 | tf_op jit(solution)/shard_map/ppermute | solution.py:200
  98.8 16.1 %collective-permute-start.22 = (bf16[256,512]{1,0:T(8,128)(2,1)S(1)}, bf16[256,512]{1,0:T(8,128)(2,1)S(1)}, u32[]{:S(2)}, u32[]{:S(2)}) collective-permute-start(bf16[256,512]{1,0:T(8,128)(2,1)S(1)} %get-tuple-element.31), channel_id=1, source_target_pairs={{0,8},{4,12},{24,16},{28,20},{1,9},{5,13},{25,17},{29,21},{2,10},{... | collective-permute-start | bytes 786440 | tf_op jit(solution)/shard_map/ppermute | solution.py:199
  107.2 29.4 %collective-permute-start.19 = (bf16[256,512]{1,0:T(8,128)(2,1)S(1)}, bf16[256,512]{1,0:T(8,128)(2,1)S(1)}, u32[]{:S(2)}, u32[]{:S(2)}) collective-permute-start(bf16[256,512]{1,0:T(8,128)(2,1)S(1)} %get-tuple-element.29), channel_id=1, source_target_pairs={{8,16},{12,20},{16,8},{20,12},{9,17},{13,21},{17,9},{21,13},{10,18... | collective-permute-start | bytes 786440 | tf_op jit(solution)/shard_map/ppermute | solution.py:200
  107.9 13.8 %collective-permute-start.17 = (bf16[256,512]{1,0:T(8,128)(2,1)S(1)}, bf16[256,512]{1,0:T(8,128)(2,1)S(1)}, u32[]{:S(2)}, u32[]{:S(2)}) collective-permute-start(bf16[256,512]{1,0:T(8,128)(2,1)S(1)} %get-tuple-element.29), channel_id=1, source_target_pairs={{0,8},{4,12},{24,16},{28,20},{1,9},{5,13},{25,17},{29,21},{2,10},{... | collective-permute-start | bytes 786440 | tf_op jit(solution)/shard_map/ppermute | solution.py:199
  114.9 12.3 %collective-permute-start.21 = (bf16[256,512]{1,0:T(8,128)(2,1)S(1)}, bf16[256,512]{1,0:T(8,128)(2,1)S(1)}, u32[]{:S(2)}, u32[]{:S(2)}) collective-permute-start(bf16[256,512]{1,0:T(8,128)(2,1)S(1)} %get-tuple-element.30), channel_id=1, source_target_pairs={{0,8},{4,12},{8,0},{12,4},{16,24},{20,28},{24,16},{28,20},{1,9},{5... | collective-permute-start | bytes 786440 | tf_op jit(solution)/shard_map/ppermute | solution.py:201
  121.6 14.5 %collective-permute-start.23 = (bf16[256,512]{1,0:T(8,128)(2,1)S(1)}, bf16[256,512]{1,0:T(8,128)(2,1)S(1)}, u32[]{:S(2)}, u32[]{:S(2)}) collective-permute-start(bf16[256,512]{1,0:T(8,128)(2,1)S(1)} %fusion.4), channel_id=1, source_target_pairs={{0,16},{4,20},{8,24},{12,28},{16,0},{20,4},{24,8},{28,12},{1,17},{... | collective-permute-start | bytes 786440 | tf_op jit(solution)/shard_map/ppermute | solution.py:203
  124.3 14.0 %collective-permute-start.16 = (bf16[256,512]{1,0:T(8,128)(2,1)S(1)}, bf16[256,512]{1,0:T(8,128)(2,1)S(1)}, u32[]{:S(2)}, u32[]{:S(2)}) collective-permute-start(bf16[256,512]{1,0:T(8,128)(2,1)S(1)} %get-tuple-element.28), channel_id=1, source_target_pairs={{0,8},{4,12},{8,0},{12,4},{16,24},{20,28},{24,16},{28,20},{1,9},{5... | collective-permute-start | bytes 786440 | tf_op jit(solution)/shard_map/ppermute | solution.py:201
  127.2 16.5 %collective-permute-start.18 = (bf16[256,512]{1,0:T(8,128)(2,1)S(1)}, bf16[256,512]{1,0:T(8,128)(2,1)S(1)}, u32[]{:S(2)}, u32[]{:S(2)}) collective-permute-start(bf16[256,512]{1,0:T(8,128)(2,1)S(1)} %fusion.8), channel_id=1, source_target_pairs={{0,16},{4,20},{8,24},{12,28},{16,0},{20,4},{24,8},{28,12},{1,17},{... | collective-permute-start | bytes 786440 | tf_op jit(solution)/shard_map/ppermute | solution.py:203
  136.5 9.2 %copy-start.6 = (f32[1,512,512]{2,1,0:T(8,128)S(1)}, f32[1,512,512]{2,1,0:T(8,128)}, u32[]{:S(2)}) copy-start(f32[1,512,512]{2,1,0:T(8,128)} %param.12) | copy-start | bytes 3145732
  136.5 9.2 %copy-start.7 = (f32[1,512,512]{2,1,0:T(8,128)S(1)}, f32[1,512,512]{2,1,0:T(8,128)}, u32[]{:S(2)}) copy-start(f32[1,512,512]{2,1,0:T(8,128)} %param.13) | copy-start | bytes 3145732
  144.2 6.4 %collective-permute-start.14 = (bf16[256,512]{1,0:T(8,128)(2,1)S(1)}, bf16[256,512]{1,0:T(8,128)(2,1)S(1)}, u32[]{:S(2)}, u32[]{:S(2)}) collective-permute-start(bf16[256,512]{1,0:T(8,128)(2,1)S(1)} %fusion.12), channel_id=1, source_target_pairs={{0,2},{1,3},{2,0},{3,1},{4,6},{5,7},{6,4},{7,5},{8,10},{9,11},{10,... | collective-permute-start | bytes 786440 | tf_op jit(solution)/shard_map/ppermute | solution.py:213
  (6 other events, 31.2 us)

commit v2 on v0

v2 whole, which is shorter than its diff:
```python
import functools

import jax
import jax.numpy as jnp
from jax import lax
from jax.experimental import pallas as pl
from jax.experimental.pallas import tpu as pltpu
from jax.sharding import PartitionSpec as P

learn_rate = 0.2
decay_rate = 0.5

LANES = 128
CUTS = (2, 2)

small_cost = pl.CostEstimate(flops=1, bytes_accessed=1, transcendentals=0)
whole = pl.BlockSpec(memory_space=pltpu.VMEM)
smalls = pl.BlockSpec(memory_space=pltpu.SMEM)
anywhere = pl.BlockSpec(memory_space=pl.ANY)
done_shape = pltpu.HBM((8, 128), jnp.float32)
MIB = 1024 * 1024


def cell_grads(count_block, shifted, block):
    safe_count = jnp.maximum(count_block, 1).astype(jnp.float32)
    weight = (0.1 / block) + (0.25 / block) * jnp.sqrt(safe_count)
    fitted = weight * (shifted - jnp.log(safe_count))
    hinge_grad = (0.5 / block) * jnp.tanh(0.5 * shifted) + (0.5 / block)
    return jnp.where(count_block > 0, fitted, hinge_grad).astype(jnp.bfloat16)


def in_order(
    kernel, tokens, out_shape, in_specs, out_specs=None, grid=(), vmem=16, scalars=None
):
    ahead = scalars is not None

    def wrapped(*refs):
        done = refs[-1]
        done[...] = jnp.zeros_like(done)
        kernel(*refs[:ahead], *refs[ahead + len(tokens) : -1])

    done_spec = pl.BlockSpec((8, 128), lambda *ids: (0, 0)) if grid else whole
    out_specs = [whole] * len(out_shape) if out_specs is None else out_specs
    call = pl.pallas_call(
        wrapped,
        grid_spec=pltpu.PrefetchScalarGridSpec(
            num_scalar_prefetch=int(ahead),
            grid=grid,
            in_specs=[anywhere] * len(tokens) + list(in_specs),
            out_specs=list(out_specs) + [done_spec],
        ),
        out_shape=list(out_shape) + [done_shape],
        cost_estimate=small_cost,
        compiler_params=pltpu.CompilerParams(vmem_limit_bytes=vmem * MIB),
    )
    held = [
        pltpu.with_memory_space_constraint(token, pltpu.HBM) if token.shape == (8, 128) else token
        for token in tokens
    ]
    return lambda *args: call(*([scalars] if ahead else []), *held, *args)


def in_vmem(*values):
    return [pltpu.with_memory_space_constraint(value, pltpu.VMEM) for value in values]


def in_hbm(*values):
    return [pltpu.with_memory_space_constraint(value, pltpu.HBM) for value in values]


def gated(value, *tokens):
    return pl.pallas_call(
        lambda *refs: None,
        in_specs=[anywhere] * (1 + len(tokens)),
        out_specs=anywhere,
        out_shape=jax.ShapeDtypeStruct(value.shape, value.dtype),
        input_output_aliases={0: 0},
        cost_estimate=small_cost,
        compiler_params=pltpu.CompilerParams(vmem_limit_bytes=MIB),
    )(value, *tokens)


def halve_kernel(whole_cols, half_cols):
    half_cols[...] = whole_cols[0].astype(jnp.bfloat16)


def halved(col_embed, start, units, tokens):
    width = col_embed.shape[2]
    return in_order(
        halve_kernel,
        tokens,
        [pltpu.HBM((units * LANES, width), jnp.bfloat16)],
        [pl.BlockSpec((1, LANES, width), lambda unit: (0, start + unit, 0))],
        [pl.BlockSpec((LANES, width), lambda unit: (unit, 0))],
        grid=(units,),
    )(pltpu.with_memory_space_constraint(col_embed, pltpu.HBM))


def pick_kernel(slots, seat, own, near, far, cross, asked, kept):
    for first, out in ((5, asked), (3, kept)):
        for slot in range(slots):
            for away, ref in enumerate((own, near, far, cross)):

                @pl.when(seat[first + slot] == away)
                def _(ref=ref, out=out, slot=slot):
                    for unit in range(out.shape[0]):
                        out[unit, pl.ds(slot * LANES, LANES), :] = ref[pl.ds(unit * LANES, LANES), :]


def picked(seat, pieces, slots, tokens):
    size, width = pieces[0].shape
    shape = (size // LANES, slots * LANES, width)
    return in_order(
        functools.partial(pick_kernel, slots),
        tokens,
        [jax.ShapeDtypeStruct(shape, jnp.bfloat16)] * 2,
        [smalls] + [whole] * 4,
    )(seat, *in_hbm(pieces[0]), *pieces[1:])


def count_terms(count, row_term, col_logs, block):
    safe = jnp.maximum(count, 1).astype(jnp.float32)
    some = (0.1 / block) + (0.25 / block) * jnp.sqrt(safe)
    return jnp.where(count > 0, some, 0.0), jnp.log(safe) - (row_term + col_logs)


def block_terms(rows, cols, weight, target, block):
    predicted = lax.dot_general(
        rows, cols, (((1,), (1,)), ((), ())), preferred_element_type=jnp.float32
    )
    error = predicted - target
    hinge_grad = (0.5 / block) * jnp.tanh(0.5 * error) + (0.5 / block)
    cell = jnp.where(weight > 0.0, weight * error, hinge_grad).astype(jnp.bfloat16)
    return jnp.dot(cell, cols, preferred_element_type=jnp.float32), lax.dot_general(
        cell, rows, (((0,), (0,)), ((), ())), preferred_element_type=jnp.float32
    )


def own_kernel(start, slots, seat, row_term, col_freq, own, core, chip, both, cols, *rest):
    counts, rest = rest[: 2 * slots], rest[2 * slots :]
    home_grad, core_grad, col_grad, weight, target = rest
    step = pl.program_id(0)
    block, size = row_term.shape[0], own.shape[0]

    @pl.when(step == 0)
    def _():
        home_grad[...] = jnp.zeros_like(home_grad)
        core_grad[...] = jnp.zeros_like(core_grad)

    def logs(slot, which):
        at = seat[1 + slot] * block + (seat[0] ^ which) * (block // 2) + (start + step) * LANES
        return jnp.log(col_freq[:, pl.ds(pl.multiple_of(at, LANES), LANES)].astype(jnp.float32))

    col_logs = [[logs(slot, which) for slot in range(slots)] for which in range(2)]
    some = cols[0]
    total = None
    for piece, ref in enumerate((own, core, chip, both)):
        at = pl.ds(pl.multiple_of((seat[7] ^ piece) * size, size), size)
        sides = []
        for which in range(2):
            pairs = [
                count_terms(
                    counts[which * slots + slot][0, 0, 0, at, :],
                    row_term[at, :],
                    col_logs[which][slot],
                    block,
                )
                for slot in range(slots)
            ]
            sides.append([jnp.concatenate(pair, axis=1) for pair in zip(*pairs)])
        row_part, col_part = block_terms(ref[...], some, *sides[0], block)
        row_grad = core_grad if piece % 2 else home_grad
        row_grad[piece // 2] += row_part
        total = col_part if total is None else total + col_part
        weight[step, at, :], target[step, at, :] = sides[1]
    col_grad[0] = total


def other_kernel(block, seat, own, core, chip, both, cols, weight, target, *rest):
    home_before, core_before, home_grad, core_grad, col_grad = rest
    size = own.shape[0]
    for unit in range(cols.shape[0]):
        total = None
        for piece, ref in enumerate((own, core, chip, both)):
            at = pl.ds(pl.multiple_of((seat[7] ^ piece) * size, size), size)
            row_part, col_part = block_terms(
                ref[...], cols[unit], weight[unit, at, :], target[unit, at, :], block
            )
            row_grad = core_grad if piece % 2 else home_grad
            before = row_grad if unit else (core_before if piece % 2 else home_before)
            row_grad[piece // 2] = before[piece // 2] + row_part
            total = col_part if total is None else total + col_part
        col_grad[unit] = total.astype(col_grad.dtype)


def own_grads(seat, row_term, col_freq, rows, cols, counts, start, tokens):
    size, width = rows[0].shape
    units, both, _ = cols.shape
    slots, block = counts.shape[2:4]
    halves = block // 2 // LANES
    grad_shape = pltpu.VMEM((2, size, width), jnp.float32)
    term_shape = pltpu.VMEM((units, block, both), jnp.float32)
    col_spec = pl.BlockSpec((1, both, width), lambda unit, seat: (unit, 0, 0))

    def count_spec(slot, which):
        return pl.BlockSpec(
            (1, 1, 1, block, LANES),
            lambda unit, seat: (0, 0, slot, 0, (seat[0] ^ which) * halves + start + unit),
        )

    count_specs = [count_spec(slot, which) for which in range(2) for slot in range(slots)]
    counts = pltpu.with_memory_space_constraint(counts, pltpu.HBM)
    return in_order(
        functools.partial(own_kernel, start, slots),
        tokens,
        [grad_shape, grad_shape, pltpu.HBM(cols.shape, jnp.float32), term_shape, term_shape],
        [whole] * 6 + [col_spec] + count_specs,
        [whole, whole, col_spec, whole, whole],
        grid=(units,),
        vmem=32,
        scalars=seat,
    )(row_term, col_freq, *rows, cols, *[counts] * (2 * slots))


def other_grads(seat, rows, cols, weight, target, before, tokens):
    size, width = rows[0].shape
    grad_shape = jax.ShapeDtypeStruct((2, size, width), jnp.float32)
    return in_order(
        functools.partial(other_kernel, weight.shape[1]),
        tokens,
        [grad_shape, grad_shape, pltpu.HBM(cols.shape, jnp.bfloat16)],
        [smalls] + [whole] * 9,
        vmem=24,
    )(seat, *rows, cols, *in_vmem(weight, target, *before))


def sum_kernel(slots, seat, mine, theirs, home, near, far, cross):
    for unit in range(mine.shape[0]):
        for away, out in enumerate((home, near, far, cross)):
            total = jnp.zeros(out.shape[1:], jnp.float32)
            for slot in range(slots):
                at = pl.ds(slot * LANES, LANES)
                total = total + jnp.where(seat[3 + slot] == away, mine[unit, at, :], 0.0)
                total = total + jnp.where(
                    seat[5 + slot] == away, theirs[unit, at, :].astype(jnp.float32), 0.0
                )
            out[unit] = total.astype(out.dtype)


def block_sums(seat, mine, theirs, slots, tokens):
    units, _, width = mine.shape
    shape = (units, LANES, width)
    return in_order(
        functools.partial(sum_kernel, slots),
        tokens,
        [
            pltpu.HBM(shape, jnp.float32),
            pltpu.HBM(shape, jnp.bfloat16),
            jax.ShapeDtypeStruct(shape, jnp.float32),
            jax.ShapeDtypeStruct(shape, jnp.bfloat16),
        ],
        [smalls, whole, whole],
    )(seat, mine, theirs)


def crossed_body(
    row_embed,
    row_accum,
    col_embed,
    col_accum,
    col_freq,
    row_freq,
    block_cols,
    counts,
    excluded,
    log_total,
):
    block = counts.shape[3]
    slots = counts.shape[2]
    width = col_embed.shape[2]
    row_index = lax.axis_index("row")
    col_index = lax.axis_index("col")
    half = row_index % 2
    home = row_index // 2

    mate_swap = [(i, i ^ 1) for i in range(8)]
    near_swap = [(i, i ^ 2) for i in range(8)]
    far_swap = [(i, i ^ 4) for i in range(8)]
    core_swap = [(i, i ^ 1) for i in range(4)]
    chip_swap = [(i, i ^ 2) for i in range(4)]

    def swap(name, value, axis, pairs):
        with jax.named_scope(name):
            return lax.ppermute(value, axis, pairs)

    chosen = block_cols[0, 0]
    mate_chosen = swap("mate_chosen", chosen, "row", mate_swap)
    seat = jnp.concatenate(
        [half[None], chosen, chosen ^ home, mate_chosen ^ home, col_index[None]]
    ).astype(jnp.int32)

    starts = [sum(CUTS[:part]) for part in range(len(CUTS))]

    def spread_cols(part, *tokens):
        own, done = halved(col_embed, starts[part], CUTS[part], tokens)
        far = swap(f"cols_far_{part}", own, "row", far_swap)
        near = swap(f"cols_near_{part}", own, "row", near_swap)
        return (own, near, far), done

    def all_cols(part, own, near, far):
        return own, near, far, swap(f"cols_cross_{part}", far, "row", near_swap)

    cols_0, done = spread_cols(0)
    row_half = row_embed.astype(jnp.bfloat16)
    core_rows = swap("core_rows", row_half, "col", core_swap)
    chip_rows = swap("chip_rows", row_half, "col", chip_swap)
    both_rows = swap("both_rows", chip_rows, "col", core_swap)
    rows = (row_half, core_rows, chip_rows, both_rows)
    row_term = (jnp.log(row_freq.astype(jnp.float32)) - log_total)[:, None]

    def own(part, cols, done):
        home_grad, core_grad, col_grad, *terms, done = own_grads(
            seat, row_term, col_freq, rows, cols, counts, starts[part], (done,)
        )
        return (home_grad, core_grad), col_grad, terms, done

    def other(cols, terms, before, *tokens):
        home_grad, core_grad, col_grad, done = other_grads(
            seat, rows, cols, *terms, before, tokens
        )
        return (home_grad, core_grad), col_grad, done

    parts = len(CUTS)
    cols, row_grads, summed, sent = all_cols(0, *cols_0), [], [], ()

    def sum_part(part, mine, from_mate, *tokens):
        home_sum, near, far, cross, done = block_sums(seat, mine, from_mate, slots, tokens)
        cross = swap(f"grads_cross_{part}", cross, "row", near_swap)
        return (home_sum, near, far, cross), done

    def send_part(part, sums):
        home_sum, near, far, cross = sums
        far = (far + cross.astype(jnp.float32)).astype(jnp.bfloat16)
        near = swap(f"grads_near_{part}", near, "row", near_swap)
        far = swap(f"grads_far_{part}", far, "row", far_swap)
        total = home_sum + near.astype(jnp.float32) + far.astype(jnp.float32)
        summed.append(total.reshape(-1, width))
        return near, far

    for part in range(parts):
        asked, kept, done = picked(seat, cols, slots, (done, both_rows))
        received = swap(f"cols_mate_{part}", asked, "row", mate_swap)
        if part + 1 < parts:
            cols, done = spread_cols(part + 1, done)
        own_rows, mine, terms, done = own(part, kept, done)
        if part + 1 < parts:
            own_cols, near, far = cols
            cols = all_cols(part + 1, own_cols, near, gated(far, done, near))
        if part:
            sums, done = sum_part(part - 1, *waiting, done, *sent)
            sent = send_part(part - 1, sums)
            other_rows, theirs, done = other(received, terms, own_rows, done, sums[3])
        else:
            other_rows, theirs, done = other(received, terms, own_rows, done)
        row_grads.append(other_rows)
        waiting = mine, swap(f"grads_mate_{part}", theirs, "row", mate_swap)

    home_grad, core_grad = [sum(pieces[1:], pieces[0]) for pieces in zip(*row_grads)]
    from_core = swap("row_grads_core", core_grad, "col", core_swap)
    chip_grad = (home_grad[1] + from_core[1]).astype(jnp.bfloat16)
    from_chip = swap("row_grads_chip", chip_grad, "col", chip_swap)
    own_grad = home_grad[0] + from_core[0] + from_chip.astype(jnp.float32)
    row_new = row_updates(row_embed, row_accum, row_freq, excluded, block, own_grad)

    sums, done = sum_part(parts - 1, *waiting, done, *sent)
    send_part(parts - 1, sums)
    return (*row_new, *col_updates(col_embed, col_accum, jnp.concatenate(summed, axis=0)))


def row_updates(row_embed, row_accum, row_freq, excluded, block, own_grad):
    own_rows = row_embed.shape[0]
    col_index = lax.axis_index("col")
    row_index = lax.axis_index("row")
    own_freq = lax.dynamic_slice_in_dim(row_freq, col_index * own_rows, own_rows).astype(
        jnp.float32
    )
    row_ids = row_index * block + col_index * own_rows + jnp.arange(own_rows, dtype=jnp.int32)
    decayed = jnp.all(row_ids[:, None] != excluded[None, :], axis=1)
    freq_root = jnp.sqrt(own_freq)
    decay_coef = jnp.where(decayed, decay_rate * freq_root / (freq_root + 30.0), jnp.float32(0.0))
    full_grad = own_grad + decay_coef[:, None] * row_embed
    row_accum_new = row_accum + full_grad * full_grad
    row_embed_new = row_embed - learn_rate * full_grad / jnp.sqrt(row_accum_new)
    return row_embed_new, row_accum_new


def col_updates(col_embed, col_accum, col_grad):
    col_step = col_grad[None]
    col_accum_new = col_accum + col_step * col_step
    col_embed_new = col_embed - learn_rate * col_step / jnp.sqrt(col_accum_new)
    return col_embed_new, col_accum_new


def gathered_body(
    row_embed,
    row_accum,
    col_embed,
    col_accum,
    col_freq,
    row_freq,
    block_cols,
    counts,
    excluded,
    log_total,
):
    block = counts.shape[3]
    slots = counts.shape[2]
    width = row_embed.shape[1]
    chosen = block_cols[0, 0]
    block_rows = lax.all_gather(row_embed.astype(jnp.bfloat16), "col", axis=0, tiled=True)
    group = lax.all_gather(col_embed[0].astype(jnp.bfloat16), "row", axis=0, tiled=True)
    row_term = (jnp.log(row_freq.astype(jnp.float32)) - log_total)[:, None]
    col_logs = jnp.log(col_freq[0].astype(jnp.float32))
    row_grad = jnp.zeros((block, width), jnp.float32)
    summed = jnp.zeros(group.shape, jnp.float32)
    for slot in range(slots):
        start = chosen[slot] * block
        cols = lax.dynamic_slice_in_dim(group, start, block)
        predicted = lax.dot_general(
            block_rows, cols, (((1,), (1,)), ((), ())), preferred_element_type=jnp.float32
        )
        shifted = predicted + row_term + lax.dynamic_slice_in_dim(col_logs, start, block)[None]
        cell = cell_grads(counts[0, 0, slot], shifted, block)
        row_grad = row_grad + jnp.dot(cell, cols, preferred_element_type=jnp.float32)
        term = lax.dot_general(
            cell, block_rows, (((0,), (0,)), ((), ())), preferred_element_type=jnp.float32
        )
        summed = lax.dynamic_update_slice_in_dim(summed, term, start, 0)
    col_grad = lax.psum_scatter(summed, "row", scatter_dimension=0, tiled=True)
    own_grad = lax.psum_scatter(row_grad, "col", scatter_dimension=0, tiled=True)
    return (
        *row_updates(row_embed, row_accum, row_freq, excluded, block, own_grad),
        *col_updates(col_embed, col_accum, col_grad),
    )


def body(row_embed, row_accum, col_embed, col_accum, col_freq, row_freq, block_cols, counts, *rest):
    halves = lax.axis_size("row") == 8 and 2 * col_embed.shape[1] == counts.shape[3]
    pick = crossed_body if halves and lax.axis_size("col") == 4 else gathered_body
    return pick(
        row_embed, row_accum, col_embed, col_accum, col_freq, row_freq, block_cols, counts, *rest
    )


def solution(mesh):
    in_specs = (
        P(("row", "col"), None),
        P(("row", "col"), None),
        P("col", "row", None),
        P("col", "row", None),
        P("col", None),
        P("row"),
        P("row", "col", None),
        P("row", "col", None, None, None),
        P(),
        P(),
    )
    out_specs = (
        P(("row", "col"), None),
        P(("row", "col"), None),
        P("col", "row", None),
        P("col", "row", None),
    )
    return jax.shard_map(body, mesh=mesh, in_specs=in_specs, out_specs=out_specs, check_vma=False)
```

time: 333 us -> 129 us (0.39)
  waiting for transfers between devices: 196 us -> 48.7 us
  local copies, waits for them, and re-layouts: 77.5 us -> 6.18 us
  Pallas kernels: 0 us -> 34.7 us
  starting transfers between devices: 0.34 us -> 27.9 us
  matrix products: 21.5 us -> 0 us
  between operations: 15.9 us -> 1.48 us
  other arithmetic: 21.9 us -> 9.87 us
    reduce_scatter x2 -> x0, waiting for transfers between devices: 144 us -> none  [the longest x1 144 us: body(): col_grad = lax.psum_scatter(summed, 'row', scatter_dimension=0, tiled=True)]
    all_gather x2 -> x0, waiting for transfers between devices: 51.6 us -> none  [the longest x1 51.6 us: body(): lax.all_gather(col_embed.astype(jnp.bfloat16), 'row', axis=1, tiled=True)]
    ppermute x0 -> x22, waiting for transfers between devices: none -> 48.7 us  [swap(): return lax.ppermute(value, axis, pairs)]
    pallas_call x0 -> x11, Pallas kernels: none -> 34.7 us  [the longest x10 34.7 us: in_order(): return lambda *args: call(*([scalars] if ahead else []), *held, *args)]
    gather x2 -> x0, local copies, waits for them, and re-layouts: 33.6 us -> none  [body(): picked = jnp.take(col_parts[slot_id], offset, axis=0)]
    ppermute x0 -> x22, starting transfers between devices: none -> 27.9 us  [swap(): return lax.ppermute(value, axis, pairs)]
    dot_general x6 -> x0, matrix products: 21.5 us -> none  [the longest x2 11.4 us: body(): lax.dot_general(block_rows, col_block, (((1,), (1,)), ((), ())), preferre...]
    scatter x1 -> x0, local copies, waits for them, and re-layouts: 19.2 us -> none  [body(): jnp.zeros((slots * block, width), jnp.bfloat16).at[target]]
  transfers between devices with their start and end apart: 4 -> 22, of which waited for: 2 -> 10; matrix products, arithmetic and copies ran while one was open for 29% -> 6% of each run, Pallas kernels for 0% -> 22%
where the time goes in v2:
time: 129 us
  waiting for transfers between devices  48.7 us (38%)
  Pallas kernels  34.7 us (27%)
  starting transfers between devices  27.9 us (22%)
  other arithmetic  9.87 us (8%)
  local copies, waits for them, and re-layouts  6.18 us (5%)
  between operations  1.48 us (1%)
    ppermute x22, waiting for transfers between devices, swap(): return lax.ppermute(value, axis, pairs)  48.7 us
    pallas_call x10, Pallas kernels, in_order(): return lambda *args: call(*([scalars] if ahead else []), *held, *args)  34.7 us
    ppermute x22, starting transfers between devices, swap(): return lax.ppermute(value, axis, pairs)  27.9 us
    unnamed x38, local copies, waits for them, and re-layouts  5.22 us
  transfers between devices with their start and end apart: 22, of which 10 were waited for; matrix products, arithmetic and copies ran while one was open for 6% of the time, Pallas kernels for 22%

profile of v2, /device:TPU:0, one launch (start us, length us, event | category | flops | bytes accessed | tf_op | source)
XLA Modules:
  0.0 128.8 jit_solution(14812466339898682526)
XLA Ops:
  1.7 3.0 %collective-permute-start.1 = (bf16[256,512]{1,0:T(8,128)(2,1)S(1)}, bf16[256,512]{1,0:T(8,128)(2,1)S(1)}, u32[]{:S(2)}, u32[]{:S(2)}) collective-permute-start(bf16[256,512]{1,0:T(8,128)(2,1)S(1)} %convert_element_type.42.refs_4_.refs_2_.refs_3_), channel_id=1, source_target_pairs={{0,2},{1,3},{2,0},{3,1},{4,6},{5,7},{6,4},{7,5},{8,10},{9,11},{10,... | collective-permute-start | bytes 786440 | tf_op jit(solution)/shard_map/chip_rows/ppermute | solution.py:294
  4.7 1.7 %shard_map.129 = (bf16[256,512]{1,0:T(8,128)(2,1)}, f32[8,128]{1,0:T(8,128)}) custom-call(f32[1,512,512]{2,1,0:T(8,128)} %refs_1_.1), custom_call_target="tpu_custom_call" | custom-call | flops 1 | bytes 1 | tf_op jit(solution)/shard_map/pallas_call | solution.py:60
  6.4 2.6 %collective-permute-start.4 = (bf16[256,512]{1,0:T(8,128)(2,1)}, bf16[256,512]{1,0:T(8,128)(2,1)S(1)}, u32[]{:S(2)}, u32[]{:S(2)}) collective-permute-start(bf16[256,512]{1,0:T(8,128)(2,1)} %get-tuple-element.44.refs_3_), channel_id=1, source_target_pairs={{0,16},{4,20},{8,24},{12,28},{16,0},{20,4},{24,8},{28,12},{1,17},{... | collective-permute-start | bytes 786440 | tf_op jit(solution)/shard_map/cols_far_0/ppermute | solution.py:294
  9.0 1.6 %collective-permute-start.3 = (bf16[256,512]{1,0:T(8,128)(2,1)}, bf16[256,512]{1,0:T(8,128)(2,1)S(1)}, u32[]{:S(2)}, u32[]{:S(2)}) collective-permute-start(bf16[256,512]{1,0:T(8,128)(2,1)} %get-tuple-element.44.refs_3_), channel_id=1, source_target_pairs={{0,8},{4,12},{8,0},{12,4},{16,24},{20,28},{24,16},{28,20},{1,9},{5... | collective-permute-start | bytes 786440 | tf_op jit(solution)/shard_map/cols_near_0/ppermute | solution.py:294
  10.6 1.5 %collective-permute-start = (s32[2]{0:T(128)}, s32[2]{0:T(128)S(1)}, u32[]{:S(2)}, u32[]{:S(2)}) collective-permute-start(s32[2]{0:T(128)} %bitcast.23), channel_id=1, source_target_pairs={{0,4},{4,0},{8,12},{12,8},{16,20},{20,16},{24,28},{28,24},{1,5},{5... | collective-permute-start | bytes 32 | tf_op jit(solution)/shard_map/mate_chosen/ppermute | solution.py:294
  12.1 8.9 %collective-permute-done.4.refs_5_ = bf16[256,512]{1,0:T(8,128)(2,1)S(1)} collective-permute-done((bf16[256,512]{1,0:T(8,128)(2,1)}, bf16[256,512]{1,0:T(8,128)(2,1)S(1)}, u32[]{:S(2)}, u32[]{:S(2)}) %collective-permute-start.4) | collective-permute-done | bytes 262176 | tf_op jit(solution)/shard_map/cols_far_0/ppermute | solution.py:294
  23.1 5.1 %collective-permute-done.5.refs_6_ = bf16[256,512]{1,0:T(8,128)(2,1)S(1)} collective-permute-done((bf16[256,512]{1,0:T(8,128)(2,1)S(1)}, bf16[256,512]{1,0:T(8,128)(2,1)S(1)}, u32[]{:S(2)}, u32[]{:S(2)}) %collective-permute-start.5) | collective-permute-done | bytes 262176 | tf_op jit(solution)/shard_map/cols_cross_0/ppermute | solution.py:294
  28.2 1.9 %shard_map.130 = (bf16[2,256,512]{2,1,0:T(8,128)(2,1)}, bf16[2,256,512]{2,1,0:T(8,128)(2,1)S(1)}, f32[8,128]{1,0:T(8,128)}) custom-call(f32[8,128]{1,0:T(8,128)} %get-tuple-element.43.refs_0_, bf16[256,512]{1,0:T(8,128)(2,1)S(1)} %collective-permute-done.2.refs_1_.refs_7_.refs_5_.refs_6_, s32[8]{0:T(128)S(1)} %concatenate.24.refs_2_.refs_0_.refs_1_.refs_3_, ...), custom_call_target="tpu_custom_call" | custom-call | flops 1 | bytes 1 | tf_op jit(solution)/shard_map/pallas_call | solution.py:60
  30.1 1.5 %collective-permute-start.7 = (bf16[2,256,512]{2,1,0:T(8,128)(2,1)}, bf16[2,256,512]{2,1,0:T(8,128)(2,1)S(1)}, u32[]{:S(2)}, u32[]{:S(2)}) collective-permute-start(bf16[2,256,512]{2,1,0:T(8,128)(2,1)} %get-tuple-element.49), channel_id=1, source_target_pairs={{0,4},{4,0},{8,12},{12,8},{16,20},{20,16},{24,28},{28,24},{1,5},{5... | collective-permute-start | bytes 1572872 | tf_op jit(solution)/shard_map/cols_mate_0/ppermute | solution.py:294
  31.7 1.7 %shard_map.131 = (bf16[256,512]{1,0:T(8,128)(2,1)}, f32[8,128]{1,0:T(8,128)}) custom-call(f32[8,128]{1,0:T(8,128)} %get-tuple-element.45.refs_0_, f32[1,512,512]{2,1,0:T(8,128)} %refs_1_.1), custom_call_target="tpu_custom_call" | custom-call | flops 1 | bytes 1 | tf_op jit(solution)/shard_map/pallas_call | solution.py:60
  33.4 1.7 %collective-permute-start.8 = (bf16[256,512]{1,0:T(8,128)(2,1)}, bf16[256,512]{1,0:T(8,128)(2,1)S(1)}, u32[]{:S(2)}, u32[]{:S(2)}) collective-permute-start(bf16[256,512]{1,0:T(8,128)(2,1)} %get-tuple-element.56.refs_3_), channel_id=1, source_target_pairs={{0,8},{4,12},{8,0},{12,4},{16,24},{20,28},{24,16},{28,20},{1,9},{5... | collective-permute-start | bytes 786440 | tf_op jit(solution)/shard_map/cols_near_1/ppermute | solution.py:294
  35.1 3.3 %collective-permute-start.9 = (bf16[256,512]{1,0:T(8,128)(2,1)}, bf16[256,512]{1,0:T(8,128)(2,1)S(1)}, u32[]{:S(2)}, u32[]{:S(2)}) collective-permute-start(bf16[256,512]{1,0:T(8,128)(2,1)} %get-tuple-element.56.refs_3_), channel_id=1, source_target_pairs={{0,16},{4,20},{8,24},{12,28},{16,0},{20,4},{24,8},{28,12},{1,17},{... | collective-permute-start | bytes 786440 | tf_op jit(solution)/shard_map/cols_far_1/ppermute | solution.py:294
  39.3 7.6 %shard_map.132 = (f32[2,256,512]{2,1,0:T(8,128)S(1)}, f32[2,256,512]{2,1,0:T(8,128)S(1)}, f32[2,256,512]{2,1,0:T(8,128)}, f32[2,1024,256]{2,1,0:T(8,128)S(1)}, f...) custom-call(s32[8]{0:T(128)S(1)} %concatenate.24.refs_2_.refs_0_.refs_1_.refs_3_, f32[8,128]{1,0:T(8,128)} %get-tuple-element.46.refs_1_, ...), custom_call_target="tpu_custom_call" | custom-call | flops 1 | bytes 1 | tf_op jit(solution)/shard_map/pallas_call | solution.py:60
  47.6 3.3 %collective-permute-done.9.refs_0_ = bf16[256,512]{1,0:T(8,128)(2,1)S(1)} collective-permute-done((bf16[256,512]{1,0:T(8,128)(2,1)}, bf16[256,512]{1,0:T(8,128)(2,1)S(1)}, u32[]{:S(2)}, u32[]{:S(2)}) %collective-permute-start.9) | collective-permute-done | bytes 262176 | tf_op jit(solution)/shard_map/cols_far_1/ppermute | solution.py:294
  53.8 4.4 %shard_map.133 = (f32[2,256,512]{2,1,0:T(8,128)S(1)}, f32[2,256,512]{2,1,0:T(8,128)S(1)}, bf16[2,256,512]{2,1,0:T(8,128)(2,1)}, f32[8,128]{1,0:T(8,128)}) custom-call(f32[8,128]{1,0:T(8,128)} %get-tuple-element.48.refs_0_.refs_1_, s32[8]{0:T(128)S(1)} %concatenate.24.refs_2_.refs_0_.refs_1_.refs_3_, ...), custom_call_target="tpu_custom_call" | custom-call | flops 1 | bytes 1 | tf_op jit(solution)/shard_map/pallas_call | solution.py:60
  58.7 1.9 %shard_map.135 = (bf16[2,256,512]{2,1,0:T(8,128)(2,1)S(1)}, bf16[2,256,512]{2,1,0:T(8,128)(2,1)S(1)}, f32[8,128]{1,0:T(8,128)}) custom-call(f32[8,128]{1,0:T(8,128)} %get-tuple-element.55.refs_0_, bf16[256,512]{1,0:T(8,128)(2,1)S(1)} %collective-permute-done.2.refs_1_.refs_7_.refs_5_.refs_6_, s32[8]{0:T(128)S(1)} %concatenate.24.refs_2_.refs_0_.refs_1_.refs_3_, ...), custom_call_target="tpu_custom_call" | custom-call | flops 1 | bytes 1 | tf_op jit(solution)/shard_map/pallas_call | solution.py:60
  62.1 7.6 %shard_map.136 = (f32[2,256,512]{2,1,0:T(8,128)S(1)}, f32[2,256,512]{2,1,0:T(8,128)S(1)}, f32[2,256,512]{2,1,0:T(8,128)}, f32[2,1024,256]{2,1,0:T(8,128)S(1)}, f...) custom-call(s32[8]{0:T(128)S(1)} %concatenate.24.refs_2_.refs_0_.refs_1_.refs_3_, f32[8,128]{1,0:T(8,128)} %get-tuple-element.57.refs_1_, ...), custom_call_target="tpu_custom_call" | custom-call | flops 1 | bytes 1 | tf_op jit(solution)/shard_map/pallas_call | solution.py:60
  69.7 3.6 %collective-permute-done.11.refs_3_ = bf16[2,256,512]{2,1,0:T(8,128)(2,1)S(1)} collective-permute-done((bf16[2,256,512]{2,1,0:T(8,128)(2,1)}, bf16[2,256,512]{2,1,0:T(8,128)(2,1)S(1)}, u32[]{:S(2)}, u32[]{:S(2)}) %collective-permute-start.11) | collective-permute-done | bytes 524320 | tf_op jit(solution)/shard_map/grads_mate_0/ppermute | solution.py:294
  73.3 1.8 %shard_map.137 = (f32[2,128,512]{2,1,0:T(8,128)}, bf16[2,128,512]{2,1,0:T(8,128)(2,1)}, f32[2,128,512]{2,1,0:T(8,128)S(1)}, bf16[2,128,512]{2,1,0:T(8,128)(2,1)S(1)}, f32[8,128]{1,0:T(8,128)}) custom-call(f32[8,128]{1,0:T(8,128)} %get-tuple-element.59.refs_0_, s32[8]{0:T(128)S(1)} %concatenate.24.refs_2_.refs_0_.refs_1_.refs_3_, ...), custom_call_target="tpu_custom_call" | custom-call | flops 1 | bytes 1 | tf_op jit(solution)/shard_map/pallas_call | solution.py:60
  75.0 1.7 %collective-permute-start.12 = (bf16[2,128,512]{2,1,0:T(8,128)(2,1)S(1)}, bf16[2,128,512]{2,1,0:T(8,128)(2,1)S(1)}, u32[]{:S(2)}, u32[]{:S(2)}) collective-permute-start(bf16[2,128,512]{2,1,0:T(8,128)(2,1)S(1)} %get-tuple-element.63), channel_id=1, source_target_pairs={{0,8},{4,12},{8,0},{12,4},{16,24},{20,28},{24,16},{28,20},{1,9},{5... | collective-permute-start | bytes 786440 | tf_op jit(solution)/shard_map/grads_cross_0/ppermute | solution.py:294
  76.8 6.1 %collective-permute-done.13.refs_7_ = bf16[2,256,512]{2,1,0:T(8,128)(2,1)S(1)} collective-permute-done((bf16[2,256,512]{2,1,0:T(8,128)(2,1)S(1)}, bf16[2,256,512]{2,1,0:T(8,128)(2,1)S(1)}, u32[]{:S(2)}, u32[]{:S(2)}) %collective-permute-start.13) | collective-permute-done | bytes 524320 | tf_op jit(solution)/shard_map/cols_mate_1/ppermute | solution.py:294
  82.9 4.4 %shard_map.138 = (f32[2,256,512]{2,1,0:T(8,128)S(1)}, f32[2,256,512]{2,1,0:T(8,128)S(1)}, bf16[2,256,512]{2,1,0:T(8,128)(2,1)}, f32[8,128]{1,0:T(8,128)}) custom-call(f32[8,128]{1,0:T(8,128)} %get-tuple-element.62.refs_0_, bf16[2,128,512]{2,1,0:T(8,128)(2,1)S(1)} %collective-permute-done.12.refs_1_, s32[8]{0:T(128)S(1)} %concatenate.24.refs_2_.refs_0_.refs_1_.refs_3_, ...), custom_call_target="tpu_custom_call" | custom-call | flops 1 | bytes 1 | tf_op jit(solution)/shard_map/pallas_call | solution.py:60
  88.1 2.4 %collective-permute-start.17 = (bf16[2,128,512]{2,1,0:T(8,128)(2,1)S(1)}, bf16[2,128,512]{2,1,0:T(8,128)(2,1)S(1)}, u32[]{:S(2)}, u32[]{:S(2)}) collective-permute-start(bf16[2,128,512]{2,1,0:T(8,128)(2,1)S(1)} %add_convert_fusion.1), channel_id=1, source_target_pairs={{0,16},{4,20},{8,24},{12,28},{16,0},{20,4},{24,8},{28,12},{1,17},{... | collective-permute-start | bytes 786440 | tf_op jit(solution)/shard_map/grads_far_0/ppermute | solution.py:294
  91.7 8.3 %collective-permute-done.16.refs_1_ = bf16[2,128,512]{2,1,0:T(8,128)(2,1)S(1)} collective-permute-done((bf16[2,128,512]{2,1,0:T(8,128)(2,1)}, bf16[2,128,512]{2,1,0:T(8,128)(2,1)S(1)}, u32[]{:S(2)}, u32[]{:S(2)}) %collective-permute-start.16) | collective-permute-done | bytes 262176 | tf_op jit(solution)/shard_map/grads_near_0/ppermute | solution.py:294
  101.2 1.8 %shard_map.139 = (f32[2,128,512]{2,1,0:T(8,128)}, bf16[2,128,512]{2,1,0:T(8,128)(2,1)}, f32[2,128,512]{2,1,0:T(8,128)S(1)}, bf16[2,128,512]{2,1,0:T(8,128)(2,1)S(1)}, f32[8,128]{1,0:T(8,128)}) custom-call(f32[8,128]{1,0:T(8,128)} %get-tuple-element.75.refs_0_, bf16[2,128,512]{2,1,0:T(8,128)(2,1)S(1)} %collective-permute-done.16.refs_1_, ...), custom_call_target="tpu_custom_call" | custom-call | flops 1 | bytes 1 | tf_op jit(solution)/shard_map/pallas_call | solution.py:60
  103.8 2.1 %collective-permute-start.20 = (bf16[2,128,512]{2,1,0:T(8,128)(2,1)S(1)}, bf16[2,128,512]{2,1,0:T(8,128)(2,1)}, u32[]{:S(2)}, u32[]{:S(2)}) collective-permute-start(bf16[2,128,512]{2,1,0:T(8,128)(2,1)S(1)} %get-tuple-element.81), channel_id=1, source_target_pairs={{0,8},{4,12},{8,0},{12,4},{16,24},{20,28},{24,16},{28,20},{1,9},{5... | collective-permute-start | bytes 786440 | tf_op jit(solution)/shard_map/grads_cross_1/ppermute | solution.py:294
  107.0 6.2 %collective-permute-done.20 = bf16[2,128,512]{2,1,0:T(8,128)(2,1)} collective-permute-done((bf16[2,128,512]{2,1,0:T(8,128)(2,1)S(1)}, bf16[2,128,512]{2,1,0:T(8,128)(2,1)}, u32[]{:S(2)}, u32[]{:S(2)}) %collective-permute-start.20) | collective-permute-done | bytes 262176 | tf_op jit(solution)/shard_map/grads_cross_1/ppermute | solution.py:294
  114.2 2.0 %collective-permute-start.21 = (bf16[2,128,512]{2,1,0:T(8,128)(2,1)S(1)}, bf16[2,128,512]{2,1,0:T(8,128)(2,1)S(1)}, u32[]{:S(2)}, u32[]{:S(2)}) collective-permute-start(bf16[2,128,512]{2,1,0:T(8,128)(2,1)S(1)} %add_convert_fusion), channel_id=1, source_target_pairs={{0,16},{4,20},{8,24},{12,28},{16,0},{20,4},{24,8},{28,12},{1,17},{... | collective-permute-start | bytes 786440 | tf_op jit(solution)/shard_map/grads_far_1/ppermute | solution.py:294
  118.2 2.4 %collective-permute-done.19 = bf16[2,128,512]{2,1,0:T(8,128)(2,1)S(1)} collective-permute-done((bf16[2,128,512]{2,1,0:T(8,128)(2,1)S(1)}, bf16[2,128,512]{2,1,0:T(8,128)(2,1)S(1)}, u32[]{:S(2)}, u32[]{:S(2)}) %collective-permute-start.19) | collective-permute-done | bytes 262176 | tf_op jit(solution)/shard_map/grads_near_1/ppermute | solution.py:294
  120.6 4.1 %collective-permute-done.21 = bf16[2,128,512]{2,1,0:T(8,128)(2,1)S(1)} collective-permute-done((bf16[2,128,512]{2,1,0:T(8,128)(2,1)S(1)}, bf16[2,128,512]{2,1,0:T(8,128)(2,1)S(1)}, u32[]{:S(2)}, u32[]{:S(2)}) %collective-permute-start.21) | collective-permute-done | bytes 262176 | tf_op jit(solution)/shard_map/grads_far_1/ppermute | solution.py:294
  124.9 1.7 %multiply_subtract_fusion = (f32[1,512,512]{2,1,0:T(8,128)}, f32[1,512,512]{2,1,0:T(8,128)}) fusion(f32[1,512,512]{2,1,0:T(8,128)S(1)} %copy-done.10, f32[1,256,512]{2,1,0:T(8,128)S(1)} %bitcast.21, f32[1,256,512]{2,1,0:T(8,128)S(1)} %bitcast.20, f32[1,512,512]{2,1,0:T(8,128)S(1)} %copy-done.12), kind=kLoop, calls=%fused_computation.1 | loop fusion | flops 1572864 | bytes 5242880 | tf_op jit(solution)/shard_map/sub | solution.py:400
  126.5 2.3 %multiply_subtract_fusion.1 = (f32[256,512]{1,0:T(8,128)}, f32[256,512]{1,0:T(8,128)}) fusion(f32[256,512]{1,0:T(8,128)S(1)} %copy-done.11, f32[256]{0:T(256)S(1)} %fusion.5, bf16[256,512]{1,0:T(8,128)(2,1)S(1)} %collective-permute-done.15, f32[2,256,512]{2,1,0:T(8,128)} %collective-permute-done.14, f32[2,256,512]{2,1,0:T(8,128)S(1)} %add.74, ...), kind=kLoop, calls=%fused_computation.13 | loop fusion | flops 1310720 | bytes 3408896 | tf_op jit(solution)/shard_map/sub | solution.py:393
  (79 shorter events, 17.4 us)
Async XLA Ops:
  0.6 38.4 %copy-start.16 = (s32[1024]{0:T(1024)S(1)}, s32[1024]{0:T(1024)}, u32[]{:S(2)}) copy-start(s32[1024]{0:T(1024)} %param.15) | copy-start | bytes 12292
  1.7 37.6 %copy-start.8 = (s32[1,4096]{1,0:T(1,128)S(1)}, s32[1,4096]{1,0:T(1,128)}, u32[]{:S(2)}) copy-start(s32[1,4096]{1,0:T(1,128)} %refs_3_.3) | copy-start | bytes 49156
  1.7 10.4 %collective-permute-start.1 = (bf16[256,512]{1,0:T(8,128)(2,1)S(1)}, bf16[256,512]{1,0:T(8,128)(2,1)S(1)}, u32[]{:S(2)}, u32[]{:S(2)}) collective-permute-start(bf16[256,512]{1,0:T(8,128)(2,1)S(1)} %convert_element_type.42.refs_4_.refs_2_.refs_3_), channel_id=1, source_target_pairs={{0,2},{1,3},{2,0},{3,1},{4,6},{5,7},{6,4},{7,5},{8,10},{9,11},{10,... | collective-permute-start | bytes 786440 | tf_op jit(solution)/shard_map/chip_rows/ppermute | solution.py:294
  6.4 14.6 %collective-permute-start.4 = (bf16[256,512]{1,0:T(8,128)(2,1)}, bf16[256,512]{1,0:T(8,128)(2,1)S(1)}, u32[]{:S(2)}, u32[]{:S(2)}) collective-permute-start(bf16[256,512]{1,0:T(8,128)(2,1)} %get-tuple-element.44.refs_3_), channel_id=1, source_target_pairs={{0,16},{4,20},{8,24},{12,28},{16,0},{20,4},{24,8},{28,12},{1,17},{... | collective-permute-start | bytes 786440 | tf_op jit(solution)/shard_map/cols_far_0/ppermute | solution.py:294
  9.0 14.1 %collective-permute-start.3 = (bf16[256,512]{1,0:T(8,128)(2,1)}, bf16[256,512]{1,0:T(8,128)(2,1)S(1)}, u32[]{:S(2)}, u32[]{:S(2)}) collective-permute-start(bf16[256,512]{1,0:T(8,128)(2,1)} %get-tuple-element.44.refs_3_), channel_id=1, source_target_pairs={{0,8},{4,12},{8,0},{12,4},{16,24},{20,28},{24,16},{28,20},{1,9},{5... | collective-permute-start | bytes 786440 | tf_op jit(solution)/shard_map/cols_near_0/ppermute | solution.py:294
  10.6 11.8 %collective-permute-start = (s32[2]{0:T(128)}, s32[2]{0:T(128)S(1)}, u32[]{:S(2)}, u32[]{:S(2)}) collective-permute-start(s32[2]{0:T(128)} %bitcast.23), channel_id=1, source_target_pairs={{0,4},{4,0},{8,12},{12,8},{16,20},{20,16},{24,28},{28,24},{1,5},{5... | collective-permute-start | bytes 32 | tf_op jit(solution)/shard_map/mate_chosen/ppermute | solution.py:294
  12.1 11.0 %collective-permute-start.2 = (bf16[256,512]{1,0:T(8,128)(2,1)S(1)}, bf16[256,512]{1,0:T(8,128)(2,1)S(1)}, u32[]{:S(2)}, u32[]{:S(2)}) collective-permute-start(bf16[256,512]{1,0:T(8,128)(2,1)S(1)} %collective-permute-done.1.refs_6_.refs_4_.refs_5_), channel_id=1, source_target_pairs={{0,1},{1,0},{2,3},{3,2},{4,5},{5,4},{6,7},{7,6},{8,9},{9,8},{10,11... | collective-permute-start | bytes 786440 | tf_op jit(solution)/shard_map/both_rows/ppermute | solution.py:294
  21.0 7.2 %collective-permute-start.5 = (bf16[256,512]{1,0:T(8,128)(2,1)S(1)}, bf16[256,512]{1,0:T(8,128)(2,1)S(1)}, u32[]{:S(2)}, u32[]{:S(2)}) collective-permute-start(bf16[256,512]{1,0:T(8,128)(2,1)S(1)} %collective-permute-done.4.refs_5_), channel_id=1, source_target_pairs={{0,8},{4,12},{8,0},{12,4},{16,24},{20,28},{24,16},{28,20},{1,9},{5... | collective-permute-start | bytes 786440 | tf_op jit(solution)/shard_map/cols_cross_0/ppermute | solution.py:294
  30.1 21.8 %collective-permute-start.7 = (bf16[2,256,512]{2,1,0:T(8,128)(2,1)}, bf16[2,256,512]{2,1,0:T(8,128)(2,1)S(1)}, u32[]{:S(2)}, u32[]{:S(2)}) collective-permute-start(bf16[2,256,512]{2,1,0:T(8,128)(2,1)} %get-tuple-element.49), channel_id=1, source_target_pairs={{0,4},{4,0},{8,12},{12,8},{16,20},{20,16},{24,28},{28,24},{1,5},{5... | collective-permute-start | bytes 1572872 | tf_op jit(solution)/shard_map/cols_mate_0/ppermute | solution.py:294
  31.6 7.6 %collective-permute-start.6 = (bf16[256,512]{1,0:T(8,128)(2,1)S(1)}, bf16[256,512]{1,0:T(8,128)(2,1)S(1)}, u32[]{:S(2)}, u32[]{:S(2)}) collective-permute-start(bf16[256,512]{1,0:T(8,128)(2,1)S(1)} %convert_element_type.42.refs_4_.refs_2_.refs_3_), channel_id=1, source_target_pairs={{0,1},{1,0},{2,3},{3,2},{4,5},{5,4},{6,7},{7,6},{8,9},{9,8},{10,11... | collective-permute-start | bytes 786440 | tf_op jit(solution)/shard_map/core_rows/ppermute | solution.py:294
  33.4 14.3 %collective-permute-start.8 = (bf16[256,512]{1,0:T(8,128)(2,1)}, bf16[256,512]{1,0:T(8,128)(2,1)S(1)}, u32[]{:S(2)}, u32[]{:S(2)}) collective-permute-start(bf16[256,512]{1,0:T(8,128)(2,1)} %get-tuple-element.56.refs_3_), channel_id=1, source_target_pairs={{0,8},{4,12},{8,0},{12,4},{16,24},{20,28},{24,16},{28,20},{1,9},{5... | collective-permute-start | bytes 786440 | tf_op jit(solution)/shard_map/cols_near_1/ppermute | solution.py:294
  35.1 15.9 %collective-permute-start.9 = (bf16[256,512]{1,0:T(8,128)(2,1)}, bf16[256,512]{1,0:T(8,128)(2,1)S(1)}, u32[]{:S(2)}, u32[]{:S(2)}) collective-permute-start(bf16[256,512]{1,0:T(8,128)(2,1)} %get-tuple-element.56.refs_3_), channel_id=1, source_target_pairs={{0,16},{4,20},{8,24},{12,28},{16,0},{20,4},{24,8},{28,12},{1,17},{... | collective-permute-start | bytes 786440 | tf_op jit(solution)/shard_map/cols_far_1/ppermute | solution.py:294
  51.7 7.0 %collective-permute-start.10 = (bf16[256,512]{1,0:T(8,128)(2,1)S(1)}, bf16[256,512]{1,0:T(8,128)(2,1)S(1)}, u32[]{:S(2)}, u32[]{:S(2)}) collective-permute-start(bf16[256,512]{1,0:T(8,128)(2,1)S(1)} %shard_map.134.refs_5_), channel_id=1, source_target_pairs={{0,8},{4,12},{8,0},{12,4},{16,24},{20,28},{24,16},{28,20},{1,9},{5... | collective-permute-start | bytes 786440 | tf_op jit(solution)/shard_map/cols_cross_1/ppermute | solution.py:294
  58.2 15.1 %collective-permute-start.11 = (bf16[2,256,512]{2,1,0:T(8,128)(2,1)}, bf16[2,256,512]{2,1,0:T(8,128)(2,1)S(1)}, u32[]{:S(2)}, u32[]{:S(2)}) collective-permute-start(bf16[2,256,512]{2,1,0:T(8,128)(2,1)} %get-tuple-element.61), channel_id=1, source_target_pairs={{0,4},{4,0},{8,12},{12,8},{16,20},{20,16},{24,28},{28,24},{1,5},{5... | collective-permute-start | bytes 1572872 | tf_op jit(solution)/shard_map/grads_mate_0/ppermute | solution.py:294
  60.6 22.3 %collective-permute-start.13 = (bf16[2,256,512]{2,1,0:T(8,128)(2,1)S(1)}, bf16[2,256,512]{2,1,0:T(8,128)(2,1)S(1)}, u32[]{:S(2)}, u32[]{:S(2)}) collective-permute-start(bf16[2,256,512]{2,1,0:T(8,128)(2,1)S(1)} %get-tuple-element.64), channel_id=1, source_target_pairs={{0,4},{4,0},{8,12},{12,8},{16,20},{20,16},{24,28},{28,24},{1,5},{5... | collective-permute-start | bytes 1572872 | tf_op jit(solution)/shard_map/cols_mate_1/ppermute | solution.py:294
  62.1 11.1 %copy-start.3 = (f32[2,256,512]{2,1,0:T(8,128)S(1)}, f32[2,256,512]{2,1,0:T(8,128)}, u32[]{:S(2)}) copy-start(f32[2,256,512]{2,1,0:T(8,128)} %get-tuple-element.60.refs_2_) | copy-start | bytes 3145732
  75.0 7.8 %collective-permute-start.12 = (bf16[2,128,512]{2,1,0:T(8,128)(2,1)S(1)}, bf16[2,128,512]{2,1,0:T(8,128)(2,1)S(1)}, u32[]{:S(2)}, u32[]{:S(2)}) collective-permute-start(bf16[2,128,512]{2,1,0:T(8,128)(2,1)S(1)} %get-tuple-element.63), channel_id=1, source_target_pairs={{0,8},{4,12},{8,0},{12,4},{16,24},{20,28},{24,16},{28,20},{1,9},{5... | collective-permute-start | bytes 786440 | tf_op jit(solution)/shard_map/grads_cross_0/ppermute | solution.py:294
  87.2 12.7 %collective-permute-start.18 = (bf16[2,256,512]{2,1,0:T(8,128)(2,1)}, bf16[2,256,512]{2,1,0:T(8,128)(2,1)S(1)}, u32[]{:S(2)}, u32[]{:S(2)}) collective-permute-start(bf16[2,256,512]{2,1,0:T(8,128)(2,1)} %get-tuple-element.77), channel_id=1, source_target_pairs={{0,4},{4,0},{8,12},{12,8},{16,20},{20,16},{24,28},{28,24},{1,5},{5... | collective-permute-start | bytes 1572872 | tf_op jit(solution)/shard_map/grads_mate_1/ppermute | solution.py:294
  87.8 12.2 %collective-permute-start.16 = (bf16[2,128,512]{2,1,0:T(8,128)(2,1)}, bf16[2,128,512]{2,1,0:T(8,128)(2,1)S(1)}, u32[]{:S(2)}, u32[]{:S(2)}) collective-permute-start(bf16[2,128,512]{2,1,0:T(8,128)(2,1)} %get-tuple-element.73), channel_id=1, source_target_pairs={{0,8},{4,12},{8,0},{12,4},{16,24},{20,28},{24,16},{28,20},{1,9},{5... | collective-permute-start | bytes 786440 | tf_op jit(solution)/shard_map/grads_near_0/ppermute | solution.py:294
  88.1 11.9 %collective-permute-start.17 = (bf16[2,128,512]{2,1,0:T(8,128)(2,1)S(1)}, bf16[2,128,512]{2,1,0:T(8,128)(2,1)S(1)}, u32[]{:S(2)}, u32[]{:S(2)}) collective-permute-start(bf16[2,128,512]{2,1,0:T(8,128)(2,1)S(1)} %add_convert_fusion.1), channel_id=1, source_target_pairs={{0,16},{4,20},{8,24},{12,28},{16,0},{20,4},{24,8},{28,12},{1,17},{... | collective-permute-start | bytes 786440 | tf_op jit(solution)/shard_map/grads_far_0/ppermute | solution.py:294
  90.5 15.3 %copy-start.17 = (s32[512]{0:T(512)S(1)}, s32[512]{0:T(512)}, u32[]{:S(2)}) copy-start(s32[512]{0:T(512)} %param.18) | copy-start | bytes 6148
  91.7 24.7 %collective-permute-start.14 = (f32[2,256,512]{2,1,0:T(8,128)}, f32[2,256,512]{2,1,0:T(8,128)}, u32[]{:S(2)}, u32[]{:S(2)}) collective-permute-start(f32[2,256,512]{2,1,0:T(8,128)} %add.75), channel_id=1, source_target_pairs={{0,1},{1,0},{2,3},{3,2},{4,5},{5,4},{6,7},{7,6},{8,9},{9,8},{10,11... | collective-permute-start | bytes 3145736 | tf_op jit(solution)/shard_map/row_grads_core/ppermute | solution.py:294
  91.7 14.4 %copy-start.1 = (f32[2,256,512]{2,1,0:T(8,128)S(1)}, f32[2,256,512]{2,1,0:T(8,128)}, u32[]{:S(2)}) copy-start(f32[2,256,512]{2,1,0:T(8,128)} %copy-done) | copy-start | bytes 3145732
  103.8 9.4 %copy-start.7 = (f32[2,128,512]{2,1,0:T(8,128)S(1)}, f32[2,128,512]{2,1,0:T(8,128)}, u32[]{:S(2)}) copy-start(f32[2,128,512]{2,1,0:T(8,128)} %copy-done.6) | copy-start | bytes 1572868
  103.8 9.4 %collective-permute-start.20 = (bf16[2,128,512]{2,1,0:T(8,128)(2,1)S(1)}, bf16[2,128,512]{2,1,0:T(8,128)(2,1)}, u32[]{:S(2)}, u32[]{:S(2)}) collective-permute-start(bf16[2,128,512]{2,1,0:T(8,128)(2,1)S(1)} %get-tuple-element.81), channel_id=1, source_target_pairs={{0,8},{4,12},{8,0},{12,4},{16,24},{20,28},{24,16},{28,20},{1,9},{5... | collective-permute-start | bytes 786440 | tf_op jit(solution)/shard_map/grads_cross_1/ppermute | solution.py:294
  106.1 10.1 %copy-start.14 = (f32[2,128,512]{2,1,0:T(8,128)S(1)}, f32[2,128,512]{2,1,0:T(8,128)}, u32[]{:S(2)}) copy-start(f32[2,128,512]{2,1,0:T(8,128)} %get-tuple-element.72) | copy-start | bytes 1572868
  106.4 18.4 %copy-start.15 = (f32[2,128,512]{2,1,0:T(8,128)S(1)}, f32[2,128,512]{2,1,0:T(8,128)}, u32[]{:S(2)}) copy-start(f32[2,128,512]{2,1,0:T(8,128)} %get-tuple-element.78) | copy-start | bytes 1572868
  107.0 13.6 %collective-permute-start.19 = (bf16[2,128,512]{2,1,0:T(8,128)(2,1)S(1)}, bf16[2,128,512]{2,1,0:T(8,128)(2,1)S(1)}, u32[]{:S(2)}, u32[]{:S(2)}) collective-permute-start(bf16[2,128,512]{2,1,0:T(8,128)(2,1)S(1)} %copy-done.18), channel_id=1, source_target_pairs={{0,8},{4,12},{8,0},{12,4},{16,24},{20,28},{24,16},{28,20},{1,9},{5... | collective-permute-start | bytes 786440 | tf_op jit(solution)/shard_map/grads_near_1/ppermute | solution.py:294
  114.2 10.5 %collective-permute-start.21 = (bf16[2,128,512]{2,1,0:T(8,128)(2,1)S(1)}, bf16[2,128,512]{2,1,0:T(8,128)(2,1)S(1)}, u32[]{:S(2)}, u32[]{:S(2)}) collective-permute-start(bf16[2,128,512]{2,1,0:T(8,128)(2,1)S(1)} %add_convert_fusion), channel_id=1, source_target_pairs={{0,16},{4,20},{8,24},{12,28},{16,0},{20,4},{24,8},{28,12},{1,17},{... | collective-permute-start | bytes 786440 | tf_op jit(solution)/shard_map/grads_far_1/ppermute | solution.py:294
  116.2 8.6 %copy-start.10 = (f32[1,512,512]{2,1,0:T(8,128)S(1)}, f32[1,512,512]{2,1,0:T(8,128)}, u32[]{:S(2)}) copy-start(f32[1,512,512]{2,1,0:T(8,128)} %refs_1_.1) | copy-start | bytes 3145732
  116.2 8.6 %copy-start.12 = (f32[1,512,512]{2,1,0:T(8,128)S(1)}, f32[1,512,512]{2,1,0:T(8,128)}, u32[]{:S(2)}) copy-start(f32[1,512,512]{2,1,0:T(8,128)} %param.13) | copy-start | bytes 3145732
  117.6 8.9 %collective-permute-start.15 = (bf16[256,512]{1,0:T(8,128)(2,1)S(1)}, bf16[256,512]{1,0:T(8,128)(2,1)S(1)}, u32[]{:S(2)}, u32[]{:S(2)}) collective-permute-start(bf16[256,512]{1,0:T(8,128)(2,1)S(1)} %fusion.4), channel_id=1, source_target_pairs={{0,2},{1,3},{2,0},{3,1},{4,6},{5,7},{6,4},{7,5},{8,10},{9,11},{10,... | collective-permute-start | bytes 786440 | tf_op jit(solution)/shard_map/row_grads_chip/ppermute | solution.py:294
  (9 other events, 13.3 us)

commit v3 on v2

--- a/solution.py
+++ b/solution.py
@@ -30,7 +30,7 @@
 
 
 def in_order(
-    kernel, tokens, out_shape, in_specs, out_specs=None, grid=(), vmem=16, scalars=None
+    kernel, tokens, out_shape, in_specs, out_specs=None, grid=(), vmem=16, scalars=None, aliases={}
 ):
     ahead = scalars is not None
 
@@ -50,14 +50,15 @@
             out_specs=list(out_specs) + [done_spec],
         ),
         out_shape=list(out_shape) + [done_shape],
+        input_output_aliases=aliases,
         cost_estimate=small_cost,
         compiler_params=pltpu.CompilerParams(vmem_limit_bytes=vmem * MIB),
     )
-    held = [
-        pltpu.with_memory_space_constraint(token, pltpu.HBM) if token.shape == (8, 128) else token
-        for token in tokens
-    ]
-    return lambda *args: call(*([scalars] if ahead else []), *held, *args)
+    return lambda *args: call(*([scalars] if ahead else []), *held(tokens), *args)
+
+
+def held(tokens):
+    return [*map(lambda token: in_hbm(token)[0] if token.shape == (8, 128) else token, tokens)]
 
 
 def in_vmem(*values):
@@ -68,32 +69,38 @@
     return [pltpu.with_memory_space_constraint(value, pltpu.HBM) for value in values]
 
 
-def gated(value, *tokens):
+def gated(values, tokens):
     return pl.pallas_call(
         lambda *refs: None,
-        in_specs=[anywhere] * (1 + len(tokens)),
-        out_specs=anywhere,
-        out_shape=jax.ShapeDtypeStruct(value.shape, value.dtype),
-        input_output_aliases={0: 0},
+        in_specs=[anywhere] * (len(values) + len(tokens)),
+        out_specs=[anywhere] * len(values),
+        out_shape=[jax.ShapeDtypeStruct(value.shape, value.dtype) for value in values],
+        input_output_aliases={i: i for i in range(len(values))},
         cost_estimate=small_cost,
         compiler_params=pltpu.CompilerParams(vmem_limit_bytes=MIB),
-    )(value, *tokens)
-
-
-def halve_kernel(whole_cols, half_cols):
-    half_cols[...] = whole_cols[0].astype(jnp.bfloat16)
-
-
-def halved(col_embed, start, units, tokens):
-    width = col_embed.shape[2]
+    )(*values, *held(tokens))
+
+
+def halve_kernel(whole_values, half_values):
+    half_values[...] = whole_values[...].reshape(half_values.shape).astype(half_values.dtype)
+
+
+def halved(values, start, rows, tokens):
+    lead, width = values.shape[:-2], values.shape[-1]
     return in_order(
         halve_kernel,
         tokens,
-        [pltpu.HBM((units * LANES, width), jnp.bfloat16)],
-        [pl.BlockSpec((1, LANES, width), lambda unit: (0, start + unit, 0))],
-        [pl.BlockSpec((LANES, width), lambda unit: (unit, 0))],
-        grid=(units,),
-    )(pltpu.with_memory_space_constraint(col_embed, pltpu.HBM))
+        [jax.ShapeDtypeStruct((rows, width), jnp.bfloat16)],
+        [
+            pl.BlockSpec(
+                (*lead, LANES, width),
+                lambda step: (*[0] * len(lead), start // LANES + step, 0),
+            )
+        ],
+        [pl.BlockSpec((LANES, width), lambda step: (step, 0))],
+        grid=(rows // LANES,),
+        vmem=4,
+    )(*in_hbm(values))
 
 
 def pick_kernel(slots, seat, own, near, far, cross, asked, kept):
@@ -138,14 +145,14 @@
 
 def own_kernel(start, slots, seat, row_term, col_freq, own, core, chip, both, cols, *rest):
     counts, rest = rest[: 2 * slots], rest[2 * slots :]
-    home_grad, core_grad, col_grad, weight, target = rest
+    row_grads, (col_grad, weight, target) = rest[:4], rest[4:]
     step = pl.program_id(0)
     block, size = row_term.shape[0], own.shape[0]
 
     @pl.when(step == 0)
     def _():
-        home_grad[...] = jnp.zeros_like(home_grad)
-        core_grad[...] = jnp.zeros_like(core_grad)
+        for row_grad in row_grads:
+            row_grad[...] = jnp.zeros_like(row_grad)
 
     def logs(slot, which):
         at = seat[1 + slot] * block + (seat[0] ^ which) * (block // 2) + (start + step) * LANES
@@ -169,15 +176,15 @@
             ]
             sides.append([jnp.concatenate(pair, axis=1) for pair in zip(*pairs)])
         row_part, col_part = block_terms(ref[...], some, *sides[0], block)
-        row_grad = core_grad if piece % 2 else home_grad
-        row_grad[piece // 2] += row_part
+        row_grads[piece][...] += row_part
         total = col_part if total is None else total + col_part
         weight[step, at, :], target[step, at, :] = sides[1]
     col_grad[0] = total
 
 
-def other_kernel(block, seat, own, core, chip, both, cols, weight, target, *rest):
-    home_before, core_before, home_grad, core_grad, col_grad = rest
+def other_kernel(block, earlier, seat, own, core, chip, both, cols, weight, target, *rest):
+    grads, sums = rest[: 4 + 4 * earlier], rest[4 + 4 * earlier : -1]
+    col_grad = rest[-1]
     size = own.shape[0]
     for unit in range(cols.shape[0]):
         total = None
@@ -186,9 +193,9 @@
             row_part, col_part = block_terms(
                 ref[...], cols[unit], weight[unit, at, :], target[unit, at, :], block
             )
-            row_grad = core_grad if piece % 2 else home_grad
-            before = row_grad if unit else (core_before if piece % 2 else home_before)
-            row_grad[piece // 2] = before[piece // 2] + row_part
+            for before in [sums[piece]] if unit else grads[piece::4]:
+                row_part = row_part + before[...]
+            sums[piece][...] = row_part
             total = col_part if total is None else total + col_part
         col_grad[unit] = total.astype(col_grad.dtype)
 
@@ -198,7 +205,7 @@
     units, both, _ = cols.shape
     slots, block = counts.shape[2:4]
     halves = block // 2 // LANES
-    grad_shape = pltpu.VMEM((2, size, width), jnp.float32)
+    grad_shape = pltpu.VMEM((size, width), jnp.float32)
     term_shape = pltpu.VMEM((units, block, both), jnp.float32)
     col_spec = pl.BlockSpec((1, both, width), lambda unit, seat: (unit, 0, 0))
 
@@ -213,25 +220,31 @@
     return in_order(
         functools.partial(own_kernel, start, slots),
         tokens,
-        [grad_shape, grad_shape, pltpu.HBM(cols.shape, jnp.float32), term_shape, term_shape],
+        [grad_shape] * 4 + [pltpu.HBM(cols.shape, jnp.float32), term_shape, term_shape],
         [whole] * 6 + [col_spec] + count_specs,
-        [whole, whole, col_spec, whole, whole],
+        [whole] * 4 + [col_spec, whole, whole],
         grid=(units,),
         vmem=32,
         scalars=seat,
     )(row_term, col_freq, *rows, cols, *[counts] * (2 * slots))
 
 
-def other_grads(seat, rows, cols, weight, target, before, tokens):
+def other_grads(seat, rows, cols, weight, target, before, earlier, tokens):
     size, width = rows[0].shape
-    grad_shape = jax.ShapeDtypeStruct((2, size, width), jnp.float32)
+    grad_shape = jax.ShapeDtypeStruct((size, width), jnp.float32)
     return in_order(
-        functools.partial(other_kernel, weight.shape[1]),
+        functools.partial(other_kernel, weight.shape[1], len(earlier)),
         tokens,
-        [grad_shape, grad_shape, pltpu.HBM(cols.shape, jnp.bfloat16)],
-        [smalls] + [whole] * 9,
-        vmem=24,
-    )(seat, *rows, cols, *in_vmem(weight, target, *before))
+        [grad_shape] * 4 + [pltpu.HBM(cols.shape, jnp.bfloat16)],
+        [smalls] + [whole] * (11 + 4 * len(earlier)),
+        vmem=32,
+    )(
+        seat,
+        *rows,
+        cols,
+        *in_vmem(weight, target, *before),
+        *[grad for grads in earlier for grad in grads],
+    )
 
 
 def sum_kernel(slots, seat, mine, theirs, home, near, far, cross):
@@ -261,6 +274,51 @@
         ],
         [smalls, whole, whole],
     )(seat, mine, theirs)
+
+
+def relay_kernel(near, far, cross, near_out, far_out):
+    near_out[...] = near[...]
+    far_out[...] = (far[...] + cross[...].astype(jnp.float32)).astype(far_out.dtype)
+
+
+def relayed(near, far, cross, tokens):
+    shape = jax.ShapeDtypeStruct(far.shape, jnp.bfloat16)
+    return in_order(relay_kernel, tokens, [shape] * 2, [whole] * 3, vmem=4)(near, far, cross)
+
+
+def add_kernel(left, right, out):
+    out[...] = (left[...] + right[...]).astype(out.dtype)
+
+
+def added(left, right, tokens):
+    shape = jax.ShapeDtypeStruct(left.shape, jnp.bfloat16)
+    return in_order(add_kernel, tokens, [shape], [whole] * 2, vmem=4)(left, right)
+
+
+def update_kernel(embed, accum, home, near, far, *rest):
+    embed_new, accum_new = rest[-2:]
+    grad = home[...] + near[...].astype(jnp.float32) + far[...].astype(jnp.float32)
+    total = accum[...] + grad * grad
+    accum_new[...] = total
+    embed_new[...] = embed[...] - learn_rate * grad / jnp.sqrt(total)
+
+
+def updated(embed, accum, start, sums, before, tokens):
+    units, _, width = sums[0].shape
+    shape = jax.ShapeDtypeStruct(embed.shape, jnp.float32)
+    outer = pl.BlockSpec((1, LANES, width), lambda unit: (0, start + unit, 0))
+    inner = pl.BlockSpec((1, LANES, width), lambda unit: (unit, 0, 0))
+    count = len(tokens) + 5
+    return in_order(
+        update_kernel,
+        tokens,
+        [shape, shape],
+        [outer, outer, inner, inner, inner] + [anywhere] * len(before),
+        [outer, outer],
+        grid=(units,),
+        vmem=8,
+        aliases={count + i: i for i in range(len(before))},
+    )(*in_hbm(embed, accum), *sums, *before)
 
 
 def crossed_body(
@@ -301,80 +359,112 @@
 
     starts = [sum(CUTS[:part]) for part in range(len(CUTS))]
 
-    def spread_cols(part, *tokens):
-        own, done = halved(col_embed, starts[part], CUTS[part], tokens)
-        far = swap(f"cols_far_{part}", own, "row", far_swap)
+    def far_cols(part, own):
+        return own, swap(f"cols_far_{part}", own, "row", far_swap)
+
+    def near_cols(part, own, far):
         near = swap(f"cols_near_{part}", own, "row", near_swap)
-        return (own, near, far), done
-
-    def all_cols(part, own, near, far):
         return own, near, far, swap(f"cols_cross_{part}", far, "row", near_swap)
 
-    cols_0, done = spread_cols(0)
-    row_half = row_embed.astype(jnp.bfloat16)
+    cols = near_cols(0, *far_cols(0, col_embed[0, : CUTS[0] * LANES].astype(jnp.bfloat16)))
+    row_half, done = halved(row_embed, 0, row_embed.shape[0], cols[:1])
     core_rows = swap("core_rows", row_half, "col", core_swap)
     chip_rows = swap("chip_rows", row_half, "col", chip_swap)
     both_rows = swap("both_rows", chip_rows, "col", core_swap)
     rows = (row_half, core_rows, chip_rows, both_rows)
+    parts = len(CUTS)
+
+    def own_cols(part, *tokens):
+        if part >= parts:
+            return None, tokens[0]
+        return halved(col_embed, starts[part] * LANES, CUTS[part] * LANES, tokens)
+
+    own_next, done = own_cols(1, done)
+    coming = far_cols(1, *gated((own_next,), (*cols[1:3], done)))
     row_term = (jnp.log(row_freq.astype(jnp.float32)) - log_total)[:, None]
 
     def own(part, cols, done):
-        home_grad, core_grad, col_grad, *terms, done = own_grads(
+        *grads, col_grad, weight, target, done = own_grads(
             seat, row_term, col_freq, rows, cols, counts, starts[part], (done,)
         )
-        return (home_grad, core_grad), col_grad, terms, done
-
-    def other(cols, terms, before, *tokens):
-        home_grad, core_grad, col_grad, done = other_grads(
-            seat, rows, cols, *terms, before, tokens
-        )
-        return (home_grad, core_grad), col_grad, done
-
-    parts = len(CUTS)
-    cols, row_grads, summed, sent = all_cols(0, *cols_0), [], [], ()
+        return grads, col_grad, (weight, target), done
+
+    def other(cols, terms, before, earlier, done):
+        *grads, col_grad, done = other_grads(seat, rows, cols, *terms, before, earlier, (done,))
+        return grads, col_grad, done
+
+    row_grads, col_new, sent = [], (), None
+
+    def pick_part(part, cols, coming, *tokens):
+        if coming is not None:
+            tokens += coming[1:]
+        asked, kept, done = picked(seat, cols, slots, tokens)
+        received = swap(f"cols_mate_{part}", asked, "row", mate_swap)
+        after_next = None
+        if coming is not None:
+            cols = near_cols(part + 1, *gated(coming, (done,)))
+            own_next, done = own_cols(part + 2, done)
+            if own_next is not None:
+                after_next = far_cols(part + 2, own_next)
+        return kept, received, cols, after_next, done
 
     def sum_part(part, mine, from_mate, *tokens):
         home_sum, near, far, cross, done = block_sums(seat, mine, from_mate, slots, tokens)
         cross = swap(f"grads_cross_{part}", cross, "row", near_swap)
         return (home_sum, near, far, cross), done
 
-    def send_part(part, sums):
+    def send_part(part, sums, *tokens):
         home_sum, near, far, cross = sums
-        far = (far + cross.astype(jnp.float32)).astype(jnp.bfloat16)
+        near, far, done = relayed(near, far, cross, tokens)
         near = swap(f"grads_near_{part}", near, "row", near_swap)
         far = swap(f"grads_far_{part}", far, "row", far_swap)
-        total = home_sum + near.astype(jnp.float32) + far.astype(jnp.float32)
-        summed.append(total.reshape(-1, width))
-        return near, far
-
+        return (home_sum, near, far), done
+
+    def update_part(part, sums, *tokens):
+        *new, done = updated(col_embed, col_accum, starts[part], sums, col_new, tokens)
+        return new, done
+
+    *_, cross = cols
+    cols = (*cols[:3], *gated((cross,), (done,)))
+    kept, received, cols, coming, done = pick_part(0, cols, coming, done, core_rows, both_rows)
     for part in range(parts):
-        asked, kept, done = picked(seat, cols, slots, (done, both_rows))
-        received = swap(f"cols_mate_{part}", asked, "row", mate_swap)
-        if part + 1 < parts:
-            cols, done = spread_cols(part + 1, done)
         own_rows, mine, terms, done = own(part, kept, done)
         if part + 1 < parts:
-            own_cols, near, far = cols
-            cols = all_cols(part + 1, own_cols, near, gated(far, done, near))
+            kept, received_next, cols, coming, done = pick_part(
+                part + 1, cols, coming, done, received
+            )
+        earlier = row_grads if part + 1 == parts else []
+        other_rows, theirs, done = other(received, terms, own_rows, earlier, done)
+        from_mate = swap(f"grads_mate_{part}", theirs, "row", mate_swap)
         if part:
-            sums, done = sum_part(part - 1, *waiting, done, *sent)
-            sent = send_part(part - 1, sums)
-            other_rows, theirs, done = other(received, terms, own_rows, done, sums[3])
-        else:
-            other_rows, theirs, done = other(received, terms, own_rows, done)
+            if sent:
+                col_new, done = update_part(part - 2, sent, done)
+            sums, done = sum_part(part - 1, *waiting, done)
+            if part + 1 == parts:
+                home_grad, core_grad, chip_grad, both_grad = other_rows
+                both_core = swap("row_grads_both", both_grad, "col", core_swap)
+                from_core = swap("row_grads_core", core_grad, "col", core_swap)
+                chip_sum, done = added(chip_grad, both_core, (done,))
+                from_chip = swap("row_grads_chip", chip_sum, "col", chip_swap)
+                own_grad = home_grad + from_core + from_chip.astype(jnp.float32)
+                row_new = row_updates(
+                    row_embed, row_accum, row_freq, excluded, block, own_grad
+                )
+            sent, done = send_part(part - 1, sums, done)
         row_grads.append(other_rows)
-        waiting = mine, swap(f"grads_mate_{part}", theirs, "row", mate_swap)
-
-    home_grad, core_grad = [sum(pieces[1:], pieces[0]) for pieces in zip(*row_grads)]
-    from_core = swap("row_grads_core", core_grad, "col", core_swap)
-    chip_grad = (home_grad[1] + from_core[1]).astype(jnp.bfloat16)
-    from_chip = swap("row_grads_chip", chip_grad, "col", chip_swap)
-    own_grad = home_grad[0] + from_core[0] + from_chip.astype(jnp.float32)
-    row_new = row_updates(row_embed, row_accum, row_freq, excluded, block, own_grad)
-
-    sums, done = sum_part(parts - 1, *waiting, done, *sent)
-    send_part(parts - 1, sums)
-    return (*row_new, *col_updates(col_embed, col_accum, jnp.concatenate(summed, axis=0)))
+        waiting = mine, from_mate
+        received = received_next
+
+    sums, done = sum_part(parts - 1, *waiting, done)
+
+
+    *sums, cross = sums
+    passed = gated(sent[:1], (*sent[1:], done)) if sent else ()
+    last, done = send_part(parts - 1, (*sums, cross), done, *passed, row_new[1])
+    if sent:
+        col_new, done = update_part(parts - 2, (*passed, *sent[1:]), done)
+    col_new, done = update_part(parts - 1, last, done)
+    return (*row_new, *col_new)
 
 
 def row_updates(row_embed, row_accum, row_freq, excluded, block, own_grad):

time: 129 us -> 117 us (0.907)
  waiting for transfers between devices: 48.7 us -> 34.8 us
  other arithmetic: 9.87 us -> 2.49 us
  Pallas kernels: 34.7 us -> 42 us
  starting transfers between devices: 27.9 us -> 31.9 us
  local copies, waits for them, and re-layouts: 6.18 us -> 3.44 us
    ppermute x22 -> x23, waiting for transfers between devices: 48.7 us -> 34.8 us  [swap(): return lax.ppermute(value, axis, pairs)]
    pallas_call x11 -> x19, Pallas kernels: 34.7 us -> 42 us  [the longest x15 42 us: in_order(): call(*([scalars] if ahead else []), *held(tokens), *args)]
    ppermute x22 -> x23, starting transfers between devices: 27.9 us -> 31.9 us  [swap(): return lax.ppermute(value, axis, pairs)]
    convert_element_type x4 -> x0, other arithmetic: 3.41 us -> none  [the longest x1 1.24 us: crossed_body(): chip_grad = (home_grad[1] + from_core[1]).astype(jnp.bfloat16)]
    unnamed x38 -> x34, local copies, waits for them, and re-layouts: 5.22 us -> 2.05 us
    sub x1 -> x0, other arithmetic: 1.68 us -> none  [col_updates(): col_embed_new = col_embed - learn_rate * col_step / jnp.sqrt(col_accum_new)]
    add x4 -> x0, other arithmetic: 1.59 us -> none  [the longest x2 1.39 us: crossed_body(): sum(pieces[1:], pieces[0])]
  transfers between devices with their start and end apart: 22 -> 23, of which waited for: 10 -> 10; matrix products, arithmetic and copies ran while one was open for 6% -> 2% of each run, Pallas kernels for 22% -> 30%
where the time goes in v3:
time: 117 us; the launch traced here: 116 us
  Pallas kernels  42 us (36%)
  waiting for transfers between devices  34.8 us (30%)
  starting transfers between devices  31.9 us (27%)
  local copies, waits for them, and re-layouts  3.44 us (3%)
  other arithmetic  2.49 us (2%)
  between operations  1.51 us (1%)
    pallas_call x15, Pallas kernels, in_order(): call(*([scalars] if ahead else []), *held(tokens), *args)  42 us
    ppermute x23, waiting for transfers between devices, swap(): return lax.ppermute(value, axis, pairs)  34.8 us
    ppermute x23, starting transfers between devices, swap(): return lax.ppermute(value, axis, pairs)  31.9 us
  transfers between devices with their start and end apart: 23, of which 10 were waited for; matrix products, arithmetic and copies ran while one was open for 2% of the time, Pallas kernels for 30%

profile of v3, /device:TPU:0, one launch (start us, length us, event | category | flops | bytes accessed | tf_op | source)
XLA Modules:
  0.0 116.0 jit_solution(12313652665258287723)
XLA Ops:
  1.7 4.1 %collective-permute-start.5 = (bf16[256,512]{1,0:T(8,128)(2,1)S(1)}, bf16[256,512]{1,0:T(8,128)(2,1)S(1)}, u32[]{:S(2)}, u32[]{:S(2)}) collective-permute-start(bf16[256,512]{1,0:T(8,128)(2,1)S(1)} %fusion.refs_0_.refs_5_), channel_id=1, source_target_pairs={{0,16},{4,20},{8,24},{12,28},{16,0},{20,4},{24,8},{28,12},{1,17},{... | collective-permute-start | bytes 786440 | tf_op jit(solution)/shard_map/cols_far_0/ppermute | solution.py:352
  5.8 1.6 %collective-permute-start.4 = (bf16[256,512]{1,0:T(8,128)(2,1)S(1)}, bf16[256,512]{1,0:T(8,128)(2,1)S(1)}, u32[]{:S(2)}, u32[]{:S(2)}) collective-permute-start(bf16[256,512]{1,0:T(8,128)(2,1)S(1)} %fusion.refs_0_.refs_5_), channel_id=1, source_target_pairs={{0,8},{4,12},{8,0},{12,4},{16,24},{20,28},{24,16},{28,20},{1,9},{5... | collective-permute-start | bytes 786440 | tf_op jit(solution)/shard_map/cols_near_0/ppermute | solution.py:352
  7.4 1.6 %shard_map.129 = (bf16[256,512]{1,0:T(8,128)(2,1)S(1)}, f32[8,128]{1,0:T(8,128)}) custom-call(bf16[256,512]{1,0:T(8,128)(2,1)S(1)} %fusion.refs_0_.refs_5_, f32[256,512]{1,0:T(8,128)} %refs_1_.4), custom_call_target="tpu_custom_call" | custom-call | flops 1 | bytes 1 | tf_op jit(solution)/shard_map/pallas_call | solution.py:57
  9.0 1.5 %collective-permute-start.2 = (bf16[256,512]{1,0:T(8,128)(2,1)S(1)}, bf16[256,512]{1,0:T(8,128)(2,1)S(1)}, u32[]{:S(2)}, u32[]{:S(2)}) collective-permute-start(bf16[256,512]{1,0:T(8,128)(2,1)S(1)} %get-tuple-element.69.refs_4_.refs_2_), channel_id=1, source_target_pairs={{0,2},{1,3},{2,0},{3,1},{4,6},{5,7},{6,4},{7,5},{8,10},{9,11},{10,... | collective-permute-start | bytes 786440 | tf_op jit(solution)/shard_map/chip_rows/ppermute | solution.py:352
  10.5 1.5 %collective-permute-start = (s32[2]{0:T(128)}, s32[2]{0:T(128)S(1)}, u32[]{:S(2)}, u32[]{:S(2)}) collective-permute-start(s32[2]{0:T(128)} %bitcast.8), channel_id=1, source_target_pairs={{0,4},{4,0},{8,12},{12,8},{16,20},{20,16},{24,28},{28,24},{1,5},{5... | collective-permute-start | bytes 32 | tf_op jit(solution)/shard_map/mate_chosen/ppermute | solution.py:352
  12.1 1.6 %shard_map.130 = (bf16[256,512]{1,0:T(8,128)(2,1)S(1)}, f32[8,128]{1,0:T(8,128)}) custom-call(f32[8,128]{1,0:T(8,128)} %get-tuple-element.67.refs_0_, f32[1,512,512]{2,1,0:T(8,128)} %refs_1_.7), custom_call_target="tpu_custom_call" | custom-call | flops 1 | bytes 1 | tf_op jit(solution)/shard_map/pallas_call | solution.py:57
  13.7 4.2 %collective-permute-done.5.refs_2_.refs_7_ = bf16[256,512]{1,0:T(8,128)(2,1)S(1)} collective-permute-done((bf16[256,512]{1,0:T(8,128)(2,1)S(1)}, bf16[256,512]{1,0:T(8,128)(2,1)S(1)}, u32[]{:S(2)}, u32[]{:S(2)}) %collective-permute-start.5) | collective-permute-done | bytes 262176 | tf_op jit(solution)/shard_map/cols_far_0/ppermute | solution.py:352
  19.4 2.4 %collective-permute-start.7 = (bf16[256,512]{1,0:T(8,128)(2,1)S(1)}, bf16[256,512]{1,0:T(8,128)(2,1)S(1)}, u32[]{:S(2)}, u32[]{:S(2)}) collective-permute-start(bf16[256,512]{1,0:T(8,128)(2,1)S(1)} %collective-permute-done.5.refs_2_.refs_7_), channel_id=1, source_target_pairs={{0,8},{4,12},{8,0},{12,4},{16,24},{20,28},{24,16},{28,20},{1,9},{5... | collective-permute-start | bytes 786440 | tf_op jit(solution)/shard_map/cols_cross_0/ppermute | solution.py:352
  22.0 10.0 %collective-permute-done.7.refs_0_ = bf16[256,512]{1,0:T(8,128)(2,1)S(1)} collective-permute-done((bf16[256,512]{1,0:T(8,128)(2,1)S(1)}, bf16[256,512]{1,0:T(8,128)(2,1)S(1)}, u32[]{:S(2)}, u32[]{:S(2)}) %collective-permute-start.7) | collective-permute-done | bytes 262176 | tf_op jit(solution)/shard_map/cols_cross_0/ppermute | solution.py:352
  32.0 1.9 %shard_map.133 = (bf16[2,256,512]{2,1,0:T(8,128)(2,1)}, bf16[2,256,512]{2,1,0:T(8,128)(2,1)S(1)}, f32[8,128]{1,0:T(8,128)}) custom-call(f32[8,128]{1,0:T(8,128)} %get-tuple-element.68.refs_3_.refs_1_.refs_0_, bf16[256,512]{1,0:T(8,128)(2,1)S(1)} %collective-permute-done.1.refs_1_.refs_5_.refs_3_, ...), custom_call_target="tpu_custom_call" | custom-call | flops 1 | bytes 1 | tf_op jit(solution)/shard_map/pallas_call | solution.py:57
  35.8 1.5 %collective-permute-start.10 = (bf16[256,512]{1,0:T(8,128)(2,1)S(1)}, bf16[256,512]{1,0:T(8,128)(2,1)}, u32[]{:S(2)}, u32[]{:S(2)}) collective-permute-start(bf16[256,512]{1,0:T(8,128)(2,1)S(1)} %get-tuple-element.76.refs_5_), channel_id=1, source_target_pairs={{0,8},{4,12},{8,0},{12,4},{16,24},{20,28},{24,16},{28,20},{1,9},{5... | collective-permute-start | bytes 786440 | tf_op jit(solution)/shard_map/cols_cross_1/ppermute | solution.py:352
  38.2 7.6 %shard_map.134 = (f32[256,512]{1,0:T(8,128)S(1)}, f32[256,512]{1,0:T(8,128)S(1)}, f32[256,512]{1,0:T(8,128)S(1)}, f32[256,512]{1,0:T(8,128)S(1)}, f32[2,256,512]...) custom-call(s32[8]{0:T(128)S(1)} %concatenate.3.refs_4_.refs_0_.refs_2_.refs_1_, ...), custom_call_target="tpu_custom_call" | custom-call | flops 1 | bytes 1 | tf_op jit(solution)/shard_map/pallas_call | solution.py:57
  46.8 2.0 %shard_map.136 = (bf16[2,256,512]{2,1,0:T(8,128)(2,1)S(1)}, bf16[2,256,512]{2,1,0:T(8,128)(2,1)S(1)}, f32[8,128]{1,0:T(8,128)}) custom-call(f32[8,128]{1,0:T(8,128)} %get-tuple-element.73.refs_0_, bf16[2,256,512]{2,1,0:T(8,128)(2,1)S(1)} %collective-permute-done.8.refs_1_.refs_6_, s32[8]{0:T(128)S(1)} %concatenate.3.refs_4_.refs_0_.refs_2_.refs_1_, ...), custom_call_target="tpu_custom_call" | custom-call | flops 1 | bytes 1 | tf_op jit(solution)/shard_map/pallas_call | solution.py:57
  49.8 4.1 %shard_map.137 = (f32[256,512]{1,0:T(8,128)S(1)}, f32[256,512]{1,0:T(8,128)S(1)}, f32[256,512]{1,0:T(8,128)S(1)}, f32[256,512]{1,0:T(8,128)S(1)}, bf16[2,256,512]{2,1,0:T(8,128)(2,1)}, /*index=5*/f32[8,128]{1,0:T(8,128)}) custom-call(f32[8,128]{1,0:T(8,128)} %get-tuple-element.77.refs_0_, s32[8]{0:T(128)S(1)} %concatenate.3.refs_4_.refs_0_.refs_2_.refs_1_, ...), custom_call_target="tpu_custom_call" | custom-call | flops 1 | bytes 1 | tf_op jit(solution)/shard_map/pallas_call | solution.py:57
  54.9 7.6 %shard_map.138 = (f32[256,512]{1,0:T(8,128)S(1)}, f32[256,512]{1,0:T(8,128)S(1)}, f32[256,512]{1,0:T(8,128)S(1)}, f32[256,512]{1,0:T(8,128)S(1)}, f32[2,256,512]...) custom-call(s32[8]{0:T(128)S(1)} %concatenate.3.refs_4_.refs_0_.refs_2_.refs_1_, ...), custom_call_target="tpu_custom_call" | custom-call | flops 1 | bytes 1 | tf_op jit(solution)/shard_map/pallas_call | solution.py:57
  63.7 4.4 %shard_map.139 = (f32[256,512]{1,0:T(8,128)S(1)}, f32[256,512]{1,0:T(8,128)}, f32[256,512]{1,0:T(8,128)S(1)}, f32[256,512]{1,0:T(8,128)}, bf16[2,256,512]{2,1,0:T(8,128)(2,1)}, /*index=5*/f32[8,128]{1,0:T(8,128)}) custom-call(f32[8,128]{1,0:T(8,128)} %get-tuple-element.86.refs_0_, s32[8]{0:T(128)S(1)} %concatenate.3.refs_4_.refs_0_.refs_2_.refs_1_, ...), custom_call_target="tpu_custom_call" | custom-call | flops 1 | bytes 1 | tf_op jit(solution)/shard_map/pallas_call | solution.py:57
  68.1 2.6 %collective-permute-done.13.refs_3_ = bf16[2,256,512]{2,1,0:T(8,128)(2,1)S(1)} collective-permute-done((bf16[2,256,512]{2,1,0:T(8,128)(2,1)}, bf16[2,256,512]{2,1,0:T(8,128)(2,1)S(1)}, u32[]{:S(2)}, u32[]{:S(2)}) %collective-permute-start.13) | collective-permute-done | bytes 524320 | tf_op jit(solution)/shard_map/grads_mate_0/ppermute | solution.py:352
  70.7 1.9 %shard_map.140 = (f32[2,128,512]{2,1,0:T(8,128)}, bf16[2,128,512]{2,1,0:T(8,128)(2,1)}, f32[2,128,512]{2,1,0:T(8,128)S(1)}, bf16[2,128,512]{2,1,0:T(8,128)(2,1)}, f32[8,128]{1,0:T(8,128)}) custom-call(f32[8,128]{1,0:T(8,128)} %get-tuple-element.100.refs_0_, s32[8]{0:T(128)S(1)} %concatenate.3.refs_4_.refs_0_.refs_2_.refs_1_, f32[2,256,512]{2,1,0:T(8,128)S(1)} %copy-done.5, ...), custom_call_target="tpu_custom_call" | custom-call | flops 1 | bytes 1 | tf_op jit(solution)/shard_map/pallas_call | solution.py:57
  72.6 2.6 %collective-permute-start.16 = (bf16[2,128,512]{2,1,0:T(8,128)(2,1)}, bf16[2,128,512]{2,1,0:T(8,128)(2,1)S(1)}, u32[]{:S(2)}, u32[]{:S(2)}) collective-permute-start(bf16[2,128,512]{2,1,0:T(8,128)(2,1)} %get-tuple-element.110), channel_id=1, source_target_pairs={{0,8},{4,12},{8,0},{12,4},{16,24},{20,28},{24,16},{28,20},{1,9},{5... | collective-permute-start | bytes 786440 | tf_op jit(solution)/shard_map/grads_cross_0/ppermute | solution.py:352
  77.0 1.8 %shard_map.141 = (bf16[256,512]{1,0:T(8,128)(2,1)}, f32[8,128]{1,0:T(8,128)}) custom-call(f32[8,128]{1,0:T(8,128)} %get-tuple-element.103.refs_0_, f32[256,512]{1,0:T(8,128)S(1)} %copy-done.8, f32[256,512]{1,0:T(8,128)} %collective-permute-done.14.refs_2_), custom_call_target="tpu_custom_call" | custom-call | flops 1 | bytes 1 | tf_op jit(solution)/shard_map/pallas_call | solution.py:57
  81.6 2.0 %collective-permute-start.18 = (bf16[2,128,512]{2,1,0:T(8,128)(2,1)}, bf16[2,128,512]{2,1,0:T(8,128)(2,1)S(1)}, u32[]{:S(2)}, u32[]{:S(2)}) collective-permute-start(bf16[2,128,512]{2,1,0:T(8,128)(2,1)} %get-tuple-element.116), channel_id=1, source_target_pairs={{0,8},{4,12},{8,0},{12,4},{16,24},{20,28},{24,16},{28,20},{1,9},{5... | collective-permute-start | bytes 786440 | tf_op jit(solution)/shard_map/grads_near_0/ppermute | solution.py:352
  83.6 3.3 %collective-permute-start.19 = (bf16[2,128,512]{2,1,0:T(8,128)(2,1)}, bf16[2,128,512]{2,1,0:T(8,128)(2,1)S(1)}, u32[]{:S(2)}, u32[]{:S(2)}) collective-permute-start(bf16[2,128,512]{2,1,0:T(8,128)(2,1)} %get-tuple-element.117), channel_id=1, source_target_pairs={{0,16},{4,20},{8,24},{12,28},{16,0},{20,4},{24,8},{28,12},{1,17},{... | collective-permute-start | bytes 786440 | tf_op jit(solution)/shard_map/grads_far_0/ppermute | solution.py:352
  86.8 1.5 %collective-permute-start.15 = (bf16[256,512]{1,0:T(8,128)(2,1)}, bf16[256,512]{1,0:T(8,128)(2,1)}, u32[]{:S(2)}, u32[]{:S(2)}) collective-permute-start(bf16[256,512]{1,0:T(8,128)(2,1)} %get-tuple-element.106), channel_id=1, source_target_pairs={{0,2},{1,3},{2,0},{3,1},{4,6},{5,7},{6,4},{7,5},{8,10},{9,11},{10,... | collective-permute-start | bytes 786440 | tf_op jit(solution)/shard_map/row_grads_chip/ppermute | solution.py:352
  88.7 1.8 %shard_map.143 = (f32[2,128,512]{2,1,0:T(8,128)}, bf16[2,128,512]{2,1,0:T(8,128)(2,1)}, f32[2,128,512]{2,1,0:T(8,128)S(1)}, bf16[2,128,512]{2,1,0:T(8,128)(2,1)S(1)}, f32[8,128]{1,0:T(8,128)}) custom-call(f32[8,128]{1,0:T(8,128)} %get-tuple-element.111.refs_0_, s32[8]{0:T(128)S(1)} %concatenate.3.refs_4_.refs_0_.refs_2_.refs_1_, ...), custom_call_target="tpu_custom_call" | custom-call | flops 1 | bytes 1 | tf_op jit(solution)/shard_map/pallas_call | solution.py:57
  90.7 5.9 %collective-permute-done.18.refs_1_.refs_4_ = bf16[2,128,512]{2,1,0:T(8,128)(2,1)S(1)} collective-permute-done((bf16[2,128,512]{2,1,0:T(8,128)(2,1)}, bf16[2,128,512]{2,1,0:T(8,128)(2,1)S(1)}, u32[]{:S(2)}, u32[]{:S(2)}) %collective-permute-start.18) | collective-permute-done | bytes 262176 | tf_op jit(solution)/shard_map/grads_near_0/ppermute | solution.py:352
  96.7 2.2 %multiply_subtract_fusion = (f32[256,512]{1,0:T(8,128)}, f32[256,512]{1,0:T(8,128)S(1)}) fusion(f32[256,512]{1,0:T(8,128)S(1)} %copy-done.12, f32[256]{0:T(256)S(1)} %fusion.1, bf16[256,512]{1,0:T(8,128)(2,1)} %collective-permute-done.15, f32[256,512]{1,0:T(8,128)S(1)} %get-tuple-element.98, f32[256,512]{1,0:T(8,128)} %collective-permute-done.12, ...), kind=kLoop, calls=%fused_computation.1 | loop fusion | flops 1310720 | bytes 3408896 | tf_op jit(solution)/shard_map/sub | solution.py:483
  98.9 1.9 %collective-permute-done.20.refs_5_ = bf16[2,128,512]{2,1,0:T(8,128)(2,1)S(1)} collective-permute-done((bf16[2,128,512]{2,1,0:T(8,128)(2,1)S(1)}, bf16[2,128,512]{2,1,0:T(8,128)(2,1)S(1)}, u32[]{:S(2)}, u32[]{:S(2)}) %collective-permute-start.20) | collective-permute-done | bytes 262176 | tf_op jit(solution)/shard_map/grads_cross_1/ppermute | solution.py:352
  101.5 1.8 %collective-permute-start.21 = (bf16[2,128,512]{2,1,0:T(8,128)(2,1)S(1)}, bf16[2,128,512]{2,1,0:T(8,128)(2,1)S(1)}, u32[]{:S(2)}, u32[]{:S(2)}) collective-permute-start(bf16[2,128,512]{2,1,0:T(8,128)(2,1)S(1)} %get-tuple-element.124), channel_id=1, source_target_pairs={{0,8},{4,12},{8,0},{12,4},{16,24},{20,28},{24,16},{28,20},{1,9},{5... | collective-permute-start | bytes 786440 | tf_op jit(solution)/shard_map/grads_near_1/ppermute | solution.py:352
  103.2 1.8 %collective-permute-start.22 = (bf16[2,128,512]{2,1,0:T(8,128)(2,1)S(1)}, bf16[2,128,512]{2,1,0:T(8,128)(2,1)S(1)}, u32[]{:S(2)}, u32[]{:S(2)}) collective-permute-start(bf16[2,128,512]{2,1,0:T(8,128)(2,1)S(1)} %get-tuple-element.125), channel_id=1, source_target_pairs={{0,16},{4,20},{8,24},{12,28},{16,0},{20,4},{24,8},{28,12},{1,17},{... | collective-permute-start | bytes 786440 | tf_op jit(solution)/shard_map/grads_far_1/ppermute | solution.py:352
  105.0 2.1 %shard_map.146 = (f32[1,512,512]{2,1,0:T(8,128)}, f32[1,512,512]{2,1,0:T(8,128)}, f32[8,128]{1,0:T(8,128)}) custom-call(f32[8,128]{1,0:T(8,128)} %get-tuple-element.121.refs_0_, f32[1,512,512]{2,1,0:T(8,128)} %refs_1_.7, f32[1,512,512]{2,1,0:T(8,128)} %refs_2_.3, f32[2,128,512]{2,1,0:T(8,128)S(1)} %shard_map.144.refs_1_.refs_3_, ...), custom_call_target="tpu_custom_call" | custom-call | flops 1 | bytes 1 | tf_op jit(solution)/shard_map/pallas_call | solution.py:57
  107.1 6.9 %collective-permute-done.21.refs_4_ = bf16[2,128,512]{2,1,0:T(8,128)(2,1)S(1)} collective-permute-done((bf16[2,128,512]{2,1,0:T(8,128)(2,1)S(1)}, bf16[2,128,512]{2,1,0:T(8,128)(2,1)S(1)}, u32[]{:S(2)}, u32[]{:S(2)}) %collective-permute-start.21) | collective-permute-done | bytes 262176 | tf_op jit(solution)/shard_map/grads_near_1/ppermute | solution.py:352
  114.0 2.1 %shard_map.147 = (f32[1,512,512]{2,1,0:T(8,128)}, f32[1,512,512]{2,1,0:T(8,128)}, f32[8,128]{1,0:T(8,128)}) custom-call(f32[8,128]{1,0:T(8,128)} %get-tuple-element.122.refs_0_, f32[1,512,512]{2,1,0:T(8,128)} %refs_1_.7, f32[1,512,512]{2,1,0:T(8,128)} %refs_2_.3, f32[2,128,512]{2,1,0:T(8,128)S(1)} %copy-done.6, ...), custom_call_target="tpu_custom_call", output_to_operand_aliasing={{0}: (6, {}), {1}: (7, {})} | custom-call | flops 1 | bytes 1 | tf_op jit(solution)/shard_map/pallas_call | solution.py:57
  (77 shorter events, 14.9 us)
Async XLA Ops:
  0.6 21.3 %copy-start.16 = (s32[1,1,2]{2,1,0:T(1,128)S(1)}, s32[1,1,2]{2,1,0:T(1,128)}, u32[]{:S(2)}) copy-start(s32[1,1,2]{2,1,0:T(1,128)} %param.16) | copy-start | bytes 28
  1.7 30.3 %copy-start.1 = (bf16[256,512]{1,0:T(8,128)(2,1)}, bf16[256,512]{1,0:T(8,128)(2,1)S(1)}, u32[]{:S(2)}) copy-start(bf16[256,512]{1,0:T(8,128)(2,1)S(1)} %fusion.refs_0_.refs_5_) | copy-start | bytes 786436
  1.7 16.1 %collective-permute-start.5 = (bf16[256,512]{1,0:T(8,128)(2,1)S(1)}, bf16[256,512]{1,0:T(8,128)(2,1)S(1)}, u32[]{:S(2)}, u32[]{:S(2)}) collective-permute-start(bf16[256,512]{1,0:T(8,128)(2,1)S(1)} %fusion.refs_0_.refs_5_), channel_id=1, source_target_pairs={{0,16},{4,20},{8,24},{12,28},{16,0},{20,4},{24,8},{28,12},{1,17},{... | collective-permute-start | bytes 786440 | tf_op jit(solution)/shard_map/cols_far_0/ppermute | solution.py:352
  5.8 12.2 %collective-permute-start.4 = (bf16[256,512]{1,0:T(8,128)(2,1)S(1)}, bf16[256,512]{1,0:T(8,128)(2,1)S(1)}, u32[]{:S(2)}, u32[]{:S(2)}) collective-permute-start(bf16[256,512]{1,0:T(8,128)(2,1)S(1)} %fusion.refs_0_.refs_5_), channel_id=1, source_target_pairs={{0,8},{4,12},{8,0},{12,4},{16,24},{20,28},{24,16},{28,20},{1,9},{5... | collective-permute-start | bytes 786440 | tf_op jit(solution)/shard_map/cols_near_0/ppermute | solution.py:352
  9.0 12.8 %collective-permute-start.2 = (bf16[256,512]{1,0:T(8,128)(2,1)S(1)}, bf16[256,512]{1,0:T(8,128)(2,1)S(1)}, u32[]{:S(2)}, u32[]{:S(2)}) collective-permute-start(bf16[256,512]{1,0:T(8,128)(2,1)S(1)} %get-tuple-element.69.refs_4_.refs_2_), channel_id=1, source_target_pairs={{0,2},{1,3},{2,0},{3,1},{4,6},{5,7},{6,4},{7,5},{8,10},{9,11},{10,... | collective-permute-start | bytes 786440 | tf_op jit(solution)/shard_map/chip_rows/ppermute | solution.py:352
  10.5 21.5 %collective-permute-start.1 = (bf16[256,512]{1,0:T(8,128)(2,1)S(1)}, bf16[256,512]{1,0:T(8,128)(2,1)S(1)}, u32[]{:S(2)}, u32[]{:S(2)}) collective-permute-start(bf16[256,512]{1,0:T(8,128)(2,1)S(1)} %get-tuple-element.69.refs_4_.refs_2_), channel_id=1, source_target_pairs={{0,1},{1,0},{2,3},{3,2},{4,5},{5,4},{6,7},{7,6},{8,9},{9,8},{10,11... | collective-permute-start | bytes 786440 | tf_op jit(solution)/shard_map/core_rows/ppermute | solution.py:352
  10.5 11.4 %collective-permute-start = (s32[2]{0:T(128)}, s32[2]{0:T(128)S(1)}, u32[]{:S(2)}, u32[]{:S(2)}) collective-permute-start(s32[2]{0:T(128)} %bitcast.8), channel_id=1, source_target_pairs={{0,4},{4,0},{8,12},{12,8},{16,20},{20,16},{24,28},{28,24},{1,5},{5... | collective-permute-start | bytes 32 | tf_op jit(solution)/shard_map/mate_chosen/ppermute | solution.py:352
  13.7 24.2 %copy-start.14 = (s32[1024]{0:T(1024)S(1)}, s32[1024]{0:T(1024)}, u32[]{:S(2)}) copy-start(s32[1024]{0:T(1024)} %param.15) | copy-start | bytes 12292
  18.1 20.1 %copy-start.11 = (s32[1,4096]{1,0:T(1,128)S(1)}, s32[1,4096]{1,0:T(1,128)}, u32[]{:S(2)}) copy-start(s32[1,4096]{1,0:T(1,128)} %refs_3_.3) | copy-start | bytes 49156
  18.1 14.0 %collective-permute-start.6 = (bf16[256,512]{1,0:T(8,128)(2,1)S(1)}, bf16[256,512]{1,0:T(8,128)(2,1)S(1)}, u32[]{:S(2)}, u32[]{:S(2)}) collective-permute-start(bf16[256,512]{1,0:T(8,128)(2,1)S(1)} %shard_map.131.refs_0_), channel_id=1, source_target_pairs={{0,16},{4,20},{8,24},{12,28},{16,0},{20,4},{24,8},{28,12},{1,17},{... | collective-permute-start | bytes 786440 | tf_op jit(solution)/shard_map/cols_far_1/ppermute | solution.py:352
  19.4 12.6 %collective-permute-start.7 = (bf16[256,512]{1,0:T(8,128)(2,1)S(1)}, bf16[256,512]{1,0:T(8,128)(2,1)S(1)}, u32[]{:S(2)}, u32[]{:S(2)}) collective-permute-start(bf16[256,512]{1,0:T(8,128)(2,1)S(1)} %collective-permute-done.5.refs_2_.refs_7_), channel_id=1, source_target_pairs={{0,8},{4,12},{8,0},{12,4},{16,24},{20,28},{24,16},{28,20},{1,9},{5... | collective-permute-start | bytes 786440 | tf_op jit(solution)/shard_map/cols_cross_0/ppermute | solution.py:352
  21.9 10.1 %collective-permute-start.3 = (bf16[256,512]{1,0:T(8,128)(2,1)S(1)}, bf16[256,512]{1,0:T(8,128)(2,1)S(1)}, u32[]{:S(2)}, u32[]{:S(2)}) collective-permute-start(bf16[256,512]{1,0:T(8,128)(2,1)S(1)} %collective-permute-done.2.refs_6_.refs_4_), channel_id=1, source_target_pairs={{0,1},{1,0},{2,3},{3,2},{4,5},{5,4},{6,7},{7,6},{8,9},{9,8},{10,11... | collective-permute-start | bytes 786440 | tf_op jit(solution)/shard_map/both_rows/ppermute | solution.py:352
  34.0 12.8 %collective-permute-start.8 = (bf16[2,256,512]{2,1,0:T(8,128)(2,1)}, bf16[2,256,512]{2,1,0:T(8,128)(2,1)S(1)}, u32[]{:S(2)}, u32[]{:S(2)}) collective-permute-start(bf16[2,256,512]{2,1,0:T(8,128)(2,1)} %get-tuple-element.74), channel_id=1, source_target_pairs={{0,4},{4,0},{8,12},{12,8},{16,20},{20,16},{24,28},{28,24},{1,5},{5... | collective-permute-start | bytes 1572872 | tf_op jit(solution)/shard_map/cols_mate_0/ppermute | solution.py:352
  35.2 10.5 %copy-start.2 = (bf16[256,512]{1,0:T(8,128)(2,1)}, bf16[256,512]{1,0:T(8,128)(2,1)S(1)}, u32[]{:S(2)}) copy-start(bf16[256,512]{1,0:T(8,128)(2,1)S(1)} %get-tuple-element.75.refs_3_) | copy-start | bytes 786436
  35.2 10.5 %collective-permute-start.9 = (bf16[256,512]{1,0:T(8,128)(2,1)S(1)}, bf16[256,512]{1,0:T(8,128)(2,1)S(1)}, u32[]{:S(2)}, u32[]{:S(2)}) collective-permute-start(bf16[256,512]{1,0:T(8,128)(2,1)S(1)} %get-tuple-element.75.refs_3_), channel_id=1, source_target_pairs={{0,8},{4,12},{8,0},{12,4},{16,24},{20,28},{24,16},{28,20},{1,9},{5... | collective-permute-start | bytes 786440 | tf_op jit(solution)/shard_map/cols_near_1/ppermute | solution.py:352
  35.8 11.0 %collective-permute-start.10 = (bf16[256,512]{1,0:T(8,128)(2,1)S(1)}, bf16[256,512]{1,0:T(8,128)(2,1)}, u32[]{:S(2)}, u32[]{:S(2)}) collective-permute-start(bf16[256,512]{1,0:T(8,128)(2,1)S(1)} %get-tuple-element.76.refs_5_), channel_id=1, source_target_pairs={{0,8},{4,12},{8,0},{12,4},{16,24},{20,28},{24,16},{28,20},{1,9},{5... | collective-permute-start | bytes 786440 | tf_op jit(solution)/shard_map/cols_cross_1/ppermute | solution.py:352
  48.8 14.9 %collective-permute-start.11 = (bf16[2,256,512]{2,1,0:T(8,128)(2,1)S(1)}, bf16[2,256,512]{2,1,0:T(8,128)(2,1)S(1)}, u32[]{:S(2)}, u32[]{:S(2)}) collective-permute-start(bf16[2,256,512]{2,1,0:T(8,128)(2,1)S(1)} %get-tuple-element.87), channel_id=1, source_target_pairs={{0,4},{4,0},{8,12},{12,8},{16,20},{20,16},{24,28},{28,24},{1,5},{5... | collective-permute-start | bytes 1572872 | tf_op jit(solution)/shard_map/cols_mate_1/ppermute | solution.py:352
  53.9 16.8 %collective-permute-start.13 = (bf16[2,256,512]{2,1,0:T(8,128)(2,1)}, bf16[2,256,512]{2,1,0:T(8,128)(2,1)S(1)}, u32[]{:S(2)}, u32[]{:S(2)}) collective-permute-start(bf16[2,256,512]{2,1,0:T(8,128)(2,1)} %get-tuple-element.102), channel_id=1, source_target_pairs={{0,4},{4,0},{8,12},{12,8},{16,20},{20,16},{24,28},{28,24},{1,5},{5... | collective-permute-start | bytes 1572872 | tf_op jit(solution)/shard_map/grads_mate_0/ppermute | solution.py:352
  68.0 20.3 %copy-start.15 = (s32[512]{0:T(512)S(1)}, s32[512]{0:T(512)}, u32[]{:S(2)}) copy-start(s32[512]{0:T(512)} %param.18) | copy-start | bytes 6148
  68.1 20.6 %copy-start.4 = (f32[2,256,512]{2,1,0:T(8,128)S(1)}, f32[2,256,512]{2,1,0:T(8,128)}, u32[]{:S(2)}) copy-start(f32[2,256,512]{2,1,0:T(8,128)} %get-tuple-element.112.refs_2_) | copy-start | bytes 3145732
  68.1 7.9 %collective-permute-start.14 = (f32[256,512]{1,0:T(8,128)}, f32[256,512]{1,0:T(8,128)}, u32[]{:S(2)}, u32[]{:S(2)}) collective-permute-start(f32[256,512]{1,0:T(8,128)} %get-tuple-element.105), channel_id=1, source_target_pairs={{0,1},{1,0},{2,3},{3,2},{4,5},{5,4},{6,7},{7,6},{8,9},{9,8},{10,11... | collective-permute-start | bytes 1572872 | tf_op jit(solution)/shard_map/row_grads_both/ppermute | solution.py:352
  72.6 24.0 %copy-start = (f32[2,128,512]{2,1,0:T(8,128)S(1)}, f32[2,128,512]{2,1,0:T(8,128)}, u32[]{:S(2)}) copy-start(f32[2,128,512]{2,1,0:T(8,128)} %get-tuple-element.115.refs_0_) | copy-start | bytes 1572868
  72.6 7.1 %collective-permute-start.16 = (bf16[2,128,512]{2,1,0:T(8,128)(2,1)}, bf16[2,128,512]{2,1,0:T(8,128)(2,1)S(1)}, u32[]{:S(2)}, u32[]{:S(2)}) collective-permute-start(bf16[2,128,512]{2,1,0:T(8,128)(2,1)} %get-tuple-element.110), channel_id=1, source_target_pairs={{0,8},{4,12},{8,0},{12,4},{16,24},{20,28},{24,16},{28,20},{1,9},{5... | collective-permute-start | bytes 786440 | tf_op jit(solution)/shard_map/grads_cross_0/ppermute | solution.py:352
  75.2 13.4 %collective-permute-start.17 = (bf16[2,256,512]{2,1,0:T(8,128)(2,1)}, bf16[2,256,512]{2,1,0:T(8,128)(2,1)S(1)}, u32[]{:S(2)}, u32[]{:S(2)}) collective-permute-start(bf16[2,256,512]{2,1,0:T(8,128)(2,1)} %get-tuple-element.113), channel_id=1, source_target_pairs={{0,4},{4,0},{8,12},{12,8},{16,20},{20,16},{24,28},{28,24},{1,5},{5... | collective-permute-start | bytes 1572872 | tf_op jit(solution)/shard_map/grads_mate_1/ppermute | solution.py:352
  76.0 20.7 %collective-permute-start.12 = (f32[256,512]{1,0:T(8,128)}, f32[256,512]{1,0:T(8,128)}, u32[]{:S(2)}, u32[]{:S(2)}) collective-permute-start(f32[256,512]{1,0:T(8,128)} %get-tuple-element.99), channel_id=1, source_target_pairs={{0,1},{1,0},{2,3},{3,2},{4,5},{5,4},{6,7},{7,6},{8,9},{9,8},{10,11... | collective-permute-start | bytes 1572872 | tf_op jit(solution)/shard_map/row_grads_core/ppermute | solution.py:352
  81.6 15.1 %collective-permute-start.18 = (bf16[2,128,512]{2,1,0:T(8,128)(2,1)}, bf16[2,128,512]{2,1,0:T(8,128)(2,1)S(1)}, u32[]{:S(2)}, u32[]{:S(2)}) collective-permute-start(bf16[2,128,512]{2,1,0:T(8,128)(2,1)} %get-tuple-element.116), channel_id=1, source_target_pairs={{0,8},{4,12},{8,0},{12,4},{16,24},{20,28},{24,16},{28,20},{1,9},{5... | collective-permute-start | bytes 786440 | tf_op jit(solution)/shard_map/grads_near_0/ppermute | solution.py:352
  83.6 13.0 %collective-permute-start.19 = (bf16[2,128,512]{2,1,0:T(8,128)(2,1)}, bf16[2,128,512]{2,1,0:T(8,128)(2,1)S(1)}, u32[]{:S(2)}, u32[]{:S(2)}) collective-permute-start(bf16[2,128,512]{2,1,0:T(8,128)(2,1)} %get-tuple-element.117), channel_id=1, source_target_pairs={{0,16},{4,20},{8,24},{12,28},{16,0},{20,4},{24,8},{28,12},{1,17},{... | collective-permute-start | bytes 786440 | tf_op jit(solution)/shard_map/grads_far_0/ppermute | solution.py:352
  86.8 9.8 %collective-permute-start.15 = (bf16[256,512]{1,0:T(8,128)(2,1)}, bf16[256,512]{1,0:T(8,128)(2,1)}, u32[]{:S(2)}, u32[]{:S(2)}) collective-permute-start(bf16[256,512]{1,0:T(8,128)(2,1)} %get-tuple-element.106), channel_id=1, source_target_pairs={{0,2},{1,3},{2,0},{3,1},{4,6},{5,7},{6,4},{7,5},{8,10},{9,11},{10,... | collective-permute-start | bytes 786440 | tf_op jit(solution)/shard_map/row_grads_chip/ppermute | solution.py:352
  90.4 10.4 %collective-permute-start.20 = (bf16[2,128,512]{2,1,0:T(8,128)(2,1)S(1)}, bf16[2,128,512]{2,1,0:T(8,128)(2,1)S(1)}, u32[]{:S(2)}, u32[]{:S(2)}) collective-permute-start(bf16[2,128,512]{2,1,0:T(8,128)(2,1)S(1)} %get-tuple-element.120), channel_id=1, source_target_pairs={{0,8},{4,12},{8,0},{12,4},{16,24},{20,28},{24,16},{28,20},{1,9},{5... | collective-permute-start | bytes 786440 | tf_op jit(solution)/shard_map/grads_cross_1/ppermute | solution.py:352
  101.5 12.5 %copy-start.6 = (f32[2,128,512]{2,1,0:T(8,128)S(1)}, f32[2,128,512]{2,1,0:T(8,128)}, u32[]{:S(2)}) copy-start(f32[2,128,512]{2,1,0:T(8,128)} %get-tuple-element.123.refs_3_) | copy-start | bytes 1572868
  101.5 12.5 %collective-permute-start.21 = (bf16[2,128,512]{2,1,0:T(8,128)(2,1)S(1)}, bf16[2,128,512]{2,1,0:T(8,128)(2,1)S(1)}, u32[]{:S(2)}, u32[]{:S(2)}) collective-permute-start(bf16[2,128,512]{2,1,0:T(8,128)(2,1)S(1)} %get-tuple-element.124), channel_id=1, source_target_pairs={{0,8},{4,12},{8,0},{12,4},{16,24},{20,28},{24,16},{28,20},{1,9},{5... | collective-permute-start | bytes 786440 | tf_op jit(solution)/shard_map/grads_near_1/ppermute | solution.py:352
  103.2 10.7 %collective-permute-start.22 = (bf16[2,128,512]{2,1,0:T(8,128)(2,1)S(1)}, bf16[2,128,512]{2,1,0:T(8,128)(2,1)S(1)}, u32[]{:S(2)}, u32[]{:S(2)}) collective-permute-start(bf16[2,128,512]{2,1,0:T(8,128)(2,1)S(1)} %get-tuple-element.125), channel_id=1, source_target_pairs={{0,16},{4,20},{8,24},{12,28},{16,0},{20,4},{24,8},{28,12},{1,17},{... | collective-permute-start | bytes 786440 | tf_op jit(solution)/shard_map/grads_far_1/ppermute | solution.py:352
  (8 other events, 44.8 us)

commit v4 on v3

--- a/solution.py
+++ b/solution.py
@@ -127,20 +127,26 @@
 
 def count_terms(count, row_term, col_logs, block):
     safe = jnp.maximum(count, 1).astype(jnp.float32)
-    some = (0.1 / block) + (0.25 / block) * jnp.sqrt(safe)
+    some = (0.1 / block) + (0.25 / block) * (safe * lax.rsqrt(safe))
     return jnp.where(count > 0, some, 0.0), jnp.log(safe) - (row_term + col_logs)
 
 
-def block_terms(rows, cols, weight, target, block):
-    predicted = lax.dot_general(
-        rows, cols, (((1,), (1,)), ((), ())), preferred_element_type=jnp.float32
-    )
-    error = predicted - target
-    hinge_grad = (0.5 / block) * jnp.tanh(0.5 * error) + (0.5 / block)
-    cell = jnp.where(weight > 0.0, weight * error, hinge_grad).astype(jnp.bfloat16)
-    return jnp.dot(cell, cols, preferred_element_type=jnp.float32), lax.dot_general(
-        cell, rows, (((0,), (0,)), ((), ())), preferred_element_type=jnp.float32
-    )
+def block_terms(rows, cols, terms, block):
+    predicted = [
+        lax.dot_general(piece, cols, (((1,), (1,)), ((), ())), preferred_element_type=jnp.float32)
+        for piece in rows
+    ]
+    cells = []
+    for value, (weight, target) in zip(predicted, terms):
+        error = value - target
+        hinge_grad = (0.5 / block) * jnp.tanh(0.5 * error) + (0.5 / block)
+        cells.append(jnp.where(weight > 0.0, weight * error, hinge_grad).astype(jnp.bfloat16))
+    row_parts = [jnp.dot(cell, cols, preferred_element_type=jnp.float32) for cell in cells]
+    col_parts = [
+        lax.dot_general(cell, piece, (((0,), (0,)), ((), ())), preferred_element_type=jnp.float32)
+        for cell, piece in zip(cells, rows)
+    ]
+    return row_parts, sum(col_parts[1:], col_parts[0])
 
 
 def own_kernel(start, slots, seat, row_term, col_freq, own, core, chip, both, cols, *rest):
@@ -159,44 +165,49 @@
         return jnp.log(col_freq[:, pl.ds(pl.multiple_of(at, LANES), LANES)].astype(jnp.float32))
 
     col_logs = [[logs(slot, which) for slot in range(slots)] for which in range(2)]
-    some = cols[0]
-    total = None
-    for piece, ref in enumerate((own, core, chip, both)):
-        at = pl.ds(pl.multiple_of((seat[7] ^ piece) * size, size), size)
-        sides = []
-        for which in range(2):
-            pairs = [
-                count_terms(
-                    counts[which * slots + slot][0, 0, 0, at, :],
-                    row_term[at, :],
-                    col_logs[which][slot],
-                    block,
-                )
-                for slot in range(slots)
-            ]
-            sides.append([jnp.concatenate(pair, axis=1) for pair in zip(*pairs)])
-        row_part, col_part = block_terms(ref[...], some, *sides[0], block)
-        row_grads[piece][...] += row_part
-        total = col_part if total is None else total + col_part
-        weight[step, at, :], target[step, at, :] = sides[1]
+    downs = [pl.ds(pl.multiple_of((seat[7] ^ p) * size, size), size) for p in range(4)]
+
+    def side_terms(at, which):
+        pairs = [
+            count_terms(
+                counts[which * slots + slot][0, 0, 0, at, :],
+                row_term[at, :],
+                col_logs[which][slot],
+                block,
+            )
+            for slot in range(slots)
+        ]
+        return [jnp.concatenate(pair, axis=1) for pair in zip(*pairs)]
+
+    row_parts, total = block_terms(
+        [ref[...] for ref in (own, core, chip, both)],
+        cols[0],
+        [side_terms(at, 0) for at in downs],
+        block,
+    )
+    for row_grad, row_part in zip(row_grads, row_parts):
+        row_grad[...] += row_part
     col_grad[0] = total
+    for at in downs:
+        weight[step, at, :], target[step, at, :] = side_terms(at, 1)
 
 
 def other_kernel(block, earlier, seat, own, core, chip, both, cols, weight, target, *rest):
     grads, sums = rest[: 4 + 4 * earlier], rest[4 + 4 * earlier : -1]
     col_grad = rest[-1]
     size = own.shape[0]
+    downs = [pl.ds(pl.multiple_of((seat[7] ^ p) * size, size), size) for p in range(4)]
     for unit in range(cols.shape[0]):
-        total = None
-        for piece, ref in enumerate((own, core, chip, both)):
-            at = pl.ds(pl.multiple_of((seat[7] ^ piece) * size, size), size)
-            row_part, col_part = block_terms(
-                ref[...], cols[unit], weight[unit, at, :], target[unit, at, :], block
-            )
+        row_parts, total = block_terms(
+            [ref[...] for ref in (own, core, chip, both)],
+            cols[unit],
+            [(weight[unit, at, :], target[unit, at, :]) for at in downs],
+            block,
+        )
+        for piece, row_part in enumerate(row_parts):
             for before in [sums[piece]] if unit else grads[piece::4]:
                 row_part = row_part + before[...]
             sums[piece][...] = row_part
-            total = col_part if total is None else total + col_part
         col_grad[unit] = total.astype(col_grad.dtype)
 
 
@@ -247,43 +258,45 @@
     )
 
 
-def sum_kernel(slots, seat, mine, theirs, home, near, far, cross):
-    for unit in range(mine.shape[0]):
-        for away, out in enumerate((home, near, far, cross)):
-            total = jnp.zeros(out.shape[1:], jnp.float32)
+def sum_kernel(slots, seat, mine, theirs, home, near, *rest):
+    units = mine.shape[0]
+    for unit in range(units):
+        if len(rest) > 2:
+            outs = home.at[unit], near.at[unit], rest[unit].at[0], rest[units + unit].at[0]
+        else:
+            outs = home.at[unit], near.at[unit], rest[0].at[unit], rest[1].at[unit]
+        for away, out in enumerate(outs):
+            total = jnp.zeros(out.shape, jnp.float32)
             for slot in range(slots):
                 at = pl.ds(slot * LANES, LANES)
                 total = total + jnp.where(seat[3 + slot] == away, mine[unit, at, :], 0.0)
                 total = total + jnp.where(
                     seat[5 + slot] == away, theirs[unit, at, :].astype(jnp.float32), 0.0
                 )
-            out[unit] = total.astype(out.dtype)
-
-
-def block_sums(seat, mine, theirs, slots, tokens):
+            out[...] = total.astype(out.dtype)
+
+
+def block_sums(seat, mine, theirs, slots, split, tokens):
     units, _, width = mine.shape
     shape = (units, LANES, width)
+    count, part = (units, (1, LANES, width)) if split else (1, shape)
     return in_order(
         functools.partial(sum_kernel, slots),
         tokens,
-        [
-            pltpu.HBM(shape, jnp.float32),
-            pltpu.HBM(shape, jnp.bfloat16),
-            jax.ShapeDtypeStruct(shape, jnp.float32),
-            jax.ShapeDtypeStruct(shape, jnp.bfloat16),
-        ],
+        [pltpu.HBM(shape, jnp.float32), pltpu.HBM(shape, jnp.bfloat16)]
+        + [pltpu.HBM(part, jnp.float32)] * count
+        + [jax.ShapeDtypeStruct(part, jnp.bfloat16)] * count,
         [smalls, whole, whole],
     )(seat, mine, theirs)
 
 
-def relay_kernel(near, far, cross, near_out, far_out):
-    near_out[...] = near[...]
-    far_out[...] = (far[...] + cross[...].astype(jnp.float32)).astype(far_out.dtype)
-
-
-def relayed(near, far, cross, tokens):
+def relay_kernel(far, cross, out):
+    out[...] = (far[...] + cross[...].astype(jnp.float32)).astype(out.dtype)
+
+
+def relayed(far, cross, tokens):
     shape = jax.ShapeDtypeStruct(far.shape, jnp.bfloat16)
-    return in_order(relay_kernel, tokens, [shape] * 2, [whole] * 3, vmem=4)(near, far, cross)
+    return in_order(relay_kernel, tokens, [shape], [whole] * 2, vmem=4)(*in_hbm(far), cross)
 
 
 def add_kernel(left, right, out):
@@ -295,25 +308,30 @@
     return in_order(add_kernel, tokens, [shape], [whole] * 2, vmem=4)(left, right)
 
 
-def update_kernel(embed, accum, home, near, far, *rest):
+def update_kernel(count, embed, accum, home, near, *rest):
     embed_new, accum_new = rest[-2:]
-    grad = home[...] + near[...].astype(jnp.float32) + far[...].astype(jnp.float32)
+    far = rest[0][...]
+    for unit in range(1, count):
+        far = jnp.where(pl.program_id(0) == unit, rest[unit][...], far)
+    grad = home[...] + near[...].astype(jnp.float32) + far.astype(jnp.float32)
     total = accum[...] + grad * grad
     accum_new[...] = total
     embed_new[...] = embed[...] - learn_rate * grad / jnp.sqrt(total)
 
 
 def updated(embed, accum, start, sums, before, tokens):
-    units, _, width = sums[0].shape
+    home, near, *fars = sums
+    units, _, width = home.shape
     shape = jax.ShapeDtypeStruct(embed.shape, jnp.float32)
     outer = pl.BlockSpec((1, LANES, width), lambda unit: (0, start + unit, 0))
     inner = pl.BlockSpec((1, LANES, width), lambda unit: (unit, 0, 0))
-    count = len(tokens) + 5
+    last = inner if len(fars) == 1 else pl.BlockSpec((1, LANES, width), lambda unit: (0, 0, 0))
+    count = len(tokens) + 4 + len(fars)
     return in_order(
-        update_kernel,
+        functools.partial(update_kernel, len(fars)),
         tokens,
         [shape, shape],
-        [outer, outer, inner, inner, inner] + [anywhere] * len(before),
+        [outer, outer, inner, inner] + [last] * len(fars) + [anywhere] * len(before),
         [outer, outer],
         grid=(units,),
         vmem=8,
@@ -360,10 +378,10 @@
     starts = [sum(CUTS[:part]) for part in range(len(CUTS))]
 
     def far_cols(part, own):
-        return own, swap(f"cols_far_{part}", own, "row", far_swap)
-
-    def near_cols(part, own, far):
-        near = swap(f"cols_near_{part}", own, "row", near_swap)
+        far = swap(f"cols_far_{part}", own, "row", far_swap)
+        return own, swap(f"cols_near_{part}", own, "row", near_swap), far
+
+    def near_cols(part, own, near, far):
         return own, near, far, swap(f"cols_cross_{part}", far, "row", near_swap)
 
     cols = near_cols(0, *far_cols(0, col_embed[0, : CUTS[0] * LANES].astype(jnp.bfloat16)))
@@ -397,31 +415,36 @@
 
     def pick_part(part, cols, coming, *tokens):
         if coming is not None:
-            tokens += coming[1:]
+            tokens += coming[2:]
         asked, kept, done = picked(seat, cols, slots, tokens)
         received = swap(f"cols_mate_{part}", asked, "row", mate_swap)
         after_next = None
         if coming is not None:
-            cols = near_cols(part + 1, *gated(coming, (done,)))
+            cols = near_cols(part + 1, *coming[:2], *gated(coming[2:], (done,)))
             own_next, done = own_cols(part + 2, done)
             if own_next is not None:
                 after_next = far_cols(part + 2, own_next)
         return kept, received, cols, after_next, done
 
     def sum_part(part, mine, from_mate, *tokens):
-        home_sum, near, far, cross, done = block_sums(seat, mine, from_mate, slots, tokens)
-        cross = swap(f"grads_cross_{part}", cross, "row", near_swap)
-        return (home_sum, near, far, cross), done
+        split = part + 1 == parts
+        home_sum, near, *rest, done = block_sums(seat, mine, from_mate, slots, split, tokens)
+        count = len(rest) // 2
+        cross = [
+            swap(f"grads_cross_{part}_{i}", rest[count + i], "row", near_swap)
+            for i in range(count)
+        ]
+        return (home_sum, near, rest[:count], cross), done
 
     def send_part(part, sums, *tokens):
-        home_sum, near, far, cross = sums
-        near, far, done = relayed(near, far, cross, tokens)
+        home_sum, near, (far,), (cross,) = sums
+        far, done = relayed(far, cross, tokens)
         near = swap(f"grads_near_{part}", near, "row", near_swap)
         far = swap(f"grads_far_{part}", far, "row", far_swap)
         return (home_sum, near, far), done
 
-    def update_part(part, sums, *tokens):
-        *new, done = updated(col_embed, col_accum, starts[part], sums, col_new, tokens)
+    def update_part(start, sums, *tokens):
+        *new, done = updated(col_embed, col_accum, start, sums, col_new, tokens)
         return new, done
 
     *_, cross = cols
@@ -438,32 +461,36 @@
         from_mate = swap(f"grads_mate_{part}", theirs, "row", mate_swap)
         if part:
             if sent:
-                col_new, done = update_part(part - 2, sent, done)
+                col_new, done = update_part(starts[part - 2], sent, done)
             sums, done = sum_part(part - 1, *waiting, done)
             if part + 1 == parts:
                 home_grad, core_grad, chip_grad, both_grad = other_rows
                 both_core = swap("row_grads_both", both_grad, "col", core_swap)
                 from_core = swap("row_grads_core", core_grad, "col", core_swap)
-                chip_sum, done = added(chip_grad, both_core, (done,))
-                from_chip = swap("row_grads_chip", chip_sum, "col", chip_swap)
-                own_grad = home_grad + from_core + from_chip.astype(jnp.float32)
-                row_new = row_updates(
-                    row_embed, row_accum, row_freq, excluded, block, own_grad
-                )
-            sent, done = send_part(part - 1, sums, done)
+            extra = (both_core, from_core) if part + 1 == parts else ()
+            sent, done = send_part(part - 1, sums, done, *extra)
         row_grads.append(other_rows)
         waiting = mine, from_mate
         received = received_next
 
     sums, done = sum_part(parts - 1, *waiting, done)
-
-
-    *sums, cross = sums
+    chip_sum, row_done = added(chip_grad, both_core, (done,))
+    from_chip = swap("row_grads_chip", chip_sum, "col", chip_swap)
+    own_grad = home_grad + from_core + from_chip.astype(jnp.float32)
+    row_new = row_updates(row_embed, row_accum, row_freq, excluded, block, own_grad)
+
+
+    home_sum, near, fars, crosses = sums
     passed = gated(sent[:1], (*sent[1:], done)) if sent else ()
-    last, done = send_part(parts - 1, (*sums, cross), done, *passed, row_new[1])
+    far_sums = []
+    for unit, (far, cross) in enumerate(zip(fars, crosses)):
+        far, done = relayed(far, cross, (done, *passed))
+        far_sums.append(swap(f"grads_far_{parts - 1}_{unit}", far, "row", far_swap))
+    near = swap(f"grads_near_{parts - 1}", near, "row", near_swap)
     if sent:
-        col_new, done = update_part(parts - 2, (*passed, *sent[1:]), done)
-    col_new, done = update_part(parts - 1, last, done)
+        col_new, done = update_part(starts[parts - 2], (*passed, *sent[1:]), done)
+    sums = home_sum, near, *far_sums
+    col_new, done = update_part(starts[parts - 1], sums, done, row_new[1])
     return (*row_new, *col_new)
 
 

time: 117 us -> 115 us (0.983)
  starting transfers between devices: 31.9 us -> 34 us
  local copies, waits for them, and re-layouts: 3.44 us -> 1.47 us
  waiting for transfers between devices: 34.8 us -> 33.2 us
    ppermute x23 -> x25, starting transfers between devices: 31.9 us -> 34 us  [swap(): return lax.ppermute(value, axis, pairs)]
    unnamed x34 -> x38, local copies, waits for them, and re-layouts: 2.05 us -> 0.08 us
    ppermute x23 -> x25, waiting for transfers between devices: 34.8 us -> 33.2 us  [swap(): return lax.ppermute(value, axis, pairs)]
    pallas_call x15 -> x16, Pallas kernels: 42 us -> 42.1 us  [in_order(): call(*([scalars] if ahead else []), *held(tokens), *args)]
  transfers between devices with their start and end apart: 23 -> 25, of which waited for: 10 -> 10; matrix products, arithmetic and copies ran while one was open for 2% -> 2% of each run, Pallas kernels for 30% -> 31%
where the time goes in v4:
time: 115 us
  Pallas kernels  42.1 us (37%)
  starting transfers between devices  34 us (30%)
  waiting for transfers between devices  33.2 us (29%)
  other arithmetic  2.29 us (2%)
  between operations  1.58 us (1%)
  local copies, waits for them, and re-layouts  1.47 us (1%)
    pallas_call x16, Pallas kernels, in_order(): call(*([scalars] if ahead else []), *held(tokens), *args)  42.1 us
    ppermute x25, starting transfers between devices, swap(): return lax.ppermute(value, axis, pairs)  34 us
    ppermute x25, waiting for transfers between devices, swap(): return lax.ppermute(value, axis, pairs)  33.2 us
  transfers between devices with their start and end apart: 25, of which 10 were waited for; matrix products, arithmetic and copies ran while one was open for 2% of the time, Pallas kernels for 31%

profile of v4, /device:TPU:0, one launch (start us, length us, event | category | flops | bytes accessed | tf_op | source)
XLA Modules:
  0.0 114.5 jit_solution(5467089227263978550)
XLA Ops:
  1.7 4.1 %collective-permute-start.5 = (bf16[256,512]{1,0:T(8,128)(2,1)S(1)}, bf16[256,512]{1,0:T(8,128)(2,1)S(1)}, u32[]{:S(2)}, u32[]{:S(2)}) collective-permute-start(bf16[256,512]{1,0:T(8,128)(2,1)S(1)} %fusion.refs_0_.refs_5_), channel_id=1, source_target_pairs={{0,16},{4,20},{8,24},{12,28},{16,0},{20,4},{24,8},{28,12},{1,17},{... | collective-permute-start | bytes 786440 | tf_op jit(solution)/shard_map/cols_far_0/ppermute | solution.py:370
  5.8 1.6 %collective-permute-start.4 = (bf16[256,512]{1,0:T(8,128)(2,1)S(1)}, bf16[256,512]{1,0:T(8,128)(2,1)S(1)}, u32[]{:S(2)}, u32[]{:S(2)}) collective-permute-start(bf16[256,512]{1,0:T(8,128)(2,1)S(1)} %fusion.refs_0_.refs_5_), channel_id=1, source_target_pairs={{0,8},{4,12},{8,0},{12,4},{16,24},{20,28},{24,16},{28,20},{1,9},{5... | collective-permute-start | bytes 786440 | tf_op jit(solution)/shard_map/cols_near_0/ppermute | solution.py:370
  7.4 1.6 %shard_map.129 = (bf16[256,512]{1,0:T(8,128)(2,1)S(1)}, f32[8,128]{1,0:T(8,128)}) custom-call(bf16[256,512]{1,0:T(8,128)(2,1)S(1)} %fusion.refs_0_.refs_5_, f32[256,512]{1,0:T(8,128)} %refs_1_.3), custom_call_target="tpu_custom_call" | custom-call | flops 1 | bytes 1 | tf_op jit(solution)/shard_map/pallas_call | solution.py:57
  9.0 1.5 %collective-permute-start.2 = (bf16[256,512]{1,0:T(8,128)(2,1)S(1)}, bf16[256,512]{1,0:T(8,128)(2,1)S(1)}, u32[]{:S(2)}, u32[]{:S(2)}) collective-permute-start(bf16[256,512]{1,0:T(8,128)(2,1)S(1)} %get-tuple-element.68.refs_4_.refs_2_), channel_id=1, source_target_pairs={{0,2},{1,3},{2,0},{3,1},{4,6},{5,7},{6,4},{7,5},{8,10},{9,11},{10,... | collective-permute-start | bytes 786440 | tf_op jit(solution)/shard_map/chip_rows/ppermute | solution.py:370
  10.5 1.5 %collective-permute-start = (s32[2]{0:T(128)}, s32[2]{0:T(128)S(1)}, u32[]{:S(2)}, u32[]{:S(2)}) collective-permute-start(s32[2]{0:T(128)} %bitcast.8), channel_id=1, source_target_pairs={{0,4},{4,0},{8,12},{12,8},{16,20},{20,16},{24,28},{28,24},{1,5},{5... | collective-permute-start | bytes 32 | tf_op jit(solution)/shard_map/mate_chosen/ppermute | solution.py:370
  12.1 1.6 %shard_map.130 = (bf16[256,512]{1,0:T(8,128)(2,1)S(1)}, f32[8,128]{1,0:T(8,128)}) custom-call(f32[8,128]{1,0:T(8,128)} %get-tuple-element.66.refs_0_, f32[1,512,512]{2,1,0:T(8,128)} %refs_2_.3), custom_call_target="tpu_custom_call" | custom-call | flops 1 | bytes 1 | tf_op jit(solution)/shard_map/pallas_call | solution.py:57
  13.7 4.2 %collective-permute-done.5.refs_2_.refs_7_ = bf16[256,512]{1,0:T(8,128)(2,1)S(1)} collective-permute-done((bf16[256,512]{1,0:T(8,128)(2,1)S(1)}, bf16[256,512]{1,0:T(8,128)(2,1)S(1)}, u32[]{:S(2)}, u32[]{:S(2)}) %collective-permute-start.5) | collective-permute-done | bytes 262176 | tf_op jit(solution)/shard_map/cols_far_0/ppermute | solution.py:370
  19.4 2.5 %collective-permute-start.7 = (bf16[256,512]{1,0:T(8,128)(2,1)S(1)}, bf16[256,512]{1,0:T(8,128)(2,1)S(1)}, u32[]{:S(2)}, u32[]{:S(2)}) collective-permute-start(bf16[256,512]{1,0:T(8,128)(2,1)S(1)} %collective-permute-done.5.refs_2_.refs_7_), channel_id=1, source_target_pairs={{0,8},{4,12},{8,0},{12,4},{16,24},{20,28},{24,16},{28,20},{1,9},{5... | collective-permute-start | bytes 786440 | tf_op jit(solution)/shard_map/cols_cross_0/ppermute | solution.py:370
  22.1 10.0 %collective-permute-done.7.refs_0_ = bf16[256,512]{1,0:T(8,128)(2,1)S(1)} collective-permute-done((bf16[256,512]{1,0:T(8,128)(2,1)S(1)}, bf16[256,512]{1,0:T(8,128)(2,1)S(1)}, u32[]{:S(2)}, u32[]{:S(2)}) %collective-permute-start.7) | collective-permute-done | bytes 262176 | tf_op jit(solution)/shard_map/cols_cross_0/ppermute | solution.py:370
  32.1 1.9 %shard_map.133 = (bf16[2,256,512]{2,1,0:T(8,128)(2,1)}, bf16[2,256,512]{2,1,0:T(8,128)(2,1)S(1)}, f32[8,128]{1,0:T(8,128)}) custom-call(f32[8,128]{1,0:T(8,128)} %get-tuple-element.67.refs_3_.refs_1_.refs_0_, bf16[256,512]{1,0:T(8,128)(2,1)S(1)} %collective-permute-done.1.refs_1_.refs_5_.refs_3_, ...), custom_call_target="tpu_custom_call" | custom-call | flops 1 | bytes 1 | tf_op jit(solution)/shard_map/pallas_call | solution.py:57
  35.8 1.6 %collective-permute-start.10 = (bf16[256,512]{1,0:T(8,128)(2,1)S(1)}, bf16[256,512]{1,0:T(8,128)(2,1)}, u32[]{:S(2)}, u32[]{:S(2)}) collective-permute-start(bf16[256,512]{1,0:T(8,128)(2,1)S(1)} %shard_map.135.refs_5_), channel_id=1, source_target_pairs={{0,8},{4,12},{8,0},{12,4},{16,24},{20,28},{24,16},{28,20},{1,9},{5... | collective-permute-start | bytes 786440 | tf_op jit(solution)/shard_map/cols_cross_1/ppermute | solution.py:370
  38.3 6.7 %shard_map.134 = (f32[256,512]{1,0:T(8,128)S(1)}, f32[256,512]{1,0:T(8,128)S(1)}, f32[256,512]{1,0:T(8,128)S(1)}, f32[256,512]{1,0:T(8,128)S(1)}, f32[2,256,512]...) custom-call(s32[8]{0:T(128)S(1)} %concatenate.3.refs_4_.refs_0_.refs_2_.refs_1_, ...), custom_call_target="tpu_custom_call" | custom-call | flops 1 | bytes 1 | tf_op jit(solution)/shard_map/pallas_call | solution.py:57
  45.0 1.9 %collective-permute-done.10.refs_6_ = bf16[256,512]{1,0:T(8,128)(2,1)} collective-permute-done((bf16[256,512]{1,0:T(8,128)(2,1)S(1)}, bf16[256,512]{1,0:T(8,128)(2,1)}, u32[]{:S(2)}, u32[]{:S(2)}) %collective-permute-start.10) | collective-permute-done | bytes 262176 | tf_op jit(solution)/shard_map/cols_cross_1/ppermute | solution.py:370
  46.9 2.0 %shard_map.136 = (bf16[2,256,512]{2,1,0:T(8,128)(2,1)S(1)}, bf16[2,256,512]{2,1,0:T(8,128)(2,1)S(1)}, f32[8,128]{1,0:T(8,128)}) custom-call(f32[8,128]{1,0:T(8,128)} %get-tuple-element.72.refs_0_, bf16[2,256,512]{2,1,0:T(8,128)(2,1)S(1)} %collective-permute-done.8.refs_1_.refs_6_, s32[8]{0:T(128)S(1)} %concatenate.3.refs_4_.refs_0_.refs_2_.refs_1_, ...), custom_call_target="tpu_custom_call" | custom-call | flops 1 | bytes 1 | tf_op jit(solution)/shard_map/pallas_call | solution.py:57
  49.9 3.5 %shard_map.137 = (f32[256,512]{1,0:T(8,128)S(1)}, f32[256,512]{1,0:T(8,128)S(1)}, f32[256,512]{1,0:T(8,128)S(1)}, f32[256,512]{1,0:T(8,128)S(1)}, bf16[2,256,512]{2,1,0:T(8,128)(2,1)}, /*index=5*/f32[8,128]{1,0:T(8,128)}) custom-call(f32[8,128]{1,0:T(8,128)} %get-tuple-element.74.refs_0_, s32[8]{0:T(128)S(1)} %concatenate.3.refs_4_.refs_0_.refs_2_.refs_1_, ...), custom_call_target="tpu_custom_call" | custom-call | flops 1 | bytes 1 | tf_op jit(solution)/shard_map/pallas_call | solution.py:57
  54.4 6.6 %shard_map.138 = (f32[256,512]{1,0:T(8,128)S(1)}, f32[256,512]{1,0:T(8,128)S(1)}, f32[256,512]{1,0:T(8,128)S(1)}, f32[256,512]{1,0:T(8,128)S(1)}, f32[2,256,512]...) custom-call(s32[8]{0:T(128)S(1)} %concatenate.3.refs_4_.refs_0_.refs_2_.refs_1_, ...), custom_call_target="tpu_custom_call" | custom-call | flops 1 | bytes 1 | tf_op jit(solution)/shard_map/pallas_call | solution.py:57
  61.0 2.7 %collective-permute-done.11.refs_6_ = bf16[2,256,512]{2,1,0:T(8,128)(2,1)S(1)} collective-permute-done((bf16[2,256,512]{2,1,0:T(8,128)(2,1)S(1)}, bf16[2,256,512]{2,1,0:T(8,128)(2,1)S(1)}, u32[]{:S(2)}, u32[]{:S(2)}) %collective-permute-start.11) | collective-permute-done | bytes 524320 | tf_op jit(solution)/shard_map/cols_mate_1/ppermute | solution.py:370
  63.7 3.9 %shard_map.139 = (f32[256,512]{1,0:T(8,128)S(1)}, f32[256,512]{1,0:T(8,128)}, f32[256,512]{1,0:T(8,128)S(1)}, f32[256,512]{1,0:T(8,128)}, bf16[2,256,512]{2,1,0:T(8,128)(2,1)}, /*index=5*/f32[8,128]{1,0:T(8,128)}) custom-call(f32[8,128]{1,0:T(8,128)} %get-tuple-element.83.refs_0_, s32[8]{0:T(128)S(1)} %concatenate.3.refs_4_.refs_0_.refs_2_.refs_1_, ...), custom_call_target="tpu_custom_call" | custom-call | flops 1 | bytes 1 | tf_op jit(solution)/shard_map/pallas_call | solution.py:57
  70.7 1.9 %shard_map.140 = (f32[2,128,512]{2,1,0:T(8,128)}, bf16[2,128,512]{2,1,0:T(8,128)(2,1)}, f32[2,128,512]{2,1,0:T(8,128)}, bf16[2,128,512]{2,1,0:T(8,128)(2,1)S(1)}, f32[8,128]{1,0:T(8,128)}) custom-call(f32[8,128]{1,0:T(8,128)} %get-tuple-element.97.refs_0_, s32[8]{0:T(128)S(1)} %concatenate.3.refs_4_.refs_0_.refs_2_.refs_1_, f32[2,256,512]{2,1,0:T(8,128)S(1)} %copy-done.4, ...), custom_call_target="tpu_custom_call" | custom-call | flops 1 | bytes 1 | tf_op jit(solution)/shard_map/pallas_call | solution.py:57
  72.7 3.2 %collective-permute-start.15 = (bf16[2,128,512]{2,1,0:T(8,128)(2,1)S(1)}, bf16[2,128,512]{2,1,0:T(8,128)(2,1)S(1)}, u32[]{:S(2)}, u32[]{:S(2)}) collective-permute-start(bf16[2,128,512]{2,1,0:T(8,128)(2,1)S(1)} %get-tuple-element.103), channel_id=1, source_target_pairs={{0,8},{4,12},{8,0},{12,4},{16,24},{20,28},{24,16},{28,20},{1,9},{5... | collective-permute-start | bytes 786440 | tf_op jit(solution)/shard_map/grads_cross_0_0/ppermute | solution.py:370
  76.0 6.1 %collective-permute-done.15.refs_4_ = bf16[2,128,512]{2,1,0:T(8,128)(2,1)S(1)} collective-permute-done((bf16[2,128,512]{2,1,0:T(8,128)(2,1)S(1)}, bf16[2,128,512]{2,1,0:T(8,128)(2,1)S(1)}, u32[]{:S(2)}, u32[]{:S(2)}) %collective-permute-start.15) | collective-permute-done | bytes 262176 | tf_op jit(solution)/shard_map/grads_cross_0_0/ppermute | solution.py:370
  82.1 1.7 %shard_map.141 = (bf16[2,128,512]{2,1,0:T(8,128)(2,1)S(1)}, f32[8,128]{1,0:T(8,128)}) custom-call(f32[8,128]{1,0:T(8,128)} %get-tuple-element.100.refs_0_, f32[256,512]{1,0:T(8,128)S(1)} %collective-permute-done.14.refs_1_.refs_2_, f32[256,512]{1,0:T(8,128)S(1)} %collective-permute-done.12.refs_2_, f32[2,128,512]{2,1,0:T(8,128)} %get-tuple-element.102.refs_3_, ...), custom_call_target="tpu_custom_call" | custom-call | flops 1 | bytes 1 | tf_op jit(solution)/shard_map/pallas_call | solution.py:57
  83.8 3.8 %collective-permute-start.19 = (bf16[2,128,512]{2,1,0:T(8,128)(2,1)S(1)}, bf16[2,128,512]{2,1,0:T(8,128)(2,1)S(1)}, u32[]{:S(2)}, u32[]{:S(2)}) collective-permute-start(bf16[2,128,512]{2,1,0:T(8,128)(2,1)S(1)} %get-tuple-element.112), channel_id=1, source_target_pairs={{0,16},{4,20},{8,24},{12,28},{16,0},{20,4},{24,8},{28,12},{1,17},{... | collective-permute-start | bytes 786440 | tf_op jit(solution)/shard_map/grads_far_0/ppermute | solution.py:370
  87.6 2.3 %shard_map.142 = (f32[2,128,512]{2,1,0:T(8,128)}, bf16[2,128,512]{2,1,0:T(8,128)(2,1)}, f32[1,128,512]{2,1,0:T(8,128)}, f32[1,128,512]{2,1,0:T(8,128)}, bf16[1,1...) custom-call(f32[8,128]{1,0:T(8,128)} %get-tuple-element.104.refs_0_, ...), custom_call_target="tpu_custom_call" | custom-call | flops 1 | bytes 1 | tf_op jit(solution)/shard_map/pallas_call | solution.py:57
  90.7 1.5 %collective-permute-start.17 = (bf16[256,512]{1,0:T(8,128)(2,1)S(1)}, bf16[256,512]{1,0:T(8,128)(2,1)}, u32[]{:S(2)}, u32[]{:S(2)}) collective-permute-start(bf16[256,512]{1,0:T(8,128)(2,1)S(1)} %get-tuple-element.109), channel_id=1, source_target_pairs={{0,2},{1,3},{2,0},{3,1},{4,6},{5,7},{6,4},{7,5},{8,10},{9,11},{10,... | collective-permute-start | bytes 786440 | tf_op jit(solution)/shard_map/row_grads_chip/ppermute | solution.py:370
  95.4 5.0 %collective-permute-done.20.refs_3_ = bf16[1,128,512]{2,1,0:T(8,128)(2,1)S(1)} collective-permute-done((bf16[1,128,512]{2,1,0:T(8,128)(2,1)}, bf16[1,128,512]{2,1,0:T(8,128)(2,1)S(1)}, u32[]{:S(2)}, u32[]{:S(2)}) %collective-permute-start.20) | collective-permute-done | bytes 131104 | tf_op jit(solution)/shard_map/grads_cross_1_0/ppermute | solution.py:370
  100.4 1.5 %shard_map.145 = (bf16[1,128,512]{2,1,0:T(8,128)(2,1)S(1)}, f32[8,128]{1,0:T(8,128)}) custom-call(f32[8,128]{1,0:T(8,128)} %get-tuple-element.107.refs_0_.refs_3_, f32[2,128,512]{2,1,0:T(8,128)S(1)} %shard_map.144.refs_1_.refs_3_, f32[1,128,512]{2,1,0:T(8,128)} %get-tuple-element.113.refs_2_, bf16[1,128,512]{2,1,0:T(8,128)(2,1)S(1)} %collective-permute-done.20.refs_3_), custom_call_target="tpu_custom_call" | custom-call | flops 1 | bytes 1 | tf_op jit(solution)/shard_map/pallas_call | solution.py:57
  102.0 1.5 %shard_map.146 = (bf16[1,128,512]{2,1,0:T(8,128)(2,1)S(1)}, f32[8,128]{1,0:T(8,128)}) custom-call(f32[8,128]{1,0:T(8,128)} %get-tuple-element.115.refs_0_, f32[2,128,512]{2,1,0:T(8,128)S(1)} %shard_map.144.refs_1_.refs_3_, f32[1,128,512]{2,1,0:T(8,128)} %get-tuple-element.116.refs_2_, bf16[1,128,512]{2,1,0:T(8,128)(2,1)S(1)} %collective-permute-done.21.refs_3_), custom_call_target="tpu_custom_call" | custom-call | flops 1 | bytes 1 | tf_op jit(solution)/shard_map/pallas_call | solution.py:57
  103.5 2.9 %collective-permute-start.24 = (bf16[1,128,512]{2,1,0:T(8,128)(2,1)S(1)}, bf16[1,128,512]{2,1,0:T(8,128)(2,1)S(1)}, u32[]{:S(2)}, u32[]{:S(2)}) collective-permute-start(bf16[1,128,512]{2,1,0:T(8,128)(2,1)S(1)} %get-tuple-element.123), channel_id=1, source_target_pairs={{0,16},{4,20},{8,24},{12,28},{16,0},{20,4},{24,8},{28,12},{1,17},{... | collective-permute-start | bytes 393224 | tf_op jit(solution)/shard_map/grads_far_1_1/ppermute | solution.py:370
  106.5 2.0 %multiply_subtract_fusion = (f32[256,512]{1,0:T(8,128)}, f32[256,512]{1,0:T(8,128)S(1)}) fusion(f32[256,512]{1,0:T(8,128)S(1)} %copy-done.14, f32[256]{0:T(256)S(1)} %fusion.1, bf16[256,512]{1,0:T(8,128)(2,1)} %collective-permute-done.17, f32[256,512]{1,0:T(8,128)S(1)} %copy-done.7, f32[256,512]{1,0:T(8,128)S(1)} %collective-permute-done.12.refs_2_, ...), kind=kLoop, calls=%fused_computation.1 | loop fusion | flops 1310720 | bytes 3408896 | tf_op jit(solution)/shard_map/sub | solution.py:510
  108.5 2.3 %shard_map.147 = (f32[1,512,512]{2,1,0:T(8,128)}, f32[1,512,512]{2,1,0:T(8,128)}, f32[8,128]{1,0:T(8,128)}) custom-call(f32[8,128]{1,0:T(8,128)} %get-tuple-element.118.refs_0_, f32[1,512,512]{2,1,0:T(8,128)} %refs_2_.3, f32[1,512,512]{2,1,0:T(8,128)} %refs_3_.5, f32[2,128,512]{2,1,0:T(8,128)S(1)} %shard_map.144.refs_1_.refs_3_, ...), custom_call_target="tpu_custom_call" | custom-call | flops 1 | bytes 1 | tf_op jit(solution)/shard_map/pallas_call | solution.py:57
  112.3 2.1 %shard_map.148 = (f32[1,512,512]{2,1,0:T(8,128)}, f32[1,512,512]{2,1,0:T(8,128)}, f32[8,128]{1,0:T(8,128)}) custom-call(f32[8,128]{1,0:T(8,128)} %get-tuple-element.119.refs_0_, f32[256,512]{1,0:T(8,128)S(1)} %get-tuple-element.129.refs_1_, f32[1,512,512]{2,1,0:T(8,128)} %refs_2_.3, ...), custom_call_target="tpu_custom_call", output_to_operand_aliasing={{0}: (8, {}), {1}: (9, {})} | custom-call | flops 1 | bytes 1 | tf_op jit(solution)/shard_map/pallas_call | solution.py:57
  (86 shorter events, 15.4 us)
Async XLA Ops:
  0.6 21.3 %copy-start.18 = (s32[1,1,2]{2,1,0:T(1,128)S(1)}, s32[1,1,2]{2,1,0:T(1,128)}, u32[]{:S(2)}) copy-start(s32[1,1,2]{2,1,0:T(1,128)} %param.16) | copy-start | bytes 28
  1.7 30.4 %copy-start.1 = (bf16[256,512]{1,0:T(8,128)(2,1)}, bf16[256,512]{1,0:T(8,128)(2,1)S(1)}, u32[]{:S(2)}) copy-start(bf16[256,512]{1,0:T(8,128)(2,1)S(1)} %fusion.refs_0_.refs_5_) | copy-start | bytes 786436
  1.7 16.1 %collective-permute-start.5 = (bf16[256,512]{1,0:T(8,128)(2,1)S(1)}, bf16[256,512]{1,0:T(8,128)(2,1)S(1)}, u32[]{:S(2)}, u32[]{:S(2)}) collective-permute-start(bf16[256,512]{1,0:T(8,128)(2,1)S(1)} %fusion.refs_0_.refs_5_), channel_id=1, source_target_pairs={{0,16},{4,20},{8,24},{12,28},{16,0},{20,4},{24,8},{28,12},{1,17},{... | collective-permute-start | bytes 786440 | tf_op jit(solution)/shard_map/cols_far_0/ppermute | solution.py:370
  5.8 12.2 %collective-permute-start.4 = (bf16[256,512]{1,0:T(8,128)(2,1)S(1)}, bf16[256,512]{1,0:T(8,128)(2,1)S(1)}, u32[]{:S(2)}, u32[]{:S(2)}) collective-permute-start(bf16[256,512]{1,0:T(8,128)(2,1)S(1)} %fusion.refs_0_.refs_5_), channel_id=1, source_target_pairs={{0,8},{4,12},{8,0},{12,4},{16,24},{20,28},{24,16},{28,20},{1,9},{5... | collective-permute-start | bytes 786440 | tf_op jit(solution)/shard_map/cols_near_0/ppermute | solution.py:370
  9.0 12.9 %collective-permute-start.2 = (bf16[256,512]{1,0:T(8,128)(2,1)S(1)}, bf16[256,512]{1,0:T(8,128)(2,1)S(1)}, u32[]{:S(2)}, u32[]{:S(2)}) collective-permute-start(bf16[256,512]{1,0:T(8,128)(2,1)S(1)} %get-tuple-element.68.refs_4_.refs_2_), channel_id=1, source_target_pairs={{0,2},{1,3},{2,0},{3,1},{4,6},{5,7},{6,4},{7,5},{8,10},{9,11},{10,... | collective-permute-start | bytes 786440 | tf_op jit(solution)/shard_map/chip_rows/ppermute | solution.py:370
  10.5 21.5 %collective-permute-start.1 = (bf16[256,512]{1,0:T(8,128)(2,1)S(1)}, bf16[256,512]{1,0:T(8,128)(2,1)S(1)}, u32[]{:S(2)}, u32[]{:S(2)}) collective-permute-start(bf16[256,512]{1,0:T(8,128)(2,1)S(1)} %get-tuple-element.68.refs_4_.refs_2_), channel_id=1, source_target_pairs={{0,1},{1,0},{2,3},{3,2},{4,5},{5,4},{6,7},{7,6},{8,9},{9,8},{10,11... | collective-permute-start | bytes 786440 | tf_op jit(solution)/shard_map/core_rows/ppermute | solution.py:370
  10.5 11.4 %collective-permute-start = (s32[2]{0:T(128)}, s32[2]{0:T(128)S(1)}, u32[]{:S(2)}, u32[]{:S(2)}) collective-permute-start(s32[2]{0:T(128)} %bitcast.8), channel_id=1, source_target_pairs={{0,4},{4,0},{8,12},{12,8},{16,20},{20,16},{24,28},{28,24},{1,5},{5... | collective-permute-start | bytes 32 | tf_op jit(solution)/shard_map/mate_chosen/ppermute | solution.py:370
  13.7 24.3 %copy-start.16 = (s32[1024]{0:T(1024)S(1)}, s32[1024]{0:T(1024)}, u32[]{:S(2)}) copy-start(s32[1024]{0:T(1024)} %param.15) | copy-start | bytes 12292
  18.1 20.2 %copy-start.11 = (s32[1,4096]{1,0:T(1,128)S(1)}, s32[1,4096]{1,0:T(1,128)}, u32[]{:S(2)}) copy-start(s32[1,4096]{1,0:T(1,128)} %refs_3_.4) | copy-start | bytes 49156
  18.1 26.9 %copy-start.5 = (bf16[256,512]{1,0:T(8,128)(2,1)}, bf16[256,512]{1,0:T(8,128)(2,1)S(1)}, u32[]{:S(2)}) copy-start(bf16[256,512]{1,0:T(8,128)(2,1)S(1)} %shard_map.131.refs_3_) | copy-start | bytes 786436
  18.1 14.0 %collective-permute-start.6 = (bf16[256,512]{1,0:T(8,128)(2,1)S(1)}, bf16[256,512]{1,0:T(8,128)(2,1)S(1)}, u32[]{:S(2)}, u32[]{:S(2)}) collective-permute-start(bf16[256,512]{1,0:T(8,128)(2,1)S(1)} %shard_map.131.refs_3_), channel_id=1, source_target_pairs={{0,16},{4,20},{8,24},{12,28},{16,0},{20,4},{24,8},{28,12},{1,17},{... | collective-permute-start | bytes 786440 | tf_op jit(solution)/shard_map/cols_far_1/ppermute | solution.py:370
  19.4 12.6 %collective-permute-start.7 = (bf16[256,512]{1,0:T(8,128)(2,1)S(1)}, bf16[256,512]{1,0:T(8,128)(2,1)S(1)}, u32[]{:S(2)}, u32[]{:S(2)}) collective-permute-start(bf16[256,512]{1,0:T(8,128)(2,1)S(1)} %collective-permute-done.5.refs_2_.refs_7_), channel_id=1, source_target_pairs={{0,8},{4,12},{8,0},{12,4},{16,24},{20,28},{24,16},{28,20},{1,9},{5... | collective-permute-start | bytes 786440 | tf_op jit(solution)/shard_map/cols_cross_0/ppermute | solution.py:370
  21.9 10.1 %collective-permute-start.3 = (bf16[256,512]{1,0:T(8,128)(2,1)S(1)}, bf16[256,512]{1,0:T(8,128)(2,1)S(1)}, u32[]{:S(2)}, u32[]{:S(2)}) collective-permute-start(bf16[256,512]{1,0:T(8,128)(2,1)S(1)} %collective-permute-done.2.refs_6_.refs_4_), channel_id=1, source_target_pairs={{0,1},{1,0},{2,3},{3,2},{4,5},{5,4},{6,7},{7,6},{8,9},{9,8},{10,11... | collective-permute-start | bytes 786440 | tf_op jit(solution)/shard_map/both_rows/ppermute | solution.py:370
  34.0 12.8 %collective-permute-start.8 = (bf16[2,256,512]{2,1,0:T(8,128)(2,1)}, bf16[2,256,512]{2,1,0:T(8,128)(2,1)S(1)}, u32[]{:S(2)}, u32[]{:S(2)}) collective-permute-start(bf16[2,256,512]{2,1,0:T(8,128)(2,1)} %get-tuple-element.73), channel_id=1, source_target_pairs={{0,4},{4,0},{8,12},{12,8},{16,20},{20,16},{24,28},{28,24},{1,5},{5... | collective-permute-start | bytes 1572872 | tf_op jit(solution)/shard_map/cols_mate_0/ppermute | solution.py:370
  35.3 9.6 %collective-permute-start.9 = (bf16[256,512]{1,0:T(8,128)(2,1)S(1)}, bf16[256,512]{1,0:T(8,128)(2,1)S(1)}, u32[]{:S(2)}, u32[]{:S(2)}) collective-permute-start(bf16[256,512]{1,0:T(8,128)(2,1)S(1)} %shard_map.131.refs_3_), channel_id=1, source_target_pairs={{0,8},{4,12},{8,0},{12,4},{16,24},{20,28},{24,16},{28,20},{1,9},{5... | collective-permute-start | bytes 786440 | tf_op jit(solution)/shard_map/cols_near_1/ppermute | solution.py:370
  35.8 11.1 %collective-permute-start.10 = (bf16[256,512]{1,0:T(8,128)(2,1)S(1)}, bf16[256,512]{1,0:T(8,128)(2,1)}, u32[]{:S(2)}, u32[]{:S(2)}) collective-permute-start(bf16[256,512]{1,0:T(8,128)(2,1)S(1)} %shard_map.135.refs_5_), channel_id=1, source_target_pairs={{0,8},{4,12},{8,0},{12,4},{16,24},{20,28},{24,16},{28,20},{1,9},{5... | collective-permute-start | bytes 786440 | tf_op jit(solution)/shard_map/cols_cross_1/ppermute | solution.py:370
  48.9 14.9 %collective-permute-start.11 = (bf16[2,256,512]{2,1,0:T(8,128)(2,1)S(1)}, bf16[2,256,512]{2,1,0:T(8,128)(2,1)S(1)}, u32[]{:S(2)}, u32[]{:S(2)}) collective-permute-start(bf16[2,256,512]{2,1,0:T(8,128)(2,1)S(1)} %get-tuple-element.84), channel_id=1, source_target_pairs={{0,4},{4,0},{8,12},{12,8},{16,20},{20,16},{24,28},{28,24},{1,5},{5... | collective-permute-start | bytes 1572872 | tf_op jit(solution)/shard_map/cols_mate_1/ppermute | solution.py:370
  53.4 17.3 %collective-permute-start.13 = (bf16[2,256,512]{2,1,0:T(8,128)(2,1)}, bf16[2,256,512]{2,1,0:T(8,128)(2,1)S(1)}, u32[]{:S(2)}, u32[]{:S(2)}) collective-permute-start(bf16[2,256,512]{2,1,0:T(8,128)(2,1)} %get-tuple-element.99), channel_id=1, source_target_pairs={{0,4},{4,0},{8,12},{12,8},{16,20},{20,16},{24,28},{28,24},{1,5},{5... | collective-permute-start | bytes 1572872 | tf_op jit(solution)/shard_map/grads_mate_0/ppermute | solution.py:370
  67.6 20.0 %copy-start.3 = (f32[2,256,512]{2,1,0:T(8,128)S(1)}, f32[2,256,512]{2,1,0:T(8,128)}, u32[]{:S(2)}) copy-start(f32[2,256,512]{2,1,0:T(8,128)} %get-tuple-element.105.refs_2_) | copy-start | bytes 3145732
  67.6 14.5 %collective-permute-start.12 = (f32[256,512]{1,0:T(8,128)}, f32[256,512]{1,0:T(8,128)S(1)}, u32[]{:S(2)}, u32[]{:S(2)}) collective-permute-start(f32[256,512]{1,0:T(8,128)} %get-tuple-element.96), channel_id=1, source_target_pairs={{0,1},{1,0},{2,3},{3,2},{4,5},{5,4},{6,7},{7,6},{8,9},{9,8},{10,11... | collective-permute-start | bytes 1572872 | tf_op jit(solution)/shard_map/row_grads_core/ppermute | solution.py:370
  67.7 14.4 %collective-permute-start.14 = (f32[256,512]{1,0:T(8,128)}, f32[256,512]{1,0:T(8,128)S(1)}, u32[]{:S(2)}, u32[]{:S(2)}) collective-permute-start(f32[256,512]{1,0:T(8,128)} %get-tuple-element.101), channel_id=1, source_target_pairs={{0,1},{1,0},{2,3},{3,2},{4,5},{5,4},{6,7},{7,6},{8,9},{9,8},{10,11... | collective-permute-start | bytes 1572872 | tf_op jit(solution)/shard_map/row_grads_both/ppermute | solution.py:370
  68.2 19.4 %collective-permute-start.16 = (bf16[2,256,512]{2,1,0:T(8,128)(2,1)}, bf16[2,256,512]{2,1,0:T(8,128)(2,1)}, u32[]{:S(2)}, u32[]{:S(2)}) collective-permute-start(bf16[2,256,512]{2,1,0:T(8,128)(2,1)} %get-tuple-element.106), channel_id=1, source_target_pairs={{0,4},{4,0},{8,12},{12,8},{16,20},{20,16},{24,28},{28,24},{1,5},{5... | collective-permute-start | bytes 1572872 | tf_op jit(solution)/shard_map/grads_mate_1/ppermute | solution.py:370
  72.7 9.4 %collective-permute-start.15 = (bf16[2,128,512]{2,1,0:T(8,128)(2,1)S(1)}, bf16[2,128,512]{2,1,0:T(8,128)(2,1)S(1)}, u32[]{:S(2)}, u32[]{:S(2)}) collective-permute-start(bf16[2,128,512]{2,1,0:T(8,128)(2,1)S(1)} %get-tuple-element.103), channel_id=1, source_target_pairs={{0,8},{4,12},{8,0},{12,4},{16,24},{20,28},{24,16},{28,20},{1,9},{5... | collective-permute-start | bytes 786440 | tf_op jit(solution)/shard_map/grads_cross_0_0/ppermute | solution.py:370
  75.9 18.6 %collective-permute-start.18 = (bf16[2,128,512]{2,1,0:T(8,128)(2,1)}, bf16[2,128,512]{2,1,0:T(8,128)(2,1)S(1)}, u32[]{:S(2)}, u32[]{:S(2)}) collective-permute-start(bf16[2,128,512]{2,1,0:T(8,128)(2,1)} %get-tuple-element.111), channel_id=1, source_target_pairs={{0,8},{4,12},{8,0},{12,4},{16,24},{20,28},{24,16},{28,20},{1,9},{5... | collective-permute-start | bytes 786440 | tf_op jit(solution)/shard_map/grads_near_0/ppermute | solution.py:370
  83.8 11.5 %collective-permute-start.19 = (bf16[2,128,512]{2,1,0:T(8,128)(2,1)S(1)}, bf16[2,128,512]{2,1,0:T(8,128)(2,1)S(1)}, u32[]{:S(2)}, u32[]{:S(2)}) collective-permute-start(bf16[2,128,512]{2,1,0:T(8,128)(2,1)S(1)} %get-tuple-element.112), channel_id=1, source_target_pairs={{0,16},{4,20},{8,24},{12,28},{16,0},{20,4},{24,8},{28,12},{1,17},{... | collective-permute-start | bytes 786440 | tf_op jit(solution)/shard_map/grads_far_0/ppermute | solution.py:370
  90.0 16.5 %copy-start.7 = (f32[256,512]{1,0:T(8,128)S(1)}, f32[256,512]{1,0:T(8,128)}, u32[]{:S(2)}) copy-start(f32[256,512]{1,0:T(8,128)} %copy-done.6) | copy-start | bytes 1572868
  90.7 15.8 %collective-permute-start.17 = (bf16[256,512]{1,0:T(8,128)(2,1)S(1)}, bf16[256,512]{1,0:T(8,128)(2,1)}, u32[]{:S(2)}, u32[]{:S(2)}) collective-permute-start(bf16[256,512]{1,0:T(8,128)(2,1)S(1)} %get-tuple-element.109), channel_id=1, source_target_pairs={{0,2},{1,3},{2,0},{3,1},{4,6},{5,7},{6,4},{7,5},{8,10},{9,11},{10,... | collective-permute-start | bytes 786440 | tf_op jit(solution)/shard_map/row_grads_chip/ppermute | solution.py:370
  92.4 8.0 %collective-permute-start.20 = (bf16[1,128,512]{2,1,0:T(8,128)(2,1)}, bf16[1,128,512]{2,1,0:T(8,128)(2,1)S(1)}, u32[]{:S(2)}, u32[]{:S(2)}) collective-permute-start(bf16[1,128,512]{2,1,0:T(8,128)(2,1)} %copy-done.13), channel_id=1, source_target_pairs={{0,8},{4,12},{8,0},{12,4},{16,24},{20,28},{24,16},{28,20},{1,9},{5... | collective-permute-start | bytes 393224 | tf_op jit(solution)/shard_map/grads_cross_1_0/ppermute | solution.py:370
  93.2 8.8 %collective-permute-start.21 = (bf16[1,128,512]{2,1,0:T(8,128)(2,1)}, bf16[1,128,512]{2,1,0:T(8,128)(2,1)S(1)}, u32[]{:S(2)}, u32[]{:S(2)}) collective-permute-start(bf16[1,128,512]{2,1,0:T(8,128)(2,1)} %copy-done.12), channel_id=1, source_target_pairs={{0,8},{4,12},{8,0},{12,4},{16,24},{20,28},{24,16},{28,20},{1,9},{5... | collective-permute-start | bytes 393224 | tf_op jit(solution)/shard_map/grads_cross_1_1/ppermute | solution.py:370
  94.6 16.2 %collective-permute-start.22 = (bf16[2,128,512]{2,1,0:T(8,128)(2,1)}, bf16[2,128,512]{2,1,0:T(8,128)(2,1)S(1)}, u32[]{:S(2)}, u32[]{:S(2)}) collective-permute-start(bf16[2,128,512]{2,1,0:T(8,128)(2,1)} %get-tuple-element.121), channel_id=1, source_target_pairs={{0,8},{4,12},{8,0},{12,4},{16,24},{20,28},{24,16},{28,20},{1,9},{5... | collective-permute-start | bytes 786440 | tf_op jit(solution)/shard_map/grads_near_1/ppermute | solution.py:370
  102.0 8.9 %collective-permute-start.23 = (bf16[1,128,512]{2,1,0:T(8,128)(2,1)S(1)}, bf16[1,128,512]{2,1,0:T(8,128)(2,1)S(1)}, u32[]{:S(2)}, u32[]{:S(2)}) collective-permute-start(bf16[1,128,512]{2,1,0:T(8,128)(2,1)S(1)} %get-tuple-element.122), channel_id=1, source_target_pairs={{0,16},{4,20},{8,24},{12,28},{16,0},{20,4},{24,8},{28,12},{1,17},{... | collective-permute-start | bytes 393224 | tf_op jit(solution)/shard_map/grads_far_1_0/ppermute | solution.py:370
  103.5 8.8 %collective-permute-start.24 = (bf16[1,128,512]{2,1,0:T(8,128)(2,1)S(1)}, bf16[1,128,512]{2,1,0:T(8,128)(2,1)S(1)}, u32[]{:S(2)}, u32[]{:S(2)}) collective-permute-start(bf16[1,128,512]{2,1,0:T(8,128)(2,1)S(1)} %get-tuple-element.123), channel_id=1, source_target_pairs={{0,16},{4,20},{8,24},{12,28},{16,0},{20,4},{24,8},{28,12},{1,17},{... | collective-permute-start | bytes 393224 | tf_op jit(solution)/shard_map/grads_far_1_1/ppermute | solution.py:370
  (12 other events, 98.5 us)

commit v5 on v4

--- a/solution.py
+++ b/solution.py
@@ -454,7 +454,7 @@
         own_rows, mine, terms, done = own(part, kept, done)
         if part + 1 < parts:
             kept, received_next, cols, coming, done = pick_part(
-                part + 1, cols, coming, done, received
+                part + 1, cols, coming, done
             )
         earlier = row_grads if part + 1 == parts else []
         other_rows, theirs, done = other(received, terms, own_rows, earlier, done)

time: 115 us -> 113 us (0.983)
  starting transfers between devices: 34 us -> 31.3 us
    ppermute x25, starting transfers between devices: 34 us -> 31.3 us  [swap(): return lax.ppermute(value, axis, pairs)]
  transfers between devices with their start and end apart: 25 -> 25, of which waited for: 10 -> 10; matrix products, arithmetic and copies ran while one was open for 2% -> 3% of each run, Pallas kernels for 31% -> 35%
where the time goes in v5:
time: 113 us; the launch traced here: 112 us
  Pallas kernels  41.9 us (37%)
  waiting for transfers between devices  33.6 us (30%)
  starting transfers between devices  31.3 us (28%)
  other arithmetic  2.59 us (2%)
  between operations  1.58 us (1%)
  local copies, waits for them, and re-layouts  1.46 us (1%)
    pallas_call x16, Pallas kernels, in_order(): call(*([scalars] if ahead else []), *held(tokens), *args)  41.9 us
    ppermute x25, waiting for transfers between devices, swap(): return lax.ppermute(value, axis, pairs)  33.6 us
    ppermute x25, starting transfers between devices, swap(): return lax.ppermute(value, axis, pairs)  31.3 us
    sub x1, other arithmetic, row_updates(): row_embed_new = row_embed - learn_rate * full_grad / jnp.sqrt(row_accum_new)  2.31 us
  transfers between devices with their start and end apart: 25, of which 10 were waited for; matrix products, arithmetic and copies ran while one was open for 3% of the time, Pallas kernels for 35%

profile of v5, /device:TPU:0, one launch (start us, length us, event | category | flops | bytes accessed | tf_op | source)
XLA Modules:
  0.0 112.4 jit_solution(17653993322693290336)
XLA Ops:
  1.7 4.1 %collective-permute-start.5 = (bf16[256,512]{1,0:T(8,128)(2,1)S(1)}, bf16[256,512]{1,0:T(8,128)(2,1)S(1)}, u32[]{:S(2)}, u32[]{:S(2)}) collective-permute-start(bf16[256,512]{1,0:T(8,128)(2,1)S(1)} %fusion.refs_0_.refs_5_), channel_id=1, source_target_pairs={{0,16},{4,20},{8,24},{12,28},{16,0},{20,4},{24,8},{28,12},{1,17},{... | collective-permute-start | bytes 786440 | tf_op jit(solution)/shard_map/cols_far_0/ppermute | solution.py:370
  5.8 1.6 %collective-permute-start.4 = (bf16[256,512]{1,0:T(8,128)(2,1)S(1)}, bf16[256,512]{1,0:T(8,128)(2,1)S(1)}, u32[]{:S(2)}, u32[]{:S(2)}) collective-permute-start(bf16[256,512]{1,0:T(8,128)(2,1)S(1)} %fusion.refs_0_.refs_5_), channel_id=1, source_target_pairs={{0,8},{4,12},{8,0},{12,4},{16,24},{20,28},{24,16},{28,20},{1,9},{5... | collective-permute-start | bytes 786440 | tf_op jit(solution)/shard_map/cols_near_0/ppermute | solution.py:370
  7.4 1.6 %shard_map.129 = (bf16[256,512]{1,0:T(8,128)(2,1)S(1)}, f32[8,128]{1,0:T(8,128)}) custom-call(bf16[256,512]{1,0:T(8,128)(2,1)S(1)} %fusion.refs_0_.refs_5_, f32[256,512]{1,0:T(8,128)} %refs_1_.3), custom_call_target="tpu_custom_call" | custom-call | flops 1 | bytes 1 | tf_op jit(solution)/shard_map/pallas_call | solution.py:57
  9.0 1.5 %collective-permute-start.2 = (bf16[256,512]{1,0:T(8,128)(2,1)S(1)}, bf16[256,512]{1,0:T(8,128)(2,1)S(1)}, u32[]{:S(2)}, u32[]{:S(2)}) collective-permute-start(bf16[256,512]{1,0:T(8,128)(2,1)S(1)} %get-tuple-element.68.refs_4_.refs_2_), channel_id=1, source_target_pairs={{0,2},{1,3},{2,0},{3,1},{4,6},{5,7},{6,4},{7,5},{8,10},{9,11},{10,... | collective-permute-start | bytes 786440 | tf_op jit(solution)/shard_map/chip_rows/ppermute | solution.py:370
  10.5 1.5 %collective-permute-start = (s32[2]{0:T(128)}, s32[2]{0:T(128)S(1)}, u32[]{:S(2)}, u32[]{:S(2)}) collective-permute-start(s32[2]{0:T(128)} %bitcast.8), channel_id=1, source_target_pairs={{0,4},{4,0},{8,12},{12,8},{16,20},{20,16},{24,28},{28,24},{1,5},{5... | collective-permute-start | bytes 32 | tf_op jit(solution)/shard_map/mate_chosen/ppermute | solution.py:370
  12.1 1.6 %shard_map.130 = (bf16[256,512]{1,0:T(8,128)(2,1)S(1)}, f32[8,128]{1,0:T(8,128)}) custom-call(f32[8,128]{1,0:T(8,128)} %get-tuple-element.66.refs_0_, f32[1,512,512]{2,1,0:T(8,128)} %refs_2_.3), custom_call_target="tpu_custom_call" | custom-call | flops 1 | bytes 1 | tf_op jit(solution)/shard_map/pallas_call | solution.py:57
  13.7 4.2 %collective-permute-done.5.refs_2_.refs_7_ = bf16[256,512]{1,0:T(8,128)(2,1)S(1)} collective-permute-done((bf16[256,512]{1,0:T(8,128)(2,1)S(1)}, bf16[256,512]{1,0:T(8,128)(2,1)S(1)}, u32[]{:S(2)}, u32[]{:S(2)}) %collective-permute-start.5) | collective-permute-done | bytes 262176 | tf_op jit(solution)/shard_map/cols_far_0/ppermute | solution.py:370
  19.4 2.5 %collective-permute-start.7 = (bf16[256,512]{1,0:T(8,128)(2,1)S(1)}, bf16[256,512]{1,0:T(8,128)(2,1)S(1)}, u32[]{:S(2)}, u32[]{:S(2)}) collective-permute-start(bf16[256,512]{1,0:T(8,128)(2,1)S(1)} %collective-permute-done.5.refs_2_.refs_7_), channel_id=1, source_target_pairs={{0,8},{4,12},{8,0},{12,4},{16,24},{20,28},{24,16},{28,20},{1,9},{5... | collective-permute-start | bytes 786440 | tf_op jit(solution)/shard_map/cols_cross_0/ppermute | solution.py:370
  22.1 10.9 %collective-permute-done.7.refs_0_ = bf16[256,512]{1,0:T(8,128)(2,1)S(1)} collective-permute-done((bf16[256,512]{1,0:T(8,128)(2,1)S(1)}, bf16[256,512]{1,0:T(8,128)(2,1)S(1)}, u32[]{:S(2)}, u32[]{:S(2)}) %collective-permute-start.7) | collective-permute-done | bytes 262176 | tf_op jit(solution)/shard_map/cols_cross_0/ppermute | solution.py:370
  33.0 1.9 %shard_map.133 = (bf16[2,256,512]{2,1,0:T(8,128)(2,1)}, bf16[2,256,512]{2,1,0:T(8,128)(2,1)S(1)}, f32[8,128]{1,0:T(8,128)}) custom-call(f32[8,128]{1,0:T(8,128)} %get-tuple-element.67.refs_3_.refs_1_.refs_0_, bf16[256,512]{1,0:T(8,128)(2,1)S(1)} %collective-permute-done.1.refs_1_.refs_5_.refs_3_, ...), custom_call_target="tpu_custom_call" | custom-call | flops 1 | bytes 1 | tf_op jit(solution)/shard_map/pallas_call | solution.py:57
  36.3 1.5 %collective-permute-start.10 = (bf16[2,256,512]{2,1,0:T(8,128)(2,1)}, bf16[2,256,512]{2,1,0:T(8,128)(2,1)S(1)}, u32[]{:S(2)}, u32[]{:S(2)}) collective-permute-start(bf16[2,256,512]{2,1,0:T(8,128)(2,1)} %get-tuple-element.74), channel_id=1, source_target_pairs={{0,4},{4,0},{8,12},{12,8},{16,20},{20,16},{24,28},{28,24},{1,5},{5... | collective-permute-start | bytes 1572872 | tf_op jit(solution)/shard_map/cols_mate_0/ppermute | solution.py:370
  38.7 6.6 %shard_map.134 = (f32[256,512]{1,0:T(8,128)S(1)}, f32[256,512]{1,0:T(8,128)S(1)}, f32[256,512]{1,0:T(8,128)S(1)}, f32[256,512]{1,0:T(8,128)S(1)}, f32[2,256,512]...) custom-call(s32[8]{0:T(128)S(1)} %concatenate.3.refs_4_.refs_0_.refs_1_, ...), custom_call_target="tpu_custom_call" | custom-call | flops 1 | bytes 1 | tf_op jit(solution)/shard_map/pallas_call | solution.py:57
  45.3 2.0 %shard_map.136 = (bf16[2,256,512]{2,1,0:T(8,128)(2,1)S(1)}, bf16[2,256,512]{2,1,0:T(8,128)(2,1)S(1)}, f32[8,128]{1,0:T(8,128)}) custom-call(f32[8,128]{1,0:T(8,128)} %get-tuple-element.72.refs_0_, s32[8]{0:T(128)S(1)} %concatenate.3.refs_4_.refs_0_.refs_1_, bf16[256,512]{1,0:T(8,128)(2,1)} %copy-done.5, bf16[256,512]{1,0:T(8,128)(2,1)S(1)} %collective-permute-done.8.refs_3_, ...), custom_call_target="tpu_custom_call" | custom-call | flops 1 | bytes 1 | tf_op jit(solution)/shard_map/pallas_call | solution.py:57
  47.8 3.6 %shard_map.137 = (f32[256,512]{1,0:T(8,128)S(1)}, f32[256,512]{1,0:T(8,128)S(1)}, f32[256,512]{1,0:T(8,128)S(1)}, f32[256,512]{1,0:T(8,128)S(1)}, bf16[2,256,512]{2,1,0:T(8,128)(2,1)}, /*index=5*/f32[8,128]{1,0:T(8,128)}) custom-call(f32[8,128]{1,0:T(8,128)} %get-tuple-element.73.refs_0_, s32[8]{0:T(128)S(1)} %concatenate.3.refs_4_.refs_0_.refs_1_, ...), custom_call_target="tpu_custom_call" | custom-call | flops 1 | bytes 1 | tf_op jit(solution)/shard_map/pallas_call | solution.py:57
  51.4 1.5 %collective-permute-start.13 = (bf16[2,256,512]{2,1,0:T(8,128)(2,1)}, bf16[2,256,512]{2,1,0:T(8,128)(2,1)S(1)}, u32[]{:S(2)}, u32[]{:S(2)}) collective-permute-start(bf16[2,256,512]{2,1,0:T(8,128)(2,1)} %get-tuple-element.99), channel_id=1, source_target_pairs={{0,4},{4,0},{8,12},{12,8},{16,20},{20,16},{24,28},{28,24},{1,5},{5... | collective-permute-start | bytes 1572872 | tf_op jit(solution)/shard_map/grads_mate_0/ppermute | solution.py:370
  52.9 6.6 %shard_map.138 = (f32[256,512]{1,0:T(8,128)S(1)}, f32[256,512]{1,0:T(8,128)S(1)}, f32[256,512]{1,0:T(8,128)S(1)}, f32[256,512]{1,0:T(8,128)S(1)}, f32[2,256,512]...) custom-call(s32[8]{0:T(128)S(1)} %concatenate.3.refs_4_.refs_0_.refs_1_, ...), custom_call_target="tpu_custom_call" | custom-call | flops 1 | bytes 1 | tf_op jit(solution)/shard_map/pallas_call | solution.py:57
  59.5 2.7 %collective-permute-done.11.refs_6_ = bf16[2,256,512]{2,1,0:T(8,128)(2,1)S(1)} collective-permute-done((bf16[2,256,512]{2,1,0:T(8,128)(2,1)S(1)}, bf16[2,256,512]{2,1,0:T(8,128)(2,1)S(1)}, u32[]{:S(2)}, u32[]{:S(2)}) %collective-permute-start.11) | collective-permute-done | bytes 524320 | tf_op jit(solution)/shard_map/cols_mate_1/ppermute | solution.py:370
  62.2 4.0 %shard_map.139 = (f32[256,512]{1,0:T(8,128)S(1)}, f32[256,512]{1,0:T(8,128)}, f32[256,512]{1,0:T(8,128)S(1)}, f32[256,512]{1,0:T(8,128)}, bf16[2,256,512]{2,1,0:T(8,128)(2,1)}, /*index=5*/f32[8,128]{1,0:T(8,128)}) custom-call(f32[8,128]{1,0:T(8,128)} %get-tuple-element.83.refs_0_, s32[8]{0:T(128)S(1)} %concatenate.3.refs_4_.refs_0_.refs_1_, ...), custom_call_target="tpu_custom_call" | custom-call | flops 1 | bytes 1 | tf_op jit(solution)/shard_map/pallas_call | solution.py:57
  67.2 2.4 %collective-permute-done.13.refs_3_ = bf16[2,256,512]{2,1,0:T(8,128)(2,1)S(1)} collective-permute-done((bf16[2,256,512]{2,1,0:T(8,128)(2,1)}, bf16[2,256,512]{2,1,0:T(8,128)(2,1)S(1)}, u32[]{:S(2)}, u32[]{:S(2)}) %collective-permute-start.13) | collective-permute-done | bytes 524320 | tf_op jit(solution)/shard_map/grads_mate_0/ppermute | solution.py:370
  69.6 1.9 %shard_map.140 = (f32[2,128,512]{2,1,0:T(8,128)}, bf16[2,128,512]{2,1,0:T(8,128)(2,1)}, f32[2,128,512]{2,1,0:T(8,128)}, bf16[2,128,512]{2,1,0:T(8,128)(2,1)S(1)}, f32[8,128]{1,0:T(8,128)}) custom-call(f32[8,128]{1,0:T(8,128)} %get-tuple-element.97.refs_0_, s32[8]{0:T(128)S(1)} %concatenate.3.refs_4_.refs_0_.refs_1_, f32[2,256,512]{2,1,0:T(8,128)S(1)} %copy-done.4, ...), custom_call_target="tpu_custom_call" | custom-call | flops 1 | bytes 1 | tf_op jit(solution)/shard_map/pallas_call | solution.py:57
  73.7 6.4 %collective-permute-done.15.refs_4_ = bf16[2,128,512]{2,1,0:T(8,128)(2,1)S(1)} collective-permute-done((bf16[2,128,512]{2,1,0:T(8,128)(2,1)S(1)}, bf16[2,128,512]{2,1,0:T(8,128)(2,1)S(1)}, u32[]{:S(2)}, u32[]{:S(2)}) %collective-permute-start.15) | collective-permute-done | bytes 262176 | tf_op jit(solution)/shard_map/grads_cross_0_0/ppermute | solution.py:370
  80.1 1.7 %shard_map.141 = (bf16[2,128,512]{2,1,0:T(8,128)(2,1)S(1)}, f32[8,128]{1,0:T(8,128)}) custom-call(f32[8,128]{1,0:T(8,128)} %get-tuple-element.100.refs_0_, f32[256,512]{1,0:T(8,128)S(1)} %collective-permute-done.14.refs_1_.refs_2_, f32[256,512]{1,0:T(8,128)S(1)} %collective-permute-done.12.refs_2_, f32[2,128,512]{2,1,0:T(8,128)} %get-tuple-element.102.refs_3_, ...), custom_call_target="tpu_custom_call" | custom-call | flops 1 | bytes 1 | tf_op jit(solution)/shard_map/pallas_call | solution.py:57
  81.8 4.5 %collective-permute-start.19 = (bf16[2,128,512]{2,1,0:T(8,128)(2,1)S(1)}, bf16[2,128,512]{2,1,0:T(8,128)(2,1)S(1)}, u32[]{:S(2)}, u32[]{:S(2)}) collective-permute-start(bf16[2,128,512]{2,1,0:T(8,128)(2,1)S(1)} %get-tuple-element.112), channel_id=1, source_target_pairs={{0,16},{4,20},{8,24},{12,28},{16,0},{20,4},{24,8},{28,12},{1,17},{... | collective-permute-start | bytes 786440 | tf_op jit(solution)/shard_map/grads_far_0/ppermute | solution.py:370
  86.3 2.3 %shard_map.142 = (f32[2,128,512]{2,1,0:T(8,128)}, bf16[2,128,512]{2,1,0:T(8,128)(2,1)}, f32[1,128,512]{2,1,0:T(8,128)}, f32[1,128,512]{2,1,0:T(8,128)}, bf16[1,1...) custom-call(f32[8,128]{1,0:T(8,128)} %get-tuple-element.104.refs_0_, ...), custom_call_target="tpu_custom_call" | custom-call | flops 1 | bytes 1 | tf_op jit(solution)/shard_map/pallas_call | solution.py:57
  91.1 1.9 %collective-permute-start.21 = (bf16[1,128,512]{2,1,0:T(8,128)(2,1)}, bf16[1,128,512]{2,1,0:T(8,128)(2,1)S(1)}, u32[]{:S(2)}, u32[]{:S(2)}) collective-permute-start(bf16[1,128,512]{2,1,0:T(8,128)(2,1)} %copy-done.12), channel_id=1, source_target_pairs={{0,8},{4,12},{8,0},{12,4},{16,24},{20,28},{24,16},{28,20},{1,9},{5... | collective-permute-start | bytes 393224 | tf_op jit(solution)/shard_map/grads_cross_1_1/ppermute | solution.py:370
  93.5 5.1 %collective-permute-done.20.refs_3_ = bf16[1,128,512]{2,1,0:T(8,128)(2,1)S(1)} collective-permute-done((bf16[1,128,512]{2,1,0:T(8,128)(2,1)}, bf16[1,128,512]{2,1,0:T(8,128)(2,1)S(1)}, u32[]{:S(2)}, u32[]{:S(2)}) %collective-permute-start.20) | collective-permute-done | bytes 131104 | tf_op jit(solution)/shard_map/grads_cross_1_0/ppermute | solution.py:370
  98.6 1.5 %shard_map.145 = (bf16[1,128,512]{2,1,0:T(8,128)(2,1)S(1)}, f32[8,128]{1,0:T(8,128)}) custom-call(f32[8,128]{1,0:T(8,128)} %get-tuple-element.107.refs_0_.refs_3_, f32[2,128,512]{2,1,0:T(8,128)S(1)} %shard_map.144.refs_1_.refs_3_, f32[1,128,512]{2,1,0:T(8,128)} %get-tuple-element.113.refs_2_, bf16[1,128,512]{2,1,0:T(8,128)(2,1)S(1)} %collective-permute-done.20.refs_3_), custom_call_target="tpu_custom_call" | custom-call | flops 1 | bytes 1 | tf_op jit(solution)/shard_map/pallas_call | solution.py:57
  100.6 1.5 %shard_map.146 = (bf16[1,128,512]{2,1,0:T(8,128)(2,1)S(1)}, f32[8,128]{1,0:T(8,128)}) custom-call(f32[8,128]{1,0:T(8,128)} %get-tuple-element.115.refs_0_, f32[2,128,512]{2,1,0:T(8,128)S(1)} %shard_map.144.refs_1_.refs_3_, f32[1,128,512]{2,1,0:T(8,128)} %get-tuple-element.116.refs_2_, bf16[1,128,512]{2,1,0:T(8,128)(2,1)S(1)} %collective-permute-done.21.refs_3_), custom_call_target="tpu_custom_call" | custom-call | flops 1 | bytes 1 | tf_op jit(solution)/shard_map/pallas_call | solution.py:57
  102.2 2.5 %collective-permute-start.24 = (bf16[1,128,512]{2,1,0:T(8,128)(2,1)S(1)}, bf16[1,128,512]{2,1,0:T(8,128)(2,1)S(1)}, u32[]{:S(2)}, u32[]{:S(2)}) collective-permute-start(bf16[1,128,512]{2,1,0:T(8,128)(2,1)S(1)} %get-tuple-element.123), channel_id=1, source_target_pairs={{0,16},{4,20},{8,24},{12,28},{16,0},{20,4},{24,8},{28,12},{1,17},{... | collective-permute-start | bytes 393224 | tf_op jit(solution)/shard_map/grads_far_1_1/ppermute | solution.py:370
  104.6 2.3 %multiply_subtract_fusion = (f32[256,512]{1,0:T(8,128)}, f32[256,512]{1,0:T(8,128)S(1)}) fusion(f32[256,512]{1,0:T(8,128)} %refs_1_.3, f32[256]{0:T(256)S(1)} %fusion.1, bf16[256,512]{1,0:T(8,128)(2,1)} %collective-permute-done.17, f32[256,512]{1,0:T(8,128)S(1)} %copy-done.7, f32[256,512]{1,0:T(8,128)S(1)} %collective-permute-done.12.refs_2_, ...), kind=kLoop, calls=%fused_computation.1 | loop fusion | flops 1310720 | bytes 3408896 | tf_op jit(solution)/shard_map/sub | solution.py:510
  106.9 2.3 %shard_map.147 = (f32[1,512,512]{2,1,0:T(8,128)}, f32[1,512,512]{2,1,0:T(8,128)}, f32[8,128]{1,0:T(8,128)}) custom-call(f32[8,128]{1,0:T(8,128)} %get-tuple-element.118.refs_0_, f32[1,512,512]{2,1,0:T(8,128)} %refs_2_.3, f32[1,512,512]{2,1,0:T(8,128)} %refs_3_.5, f32[2,128,512]{2,1,0:T(8,128)S(1)} %shard_map.144.refs_1_.refs_3_, ...), custom_call_target="tpu_custom_call" | custom-call | flops 1 | bytes 1 | tf_op jit(solution)/shard_map/pallas_call | solution.py:57
  110.2 2.1 %shard_map.148 = (f32[1,512,512]{2,1,0:T(8,128)}, f32[1,512,512]{2,1,0:T(8,128)}, f32[8,128]{1,0:T(8,128)}) custom-call(f32[8,128]{1,0:T(8,128)} %get-tuple-element.119.refs_0_, f32[256,512]{1,0:T(8,128)S(1)} %get-tuple-element.129.refs_1_, f32[1,512,512]{2,1,0:T(8,128)} %refs_2_.3, ...), custom_call_target="tpu_custom_call", output_to_operand_aliasing={{0}: (8, {}), {1}: (9, {})} | custom-call | flops 1 | bytes 1 | tf_op jit(solution)/shard_map/pallas_call | solution.py:57
  (82 shorter events, 12.5 us)
Async XLA Ops:
  0.6 21.3 %copy-start.16 = (s32[1,1,2]{2,1,0:T(1,128)S(1)}, s32[1,1,2]{2,1,0:T(1,128)}, u32[]{:S(2)}) copy-start(s32[1,1,2]{2,1,0:T(1,128)} %param.16) | copy-start | bytes 28
  1.7 31.3 %copy-start.1 = (bf16[256,512]{1,0:T(8,128)(2,1)}, bf16[256,512]{1,0:T(8,128)(2,1)S(1)}, u32[]{:S(2)}) copy-start(bf16[256,512]{1,0:T(8,128)(2,1)S(1)} %fusion.refs_0_.refs_5_) | copy-start | bytes 786436
  1.7 16.1 %collective-permute-start.5 = (bf16[256,512]{1,0:T(8,128)(2,1)S(1)}, bf16[256,512]{1,0:T(8,128)(2,1)S(1)}, u32[]{:S(2)}, u32[]{:S(2)}) collective-permute-start(bf16[256,512]{1,0:T(8,128)(2,1)S(1)} %fusion.refs_0_.refs_5_), channel_id=1, source_target_pairs={{0,16},{4,20},{8,24},{12,28},{16,0},{20,4},{24,8},{28,12},{1,17},{... | collective-permute-start | bytes 786440 | tf_op jit(solution)/shard_map/cols_far_0/ppermute | solution.py:370
  5.8 12.2 %collective-permute-start.4 = (bf16[256,512]{1,0:T(8,128)(2,1)S(1)}, bf16[256,512]{1,0:T(8,128)(2,1)S(1)}, u32[]{:S(2)}, u32[]{:S(2)}) collective-permute-start(bf16[256,512]{1,0:T(8,128)(2,1)S(1)} %fusion.refs_0_.refs_5_), channel_id=1, source_target_pairs={{0,8},{4,12},{8,0},{12,4},{16,24},{20,28},{24,16},{28,20},{1,9},{5... | collective-permute-start | bytes 786440 | tf_op jit(solution)/shard_map/cols_near_0/ppermute | solution.py:370
  9.0 12.9 %collective-permute-start.2 = (bf16[256,512]{1,0:T(8,128)(2,1)S(1)}, bf16[256,512]{1,0:T(8,128)(2,1)S(1)}, u32[]{:S(2)}, u32[]{:S(2)}) collective-permute-start(bf16[256,512]{1,0:T(8,128)(2,1)S(1)} %get-tuple-element.68.refs_4_.refs_2_), channel_id=1, source_target_pairs={{0,2},{1,3},{2,0},{3,1},{4,6},{5,7},{6,4},{7,5},{8,10},{9,11},{10,... | collective-permute-start | bytes 786440 | tf_op jit(solution)/shard_map/chip_rows/ppermute | solution.py:370
  10.5 22.5 %collective-permute-start.1 = (bf16[256,512]{1,0:T(8,128)(2,1)S(1)}, bf16[256,512]{1,0:T(8,128)(2,1)S(1)}, u32[]{:S(2)}, u32[]{:S(2)}) collective-permute-start(bf16[256,512]{1,0:T(8,128)(2,1)S(1)} %get-tuple-element.68.refs_4_.refs_2_), channel_id=1, source_target_pairs={{0,1},{1,0},{2,3},{3,2},{4,5},{5,4},{6,7},{7,6},{8,9},{9,8},{10,11... | collective-permute-start | bytes 786440 | tf_op jit(solution)/shard_map/core_rows/ppermute | solution.py:370
  10.5 11.4 %collective-permute-start = (s32[2]{0:T(128)}, s32[2]{0:T(128)S(1)}, u32[]{:S(2)}, u32[]{:S(2)}) collective-permute-start(s32[2]{0:T(128)} %bitcast.8), channel_id=1, source_target_pairs={{0,4},{4,0},{8,12},{12,8},{16,20},{20,16},{24,28},{28,24},{1,5},{5... | collective-permute-start | bytes 32 | tf_op jit(solution)/shard_map/mate_chosen/ppermute | solution.py:370
  13.7 24.8 %copy-start.14 = (s32[1024]{0:T(1024)S(1)}, s32[1024]{0:T(1024)}, u32[]{:S(2)}) copy-start(s32[1024]{0:T(1024)} %param.15) | copy-start | bytes 12292
  18.1 20.6 %copy-start.11 = (s32[1,4096]{1,0:T(1,128)S(1)}, s32[1,4096]{1,0:T(1,128)}, u32[]{:S(2)}) copy-start(s32[1,4096]{1,0:T(1,128)} %refs_3_.4) | copy-start | bytes 49156
  18.1 27.2 %copy-start.5 = (bf16[256,512]{1,0:T(8,128)(2,1)}, bf16[256,512]{1,0:T(8,128)(2,1)S(1)}, u32[]{:S(2)}) copy-start(bf16[256,512]{1,0:T(8,128)(2,1)S(1)} %shard_map.131.refs_2_) | copy-start | bytes 786436
  18.1 15.0 %collective-permute-start.6 = (bf16[256,512]{1,0:T(8,128)(2,1)S(1)}, bf16[256,512]{1,0:T(8,128)(2,1)S(1)}, u32[]{:S(2)}, u32[]{:S(2)}) collective-permute-start(bf16[256,512]{1,0:T(8,128)(2,1)S(1)} %shard_map.131.refs_2_), channel_id=1, source_target_pairs={{0,16},{4,20},{8,24},{12,28},{16,0},{20,4},{24,8},{28,12},{1,17},{... | collective-permute-start | bytes 786440 | tf_op jit(solution)/shard_map/cols_far_1/ppermute | solution.py:370
  19.4 13.6 %collective-permute-start.7 = (bf16[256,512]{1,0:T(8,128)(2,1)S(1)}, bf16[256,512]{1,0:T(8,128)(2,1)S(1)}, u32[]{:S(2)}, u32[]{:S(2)}) collective-permute-start(bf16[256,512]{1,0:T(8,128)(2,1)S(1)} %collective-permute-done.5.refs_2_.refs_7_), channel_id=1, source_target_pairs={{0,8},{4,12},{8,0},{12,4},{16,24},{20,28},{24,16},{28,20},{1,9},{5... | collective-permute-start | bytes 786440 | tf_op jit(solution)/shard_map/cols_cross_0/ppermute | solution.py:370
  21.9 11.1 %collective-permute-start.3 = (bf16[256,512]{1,0:T(8,128)(2,1)S(1)}, bf16[256,512]{1,0:T(8,128)(2,1)S(1)}, u32[]{:S(2)}, u32[]{:S(2)}) collective-permute-start(bf16[256,512]{1,0:T(8,128)(2,1)S(1)} %collective-permute-done.2.refs_6_.refs_4_), channel_id=1, source_target_pairs={{0,1},{1,0},{2,3},{3,2},{4,5},{5,4},{6,7},{7,6},{8,9},{9,8},{10,11... | collective-permute-start | bytes 786440 | tf_op jit(solution)/shard_map/both_rows/ppermute | solution.py:370
  22.1 23.2 %collective-permute-start.8 = (bf16[256,512]{1,0:T(8,128)(2,1)S(1)}, bf16[256,512]{1,0:T(8,128)(2,1)S(1)}, u32[]{:S(2)}, u32[]{:S(2)}) collective-permute-start(bf16[256,512]{1,0:T(8,128)(2,1)S(1)} %shard_map.131.refs_2_), channel_id=1, source_target_pairs={{0,8},{4,12},{8,0},{12,4},{16,24},{20,28},{24,16},{28,20},{1,9},{5... | collective-permute-start | bytes 786440 | tf_op jit(solution)/shard_map/cols_near_1/ppermute | solution.py:370
  35.0 10.3 %collective-permute-start.9 = (bf16[256,512]{1,0:T(8,128)(2,1)S(1)}, bf16[256,512]{1,0:T(8,128)(2,1)}, u32[]{:S(2)}, u32[]{:S(2)}) collective-permute-start(bf16[256,512]{1,0:T(8,128)(2,1)S(1)} %shard_map.135.refs_4_), channel_id=1, source_target_pairs={{0,8},{4,12},{8,0},{12,4},{16,24},{20,28},{24,16},{28,20},{1,9},{5... | collective-permute-start | bytes 786440 | tf_op jit(solution)/shard_map/cols_cross_1/ppermute | solution.py:370
  36.3 11.5 %collective-permute-start.10 = (bf16[2,256,512]{2,1,0:T(8,128)(2,1)}, bf16[2,256,512]{2,1,0:T(8,128)(2,1)S(1)}, u32[]{:S(2)}, u32[]{:S(2)}) collective-permute-start(bf16[2,256,512]{2,1,0:T(8,128)(2,1)} %get-tuple-element.74), channel_id=1, source_target_pairs={{0,4},{4,0},{8,12},{12,8},{16,20},{20,16},{24,28},{28,24},{1,5},{5... | collective-permute-start | bytes 1572872 | tf_op jit(solution)/shard_map/cols_mate_0/ppermute | solution.py:370
  47.3 14.9 %collective-permute-start.11 = (bf16[2,256,512]{2,1,0:T(8,128)(2,1)S(1)}, bf16[2,256,512]{2,1,0:T(8,128)(2,1)S(1)}, u32[]{:S(2)}, u32[]{:S(2)}) collective-permute-start(bf16[2,256,512]{2,1,0:T(8,128)(2,1)S(1)} %get-tuple-element.84), channel_id=1, source_target_pairs={{0,4},{4,0},{8,12},{12,8},{16,20},{20,16},{24,28},{28,24},{1,5},{5... | collective-permute-start | bytes 1572872 | tf_op jit(solution)/shard_map/cols_mate_1/ppermute | solution.py:370
  51.4 18.2 %collective-permute-start.13 = (bf16[2,256,512]{2,1,0:T(8,128)(2,1)}, bf16[2,256,512]{2,1,0:T(8,128)(2,1)S(1)}, u32[]{:S(2)}, u32[]{:S(2)}) collective-permute-start(bf16[2,256,512]{2,1,0:T(8,128)(2,1)} %get-tuple-element.99), channel_id=1, source_target_pairs={{0,4},{4,0},{8,12},{12,8},{16,20},{20,16},{24,28},{28,24},{1,5},{5... | collective-permute-start | bytes 1572872 | tf_op jit(solution)/shard_map/grads_mate_0/ppermute | solution.py:370
  66.1 20.1 %copy-start.3 = (f32[2,256,512]{2,1,0:T(8,128)S(1)}, f32[2,256,512]{2,1,0:T(8,128)}, u32[]{:S(2)}) copy-start(f32[2,256,512]{2,1,0:T(8,128)} %get-tuple-element.105.refs_2_) | copy-start | bytes 3145732
  66.1 13.9 %collective-permute-start.12 = (f32[256,512]{1,0:T(8,128)}, f32[256,512]{1,0:T(8,128)S(1)}, u32[]{:S(2)}, u32[]{:S(2)}) collective-permute-start(f32[256,512]{1,0:T(8,128)} %get-tuple-element.96), channel_id=1, source_target_pairs={{0,1},{1,0},{2,3},{3,2},{4,5},{5,4},{6,7},{7,6},{8,9},{9,8},{10,11... | collective-permute-start | bytes 1572872 | tf_op jit(solution)/shard_map/row_grads_core/ppermute | solution.py:370
  66.2 13.8 %collective-permute-start.14 = (f32[256,512]{1,0:T(8,128)}, f32[256,512]{1,0:T(8,128)S(1)}, u32[]{:S(2)}, u32[]{:S(2)}) collective-permute-start(f32[256,512]{1,0:T(8,128)} %get-tuple-element.101), channel_id=1, source_target_pairs={{0,1},{1,0},{2,3},{3,2},{4,5},{5,4},{6,7},{7,6},{8,9},{9,8},{10,11... | collective-permute-start | bytes 1572872 | tf_op jit(solution)/shard_map/row_grads_both/ppermute | solution.py:370
  66.7 19.5 %collective-permute-start.16 = (bf16[2,256,512]{2,1,0:T(8,128)(2,1)}, bf16[2,256,512]{2,1,0:T(8,128)(2,1)}, u32[]{:S(2)}, u32[]{:S(2)}) collective-permute-start(bf16[2,256,512]{2,1,0:T(8,128)(2,1)} %get-tuple-element.106), channel_id=1, source_target_pairs={{0,4},{4,0},{8,12},{12,8},{16,20},{20,16},{24,28},{28,24},{1,5},{5... | collective-permute-start | bytes 1572872 | tf_op jit(solution)/shard_map/grads_mate_1/ppermute | solution.py:370
  71.6 8.5 %collective-permute-start.15 = (bf16[2,128,512]{2,1,0:T(8,128)(2,1)S(1)}, bf16[2,128,512]{2,1,0:T(8,128)(2,1)S(1)}, u32[]{:S(2)}, u32[]{:S(2)}) collective-permute-start(bf16[2,128,512]{2,1,0:T(8,128)(2,1)S(1)} %get-tuple-element.103), channel_id=1, source_target_pairs={{0,8},{4,12},{8,0},{12,4},{16,24},{20,28},{24,16},{28,20},{1,9},{5... | collective-permute-start | bytes 786440 | tf_op jit(solution)/shard_map/grads_cross_0_0/ppermute | solution.py:370
  72.9 20.2 %collective-permute-start.18 = (bf16[2,128,512]{2,1,0:T(8,128)(2,1)}, bf16[2,128,512]{2,1,0:T(8,128)(2,1)S(1)}, u32[]{:S(2)}, u32[]{:S(2)}) collective-permute-start(bf16[2,128,512]{2,1,0:T(8,128)(2,1)} %get-tuple-element.111), channel_id=1, source_target_pairs={{0,8},{4,12},{8,0},{12,4},{16,24},{20,28},{24,16},{28,20},{1,9},{5... | collective-permute-start | bytes 786440 | tf_op jit(solution)/shard_map/grads_near_0/ppermute | solution.py:370
  81.8 11.8 %collective-permute-start.19 = (bf16[2,128,512]{2,1,0:T(8,128)(2,1)S(1)}, bf16[2,128,512]{2,1,0:T(8,128)(2,1)S(1)}, u32[]{:S(2)}, u32[]{:S(2)}) collective-permute-start(bf16[2,128,512]{2,1,0:T(8,128)(2,1)S(1)} %get-tuple-element.112), channel_id=1, source_target_pairs={{0,16},{4,20},{8,24},{12,28},{16,0},{20,4},{24,8},{28,12},{1,17},{... | collective-permute-start | bytes 786440 | tf_op jit(solution)/shard_map/grads_far_0/ppermute | solution.py:370
  88.6 16.1 %copy-start.7 = (f32[256,512]{1,0:T(8,128)S(1)}, f32[256,512]{1,0:T(8,128)}, u32[]{:S(2)}) copy-start(f32[256,512]{1,0:T(8,128)} %copy-done.6) | copy-start | bytes 1572868
  89.2 15.4 %collective-permute-start.17 = (bf16[256,512]{1,0:T(8,128)(2,1)S(1)}, bf16[256,512]{1,0:T(8,128)(2,1)}, u32[]{:S(2)}, u32[]{:S(2)}) collective-permute-start(bf16[256,512]{1,0:T(8,128)(2,1)S(1)} %get-tuple-element.109), channel_id=1, source_target_pairs={{0,2},{1,3},{2,0},{3,1},{4,6},{5,7},{6,4},{7,5},{8,10},{9,11},{10,... | collective-permute-start | bytes 786440 | tf_op jit(solution)/shard_map/row_grads_chip/ppermute | solution.py:370
  90.9 7.7 %collective-permute-start.20 = (bf16[1,128,512]{2,1,0:T(8,128)(2,1)}, bf16[1,128,512]{2,1,0:T(8,128)(2,1)S(1)}, u32[]{:S(2)}, u32[]{:S(2)}) collective-permute-start(bf16[1,128,512]{2,1,0:T(8,128)(2,1)} %copy-done.13), channel_id=1, source_target_pairs={{0,8},{4,12},{8,0},{12,4},{16,24},{20,28},{24,16},{28,20},{1,9},{5... | collective-permute-start | bytes 393224 | tf_op jit(solution)/shard_map/grads_cross_1_0/ppermute | solution.py:370
  91.1 9.6 %collective-permute-start.21 = (bf16[1,128,512]{2,1,0:T(8,128)(2,1)}, bf16[1,128,512]{2,1,0:T(8,128)(2,1)S(1)}, u32[]{:S(2)}, u32[]{:S(2)}) collective-permute-start(bf16[1,128,512]{2,1,0:T(8,128)(2,1)} %copy-done.12), channel_id=1, source_target_pairs={{0,8},{4,12},{8,0},{12,4},{16,24},{20,28},{24,16},{28,20},{1,9},{5... | collective-permute-start | bytes 393224 | tf_op jit(solution)/shard_map/grads_cross_1_1/ppermute | solution.py:370
  93.1 16.2 %collective-permute-start.22 = (bf16[2,128,512]{2,1,0:T(8,128)(2,1)}, bf16[2,128,512]{2,1,0:T(8,128)(2,1)S(1)}, u32[]{:S(2)}, u32[]{:S(2)}) collective-permute-start(bf16[2,128,512]{2,1,0:T(8,128)(2,1)} %get-tuple-element.121), channel_id=1, source_target_pairs={{0,8},{4,12},{8,0},{12,4},{16,24},{20,28},{24,16},{28,20},{1,9},{5... | collective-permute-start | bytes 786440 | tf_op jit(solution)/shard_map/grads_near_1/ppermute | solution.py:370
  100.2 9.1 %collective-permute-start.23 = (bf16[1,128,512]{2,1,0:T(8,128)(2,1)S(1)}, bf16[1,128,512]{2,1,0:T(8,128)(2,1)S(1)}, u32[]{:S(2)}, u32[]{:S(2)}) collective-permute-start(bf16[1,128,512]{2,1,0:T(8,128)(2,1)S(1)} %get-tuple-element.122), channel_id=1, source_target_pairs={{0,16},{4,20},{8,24},{12,28},{16,0},{20,4},{24,8},{28,12},{1,17},{... | collective-permute-start | bytes 393224 | tf_op jit(solution)/shard_map/grads_far_1_0/ppermute | solution.py:370
  102.2 8.1 %collective-permute-start.24 = (bf16[1,128,512]{2,1,0:T(8,128)(2,1)S(1)}, bf16[1,128,512]{2,1,0:T(8,128)(2,1)S(1)}, u32[]{:S(2)}, u32[]{:S(2)}) collective-permute-start(bf16[1,128,512]{2,1,0:T(8,128)(2,1)S(1)} %get-tuple-element.123), channel_id=1, source_target_pairs={{0,16},{4,20},{8,24},{12,28},{16,0},{20,4},{24,8},{28,12},{1,17},{... | collective-permute-start | bytes 393224 | tf_op jit(solution)/shard_map/grads_far_1_1/ppermute | solution.py:370
  (10 other events, 71.2 us)

commit v6 on v5

--- a/solution.py
+++ b/solution.py
@@ -449,7 +449,7 @@
 
     *_, cross = cols
     cols = (*cols[:3], *gated((cross,), (done,)))
-    kept, received, cols, coming, done = pick_part(0, cols, coming, done, core_rows, both_rows)
+    kept, received, cols, coming, done = pick_part(0, cols, coming, done, core_rows, chip_rows)
     for part in range(parts):
         own_rows, mine, terms, done = own(part, kept, done)
         if part + 1 < parts:
@@ -467,7 +467,7 @@
                 home_grad, core_grad, chip_grad, both_grad = other_rows
                 both_core = swap("row_grads_both", both_grad, "col", core_swap)
                 from_core = swap("row_grads_core", core_grad, "col", core_swap)
-            extra = (both_core, from_core) if part + 1 == parts else ()
+            extra = (both_core,) if part + 1 == parts else ()
             sent, done = send_part(part - 1, sums, done, *extra)
         row_grads.append(other_rows)
         waiting = mine, from_mate

time: 113 us -> 113 us (level)
  waiting for transfers between devices: 33.6 us -> 32 us
    ppermute x25, waiting for transfers between devices: 33.6 us -> 32 us  [swap(): return lax.ppermute(value, axis, pairs)]
  transfers between devices with their start and end apart: 25 -> 25, of which waited for: 10 -> 9; matrix products, arithmetic and copies ran while one was open for 3% -> 3% of each run, Pallas kernels for 35% -> 36%
where the time goes in v6:
time: 113 us; the launch traced here: 112 us
  Pallas kernels  42.2 us (37%)
  waiting for transfers between devices  32 us (28%)
  starting transfers between devices  31.9 us (28%)
  other arithmetic  2.59 us (2%)
  between operations  1.55 us (1%)
  local copies, waits for them, and re-layouts  1.45 us (1%)
    pallas_call x16, Pallas kernels, in_order(): call(*([scalars] if ahead else []), *held(tokens), *args)  42.2 us
    ppermute x25, waiting for transfers between devices, swap(): return lax.ppermute(value, axis, pairs)  32 us
    ppermute x25, starting transfers between devices, swap(): return lax.ppermute(value, axis, pairs)  31.9 us
    sub x1, other arithmetic, row_updates(): row_embed_new = row_embed - learn_rate * full_grad / jnp.sqrt(row_accum_new)  2.31 us
  transfers between devices with their start and end apart: 25, of which 9 were waited for; matrix products, arithmetic and copies ran while one was open for 3% of the time, Pallas kernels for 36%

profile of v6, /device:TPU:0, one launch (start us, length us, event | category | flops | bytes accessed | tf_op | source)
XLA Modules:
  0.0 111.7 jit_solution(3559174695612154574)
XLA Ops:
  1.7 4.1 %collective-permute-start.4 = (bf16[256,512]{1,0:T(8,128)(2,1)S(1)}, bf16[256,512]{1,0:T(8,128)(2,1)S(1)}, u32[]{:S(2)}, u32[]{:S(2)}) collective-permute-start(bf16[256,512]{1,0:T(8,128)(2,1)S(1)} %fusion.refs_0_.refs_5_), channel_id=1, source_target_pairs={{0,16},{4,20},{8,24},{12,28},{16,0},{20,4},{24,8},{28,12},{1,17},{... | collective-permute-start | bytes 786440 | tf_op jit(solution)/shard_map/cols_far_0/ppermute | solution.py:370
  5.8 1.6 %collective-permute-start.3 = (bf16[256,512]{1,0:T(8,128)(2,1)S(1)}, bf16[256,512]{1,0:T(8,128)(2,1)S(1)}, u32[]{:S(2)}, u32[]{:S(2)}) collective-permute-start(bf16[256,512]{1,0:T(8,128)(2,1)S(1)} %fusion.refs_0_.refs_5_), channel_id=1, source_target_pairs={{0,8},{4,12},{8,0},{12,4},{16,24},{20,28},{24,16},{28,20},{1,9},{5... | collective-permute-start | bytes 786440 | tf_op jit(solution)/shard_map/cols_near_0/ppermute | solution.py:370
  7.4 1.6 %shard_map.129 = (bf16[256,512]{1,0:T(8,128)(2,1)S(1)}, f32[8,128]{1,0:T(8,128)}) custom-call(bf16[256,512]{1,0:T(8,128)(2,1)S(1)} %fusion.refs_0_.refs_5_, f32[256,512]{1,0:T(8,128)} %refs_1_.3), custom_call_target="tpu_custom_call" | custom-call | flops 1 | bytes 1 | tf_op jit(solution)/shard_map/pallas_call | solution.py:57
  10.5 1.5 %collective-permute-start = (s32[2]{0:T(128)}, s32[2]{0:T(128)S(1)}, u32[]{:S(2)}, u32[]{:S(2)}) collective-permute-start(s32[2]{0:T(128)} %bitcast.8), channel_id=1, source_target_pairs={{0,4},{4,0},{8,12},{12,8},{16,20},{20,16},{24,28},{28,24},{1,5},{5... | collective-permute-start | bytes 32 | tf_op jit(solution)/shard_map/mate_chosen/ppermute | solution.py:370
  12.1 1.6 %shard_map.130 = (bf16[256,512]{1,0:T(8,128)(2,1)S(1)}, f32[8,128]{1,0:T(8,128)}) custom-call(f32[8,128]{1,0:T(8,128)} %get-tuple-element.66.refs_0_, f32[1,512,512]{2,1,0:T(8,128)} %refs_2_.3), custom_call_target="tpu_custom_call" | custom-call | flops 1 | bytes 1 | tf_op jit(solution)/shard_map/pallas_call | solution.py:57
  13.7 4.2 %collective-permute-done.4.refs_2_.refs_7_ = bf16[256,512]{1,0:T(8,128)(2,1)S(1)} collective-permute-done((bf16[256,512]{1,0:T(8,128)(2,1)S(1)}, bf16[256,512]{1,0:T(8,128)(2,1)S(1)}, u32[]{:S(2)}, u32[]{:S(2)}) %collective-permute-start.4) | collective-permute-done | bytes 262176 | tf_op jit(solution)/shard_map/cols_far_0/ppermute | solution.py:370
  19.4 2.5 %collective-permute-start.6 = (bf16[256,512]{1,0:T(8,128)(2,1)S(1)}, bf16[256,512]{1,0:T(8,128)(2,1)S(1)}, u32[]{:S(2)}, u32[]{:S(2)}) collective-permute-start(bf16[256,512]{1,0:T(8,128)(2,1)S(1)} %collective-permute-done.4.refs_2_.refs_7_), channel_id=1, source_target_pairs={{0,8},{4,12},{8,0},{12,4},{16,24},{20,28},{24,16},{28,20},{1,9},{5... | collective-permute-start | bytes 786440 | tf_op jit(solution)/shard_map/cols_cross_0/ppermute | solution.py:370
  22.2 10.9 %collective-permute-done.6.refs_0_ = bf16[256,512]{1,0:T(8,128)(2,1)S(1)} collective-permute-done((bf16[256,512]{1,0:T(8,128)(2,1)S(1)}, bf16[256,512]{1,0:T(8,128)(2,1)S(1)}, u32[]{:S(2)}, u32[]{:S(2)}) %collective-permute-start.6) | collective-permute-done | bytes 262176 | tf_op jit(solution)/shard_map/cols_cross_0/ppermute | solution.py:370
  33.0 1.9 %shard_map.133 = (bf16[2,256,512]{2,1,0:T(8,128)(2,1)}, bf16[2,256,512]{2,1,0:T(8,128)(2,1)S(1)}, f32[8,128]{1,0:T(8,128)}) custom-call(f32[8,128]{1,0:T(8,128)} %get-tuple-element.67.refs_3_.refs_1_.refs_0_, bf16[256,512]{1,0:T(8,128)(2,1)S(1)} %collective-permute-done.1.refs_1_.refs_5_.refs_3_, ...), custom_call_target="tpu_custom_call" | custom-call | flops 1 | bytes 1 | tf_op jit(solution)/shard_map/pallas_call | solution.py:57
  36.3 1.5 %collective-permute-start.10 = (bf16[2,256,512]{2,1,0:T(8,128)(2,1)}, bf16[2,256,512]{2,1,0:T(8,128)(2,1)}, u32[]{:S(2)}, u32[]{:S(2)}) collective-permute-start(bf16[2,256,512]{2,1,0:T(8,128)(2,1)} %get-tuple-element.74), channel_id=1, source_target_pairs={{0,4},{4,0},{8,12},{12,8},{16,20},{20,16},{24,28},{28,24},{1,5},{5... | collective-permute-start | bytes 1572872 | tf_op jit(solution)/shard_map/cols_mate_0/ppermute | solution.py:370
  38.7 6.6 %shard_map.134 = (f32[256,512]{1,0:T(8,128)S(1)}, f32[256,512]{1,0:T(8,128)S(1)}, f32[256,512]{1,0:T(8,128)S(1)}, f32[256,512]{1,0:T(8,128)S(1)}, f32[2,256,512]...) custom-call(s32[8]{0:T(128)S(1)} %concatenate.3.refs_4_.refs_0_.refs_1_, ...), custom_call_target="tpu_custom_call" | custom-call | flops 1 | bytes 1 | tf_op jit(solution)/shard_map/pallas_call | solution.py:57
  45.3 1.9 %shard_map.136 = (bf16[2,256,512]{2,1,0:T(8,128)(2,1)S(1)}, bf16[2,256,512]{2,1,0:T(8,128)(2,1)S(1)}, f32[8,128]{1,0:T(8,128)}) custom-call(f32[8,128]{1,0:T(8,128)} %get-tuple-element.72.refs_0_, s32[8]{0:T(128)S(1)} %concatenate.3.refs_4_.refs_0_.refs_1_, bf16[256,512]{1,0:T(8,128)(2,1)} %copy-done.5, bf16[256,512]{1,0:T(8,128)(2,1)S(1)} %collective-permute-done.8.refs_3_, ...), custom_call_target="tpu_custom_call" | custom-call | flops 1 | bytes 1 | tf_op jit(solution)/shard_map/pallas_call | solution.py:57
  47.7 4.0 %shard_map.137 = (f32[256,512]{1,0:T(8,128)S(1)}, f32[256,512]{1,0:T(8,128)S(1)}, f32[256,512]{1,0:T(8,128)S(1)}, f32[256,512]{1,0:T(8,128)S(1)}, bf16[2,256,512]{2,1,0:T(8,128)(2,1)}, /*index=5*/f32[8,128]{1,0:T(8,128)}) custom-call(f32[8,128]{1,0:T(8,128)} %get-tuple-element.73.refs_0_, s32[8]{0:T(128)S(1)} %concatenate.3.refs_4_.refs_0_.refs_1_, ...), custom_call_target="tpu_custom_call" | custom-call | flops 1 | bytes 1 | tf_op jit(solution)/shard_map/pallas_call | solution.py:57
  51.7 1.5 %collective-permute-start.13 = (bf16[2,256,512]{2,1,0:T(8,128)(2,1)}, bf16[2,256,512]{2,1,0:T(8,128)(2,1)S(1)}, u32[]{:S(2)}, u32[]{:S(2)}) collective-permute-start(bf16[2,256,512]{2,1,0:T(8,128)(2,1)} %get-tuple-element.99), channel_id=1, source_target_pairs={{0,4},{4,0},{8,12},{12,8},{16,20},{20,16},{24,28},{28,24},{1,5},{5... | collective-permute-start | bytes 1572872 | tf_op jit(solution)/shard_map/grads_mate_0/ppermute | solution.py:370
  53.3 6.6 %shard_map.138 = (f32[256,512]{1,0:T(8,128)S(1)}, f32[256,512]{1,0:T(8,128)S(1)}, f32[256,512]{1,0:T(8,128)S(1)}, f32[256,512]{1,0:T(8,128)S(1)}, f32[2,256,512]...) custom-call(s32[8]{0:T(128)S(1)} %concatenate.3.refs_4_.refs_0_.refs_1_, ...), custom_call_target="tpu_custom_call" | custom-call | flops 1 | bytes 1 | tf_op jit(solution)/shard_map/pallas_call | solution.py:57
  59.8 2.3 %collective-permute-done.11.refs_6_ = bf16[2,256,512]{2,1,0:T(8,128)(2,1)S(1)} collective-permute-done((bf16[2,256,512]{2,1,0:T(8,128)(2,1)S(1)}, bf16[2,256,512]{2,1,0:T(8,128)(2,1)S(1)}, u32[]{:S(2)}, u32[]{:S(2)}) %collective-permute-start.11) | collective-permute-done | bytes 524320 | tf_op jit(solution)/shard_map/cols_mate_1/ppermute | solution.py:370
  62.1 4.0 %shard_map.139 = (f32[256,512]{1,0:T(8,128)S(1)}, f32[256,512]{1,0:T(8,128)}, f32[256,512]{1,0:T(8,128)S(1)}, f32[256,512]{1,0:T(8,128)}, bf16[2,256,512]{2,1,0:T(8,128)(2,1)}, /*index=5*/f32[8,128]{1,0:T(8,128)}) custom-call(f32[8,128]{1,0:T(8,128)} %get-tuple-element.83.refs_0_, s32[8]{0:T(128)S(1)} %concatenate.3.refs_4_.refs_0_.refs_1_, ...), custom_call_target="tpu_custom_call" | custom-call | flops 1 | bytes 1 | tf_op jit(solution)/shard_map/pallas_call | solution.py:57
  66.7 3.0 %collective-permute-done.13.refs_3_ = bf16[2,256,512]{2,1,0:T(8,128)(2,1)S(1)} collective-permute-done((bf16[2,256,512]{2,1,0:T(8,128)(2,1)}, bf16[2,256,512]{2,1,0:T(8,128)(2,1)S(1)}, u32[]{:S(2)}, u32[]{:S(2)}) %collective-permute-start.13) | collective-permute-done | bytes 524320 | tf_op jit(solution)/shard_map/grads_mate_0/ppermute | solution.py:370
  69.7 1.9 %shard_map.140 = (f32[2,128,512]{2,1,0:T(8,128)}, bf16[2,128,512]{2,1,0:T(8,128)(2,1)}, f32[2,128,512]{2,1,0:T(8,128)}, bf16[2,128,512]{2,1,0:T(8,128)(2,1)S(1)}, f32[8,128]{1,0:T(8,128)}) custom-call(f32[8,128]{1,0:T(8,128)} %get-tuple-element.97.refs_0_, s32[8]{0:T(128)S(1)} %concatenate.3.refs_4_.refs_0_.refs_1_, f32[2,256,512]{2,1,0:T(8,128)S(1)} %copy-done.4, ...), custom_call_target="tpu_custom_call" | custom-call | flops 1 | bytes 1 | tf_op jit(solution)/shard_map/pallas_call | solution.py:57
  73.7 6.0 %collective-permute-done.15.refs_3_ = bf16[2,128,512]{2,1,0:T(8,128)(2,1)S(1)} collective-permute-done((bf16[2,128,512]{2,1,0:T(8,128)(2,1)S(1)}, bf16[2,128,512]{2,1,0:T(8,128)(2,1)S(1)}, u32[]{:S(2)}, u32[]{:S(2)}) %collective-permute-start.15) | collective-permute-done | bytes 262176 | tf_op jit(solution)/shard_map/grads_cross_0_0/ppermute | solution.py:370
  79.7 1.6 %shard_map.141 = (bf16[2,128,512]{2,1,0:T(8,128)(2,1)S(1)}, f32[8,128]{1,0:T(8,128)}) custom-call(f32[8,128]{1,0:T(8,128)} %get-tuple-element.100.refs_0_, f32[256,512]{1,0:T(8,128)S(1)} %collective-permute-done.14.refs_1_.refs_2_, f32[2,128,512]{2,1,0:T(8,128)} %get-tuple-element.102.refs_2_, bf16[2,128,512]{2,1,0:T(8,128)(2,1)S(1)} %collective-permute-done.15.refs_3_), custom_call_target="tpu_custom_call" | custom-call | flops 1 | bytes 1 | tf_op jit(solution)/shard_map/pallas_call | solution.py:57
  81.3 4.6 %collective-permute-start.19 = (bf16[2,128,512]{2,1,0:T(8,128)(2,1)S(1)}, bf16[2,128,512]{2,1,0:T(8,128)(2,1)S(1)}, u32[]{:S(2)}, u32[]{:S(2)}) collective-permute-start(bf16[2,128,512]{2,1,0:T(8,128)(2,1)S(1)} %get-tuple-element.112), channel_id=1, source_target_pairs={{0,16},{4,20},{8,24},{12,28},{16,0},{20,4},{24,8},{28,12},{1,17},{... | collective-permute-start | bytes 786440 | tf_op jit(solution)/shard_map/grads_far_0/ppermute | solution.py:370
  85.9 2.3 %shard_map.142 = (f32[2,128,512]{2,1,0:T(8,128)}, bf16[2,128,512]{2,1,0:T(8,128)(2,1)}, f32[1,128,512]{2,1,0:T(8,128)}, f32[1,128,512]{2,1,0:T(8,128)}, bf16[1,1...) custom-call(f32[8,128]{1,0:T(8,128)} %get-tuple-element.104.refs_0_, ...), custom_call_target="tpu_custom_call" | custom-call | flops 1 | bytes 1 | tf_op jit(solution)/shard_map/pallas_call | solution.py:57
  90.5 1.9 %collective-permute-start.20 = (bf16[1,128,512]{2,1,0:T(8,128)(2,1)}, bf16[1,128,512]{2,1,0:T(8,128)(2,1)S(1)}, u32[]{:S(2)}, u32[]{:S(2)}) collective-permute-start(bf16[1,128,512]{2,1,0:T(8,128)(2,1)} %copy-done.11), channel_id=1, source_target_pairs={{0,8},{4,12},{8,0},{12,4},{16,24},{20,28},{24,16},{28,20},{1,9},{5... | collective-permute-start | bytes 393224 | tf_op jit(solution)/shard_map/grads_cross_1_0/ppermute | solution.py:370
  92.7 1.6 %collective-permute-done.19.refs_2_.refs_5_ = bf16[2,128,512]{2,1,0:T(8,128)(2,1)S(1)} collective-permute-done((bf16[2,128,512]{2,1,0:T(8,128)(2,1)S(1)}, bf16[2,128,512]{2,1,0:T(8,128)(2,1)S(1)}, u32[]{:S(2)}, u32[]{:S(2)}) %collective-permute-start.19) | collective-permute-done | bytes 262176 | tf_op jit(solution)/shard_map/grads_far_0/ppermute | solution.py:370
  95.0 3.7 %collective-permute-done.20.refs_3_ = bf16[1,128,512]{2,1,0:T(8,128)(2,1)S(1)} collective-permute-done((bf16[1,128,512]{2,1,0:T(8,128)(2,1)}, bf16[1,128,512]{2,1,0:T(8,128)(2,1)S(1)}, u32[]{:S(2)}, u32[]{:S(2)}) %collective-permute-start.20) | collective-permute-done | bytes 131104 | tf_op jit(solution)/shard_map/grads_cross_1_0/ppermute | solution.py:370
  98.7 1.5 %shard_map.145 = (bf16[1,128,512]{2,1,0:T(8,128)(2,1)S(1)}, f32[8,128]{1,0:T(8,128)}) custom-call(f32[8,128]{1,0:T(8,128)} %get-tuple-element.107.refs_0_.refs_3_, f32[2,128,512]{2,1,0:T(8,128)S(1)} %shard_map.144.refs_1_.refs_3_, f32[1,128,512]{2,1,0:T(8,128)} %get-tuple-element.113.refs_2_, bf16[1,128,512]{2,1,0:T(8,128)(2,1)S(1)} %collective-permute-done.20.refs_3_), custom_call_target="tpu_custom_call" | custom-call | flops 1 | bytes 1 | tf_op jit(solution)/shard_map/pallas_call | solution.py:57
  101.2 1.5 %shard_map.146 = (bf16[1,128,512]{2,1,0:T(8,128)(2,1)S(1)}, f32[8,128]{1,0:T(8,128)}) custom-call(f32[8,128]{1,0:T(8,128)} %get-tuple-element.115.refs_0_, f32[2,128,512]{2,1,0:T(8,128)S(1)} %shard_map.144.refs_1_.refs_3_, f32[1,128,512]{2,1,0:T(8,128)} %get-tuple-element.116.refs_2_, bf16[1,128,512]{2,1,0:T(8,128)(2,1)S(1)} %collective-permute-done.21.refs_3_), custom_call_target="tpu_custom_call" | custom-call | flops 1 | bytes 1 | tf_op jit(solution)/shard_map/pallas_call | solution.py:57
  102.7 1.9 %collective-permute-start.24 = (bf16[1,128,512]{2,1,0:T(8,128)(2,1)S(1)}, bf16[1,128,512]{2,1,0:T(8,128)(2,1)S(1)}, u32[]{:S(2)}, u32[]{:S(2)}) collective-permute-start(bf16[1,128,512]{2,1,0:T(8,128)(2,1)S(1)} %get-tuple-element.123), channel_id=1, source_target_pairs={{0,16},{4,20},{8,24},{12,28},{16,0},{20,4},{24,8},{28,12},{1,17},{... | collective-permute-start | bytes 393224 | tf_op jit(solution)/shard_map/grads_far_1_1/ppermute | solution.py:370
  104.7 2.3 %multiply_subtract_fusion = (f32[256,512]{1,0:T(8,128)}, f32[256,512]{1,0:T(8,128)S(1)}) fusion(f32[256,512]{1,0:T(8,128)S(1)} %copy-done.12, f32[256]{0:T(256)S(1)} %fusion.1, bf16[256,512]{1,0:T(8,128)(2,1)} %collective-permute-done.17, f32[256,512]{1,0:T(8,128)S(1)} %get-tuple-element.95, f32[256,512]{1,0:T(8,128)} %collective-permute-done.12, ...), kind=kLoop, calls=%fused_computation.1 | loop fusion | flops 1310720 | bytes 3408896 | tf_op jit(solution)/shard_map/sub | solution.py:510
  107.0 2.3 %shard_map.147 = (f32[1,512,512]{2,1,0:T(8,128)}, f32[1,512,512]{2,1,0:T(8,128)}, f32[8,128]{1,0:T(8,128)}) custom-call(f32[8,128]{1,0:T(8,128)} %get-tuple-element.118.refs_0_, f32[1,512,512]{2,1,0:T(8,128)} %refs_2_.3, f32[1,512,512]{2,1,0:T(8,128)} %refs_3_.5, f32[2,128,512]{2,1,0:T(8,128)S(1)} %shard_map.144.refs_1_.refs_3_, ...), custom_call_target="tpu_custom_call" | custom-call | flops 1 | bytes 1 | tf_op jit(solution)/shard_map/pallas_call | solution.py:57
  109.5 2.1 %shard_map.148 = (f32[1,512,512]{2,1,0:T(8,128)}, f32[1,512,512]{2,1,0:T(8,128)}, f32[8,128]{1,0:T(8,128)}) custom-call(f32[8,128]{1,0:T(8,128)} %get-tuple-element.119.refs_0_, f32[256,512]{1,0:T(8,128)S(1)} %get-tuple-element.129.refs_1_, f32[1,512,512]{2,1,0:T(8,128)} %refs_2_.3, ...), custom_call_target="tpu_custom_call", output_to_operand_aliasing={{0}: (8, {}), {1}: (9, {})} | custom-call | flops 1 | bytes 1 | tf_op jit(solution)/shard_map/pallas_call | solution.py:57
  (80 shorter events, 13.4 us)
Async XLA Ops:
  0.6 21.3 %copy-start.15 = (s32[1,1,2]{2,1,0:T(1,128)S(1)}, s32[1,1,2]{2,1,0:T(1,128)}, u32[]{:S(2)}) copy-start(s32[1,1,2]{2,1,0:T(1,128)} %param.16) | copy-start | bytes 28
  1.7 31.3 %copy-start.1 = (bf16[256,512]{1,0:T(8,128)(2,1)}, bf16[256,512]{1,0:T(8,128)(2,1)S(1)}, u32[]{:S(2)}) copy-start(bf16[256,512]{1,0:T(8,128)(2,1)S(1)} %fusion.refs_0_.refs_5_) | copy-start | bytes 786436
  1.7 16.1 %collective-permute-start.4 = (bf16[256,512]{1,0:T(8,128)(2,1)S(1)}, bf16[256,512]{1,0:T(8,128)(2,1)S(1)}, u32[]{:S(2)}, u32[]{:S(2)}) collective-permute-start(bf16[256,512]{1,0:T(8,128)(2,1)S(1)} %fusion.refs_0_.refs_5_), channel_id=1, source_target_pairs={{0,16},{4,20},{8,24},{12,28},{16,0},{20,4},{24,8},{28,12},{1,17},{... | collective-permute-start | bytes 786440 | tf_op jit(solution)/shard_map/cols_far_0/ppermute | solution.py:370
  5.8 12.2 %collective-permute-start.3 = (bf16[256,512]{1,0:T(8,128)(2,1)S(1)}, bf16[256,512]{1,0:T(8,128)(2,1)S(1)}, u32[]{:S(2)}, u32[]{:S(2)}) collective-permute-start(bf16[256,512]{1,0:T(8,128)(2,1)S(1)} %fusion.refs_0_.refs_5_), channel_id=1, source_target_pairs={{0,8},{4,12},{8,0},{12,4},{16,24},{20,28},{24,16},{28,20},{1,9},{5... | collective-permute-start | bytes 786440 | tf_op jit(solution)/shard_map/cols_near_0/ppermute | solution.py:370
  9.0 13.0 %collective-permute-start.2 = (bf16[256,512]{1,0:T(8,128)(2,1)S(1)}, bf16[256,512]{1,0:T(8,128)(2,1)S(1)}, u32[]{:S(2)}, u32[]{:S(2)}) collective-permute-start(bf16[256,512]{1,0:T(8,128)(2,1)S(1)} %get-tuple-element.68.refs_4_.refs_2_), channel_id=1, source_target_pairs={{0,2},{1,3},{2,0},{3,1},{4,6},{5,7},{6,4},{7,5},{8,10},{9,11},{10,... | collective-permute-start | bytes 786440 | tf_op jit(solution)/shard_map/chip_rows/ppermute | solution.py:370
  10.5 22.5 %collective-permute-start.1 = (bf16[256,512]{1,0:T(8,128)(2,1)S(1)}, bf16[256,512]{1,0:T(8,128)(2,1)S(1)}, u32[]{:S(2)}, u32[]{:S(2)}) collective-permute-start(bf16[256,512]{1,0:T(8,128)(2,1)S(1)} %get-tuple-element.68.refs_4_.refs_2_), channel_id=1, source_target_pairs={{0,1},{1,0},{2,3},{3,2},{4,5},{5,4},{6,7},{7,6},{8,9},{9,8},{10,11... | collective-permute-start | bytes 786440 | tf_op jit(solution)/shard_map/core_rows/ppermute | solution.py:370
  10.5 11.4 %collective-permute-start = (s32[2]{0:T(128)}, s32[2]{0:T(128)S(1)}, u32[]{:S(2)}, u32[]{:S(2)}) collective-permute-start(s32[2]{0:T(128)} %bitcast.8), channel_id=1, source_target_pairs={{0,4},{4,0},{8,12},{12,8},{16,20},{20,16},{24,28},{28,24},{1,5},{5... | collective-permute-start | bytes 32 | tf_op jit(solution)/shard_map/mate_chosen/ppermute | solution.py:370
  13.7 24.8 %copy-start.13 = (s32[1024]{0:T(1024)S(1)}, s32[1024]{0:T(1024)}, u32[]{:S(2)}) copy-start(s32[1024]{0:T(1024)} %param.15) | copy-start | bytes 12292
  18.1 20.6 %copy-start.9 = (s32[1,4096]{1,0:T(1,128)S(1)}, s32[1,4096]{1,0:T(1,128)}, u32[]{:S(2)}) copy-start(s32[1,4096]{1,0:T(1,128)} %refs_3_.4) | copy-start | bytes 49156
  18.1 27.2 %copy-start.5 = (bf16[256,512]{1,0:T(8,128)(2,1)}, bf16[256,512]{1,0:T(8,128)(2,1)S(1)}, u32[]{:S(2)}) copy-start(bf16[256,512]{1,0:T(8,128)(2,1)S(1)} %shard_map.131.refs_2_) | copy-start | bytes 786436
  18.1 15.0 %collective-permute-start.5 = (bf16[256,512]{1,0:T(8,128)(2,1)S(1)}, bf16[256,512]{1,0:T(8,128)(2,1)S(1)}, u32[]{:S(2)}, u32[]{:S(2)}) collective-permute-start(bf16[256,512]{1,0:T(8,128)(2,1)S(1)} %shard_map.131.refs_2_), channel_id=1, source_target_pairs={{0,16},{4,20},{8,24},{12,28},{16,0},{20,4},{24,8},{28,12},{1,17},{... | collective-permute-start | bytes 786440 | tf_op jit(solution)/shard_map/cols_far_1/ppermute | solution.py:370
  19.4 13.6 %collective-permute-start.6 = (bf16[256,512]{1,0:T(8,128)(2,1)S(1)}, bf16[256,512]{1,0:T(8,128)(2,1)S(1)}, u32[]{:S(2)}, u32[]{:S(2)}) collective-permute-start(bf16[256,512]{1,0:T(8,128)(2,1)S(1)} %collective-permute-done.4.refs_2_.refs_7_), channel_id=1, source_target_pairs={{0,8},{4,12},{8,0},{12,4},{16,24},{20,28},{24,16},{28,20},{1,9},{5... | collective-permute-start | bytes 786440 | tf_op jit(solution)/shard_map/cols_cross_0/ppermute | solution.py:370
  22.1 23.3 %collective-permute-start.8 = (bf16[256,512]{1,0:T(8,128)(2,1)S(1)}, bf16[256,512]{1,0:T(8,128)(2,1)S(1)}, u32[]{:S(2)}, u32[]{:S(2)}) collective-permute-start(bf16[256,512]{1,0:T(8,128)(2,1)S(1)} %shard_map.131.refs_2_), channel_id=1, source_target_pairs={{0,8},{4,12},{8,0},{12,4},{16,24},{20,28},{24,16},{28,20},{1,9},{5... | collective-permute-start | bytes 786440 | tf_op jit(solution)/shard_map/cols_near_1/ppermute | solution.py:370
  22.1 16.6 %collective-permute-start.7 = (bf16[256,512]{1,0:T(8,128)(2,1)S(1)}, bf16[256,512]{1,0:T(8,128)(2,1)S(1)}, u32[]{:S(2)}, u32[]{:S(2)}) collective-permute-start(bf16[256,512]{1,0:T(8,128)(2,1)S(1)} %collective-permute-done.2.refs_2_.refs_6_.refs_4_), channel_id=1, source_target_pairs={{0,1},{1,0},{2,3},{3,2},{4,5},{5,4},{6,7},{7,6},{8,9},{9,8},{10,11... | collective-permute-start | bytes 786440 | tf_op jit(solution)/shard_map/both_rows/ppermute | solution.py:370
  35.0 10.3 %collective-permute-start.9 = (bf16[256,512]{1,0:T(8,128)(2,1)S(1)}, bf16[256,512]{1,0:T(8,128)(2,1)S(1)}, u32[]{:S(2)}, u32[]{:S(2)}) collective-permute-start(bf16[256,512]{1,0:T(8,128)(2,1)S(1)} %shard_map.135.refs_4_), channel_id=1, source_target_pairs={{0,8},{4,12},{8,0},{12,4},{16,24},{20,28},{24,16},{28,20},{1,9},{5... | collective-permute-start | bytes 786440 | tf_op jit(solution)/shard_map/cols_cross_1/ppermute | solution.py:370
  36.3 11.5 %collective-permute-start.10 = (bf16[2,256,512]{2,1,0:T(8,128)(2,1)}, bf16[2,256,512]{2,1,0:T(8,128)(2,1)}, u32[]{:S(2)}, u32[]{:S(2)}) collective-permute-start(bf16[2,256,512]{2,1,0:T(8,128)(2,1)} %get-tuple-element.74), channel_id=1, source_target_pairs={{0,4},{4,0},{8,12},{12,8},{16,20},{20,16},{24,28},{28,24},{1,5},{5... | collective-permute-start | bytes 1572872 | tf_op jit(solution)/shard_map/cols_mate_0/ppermute | solution.py:370
  47.2 14.9 %collective-permute-start.11 = (bf16[2,256,512]{2,1,0:T(8,128)(2,1)S(1)}, bf16[2,256,512]{2,1,0:T(8,128)(2,1)S(1)}, u32[]{:S(2)}, u32[]{:S(2)}) collective-permute-start(bf16[2,256,512]{2,1,0:T(8,128)(2,1)S(1)} %get-tuple-element.84), channel_id=1, source_target_pairs={{0,4},{4,0},{8,12},{12,8},{16,20},{20,16},{24,28},{28,24},{1,5},{5... | collective-permute-start | bytes 1572872 | tf_op jit(solution)/shard_map/cols_mate_1/ppermute | solution.py:370
  51.7 17.9 %collective-permute-start.13 = (bf16[2,256,512]{2,1,0:T(8,128)(2,1)}, bf16[2,256,512]{2,1,0:T(8,128)(2,1)S(1)}, u32[]{:S(2)}, u32[]{:S(2)}) collective-permute-start(bf16[2,256,512]{2,1,0:T(8,128)(2,1)} %get-tuple-element.99), channel_id=1, source_target_pairs={{0,4},{4,0},{8,12},{12,8},{16,20},{20,16},{24,28},{28,24},{1,5},{5... | collective-permute-start | bytes 1572872 | tf_op jit(solution)/shard_map/grads_mate_0/ppermute | solution.py:370
  66.1 19.9 %copy-start.3 = (f32[2,256,512]{2,1,0:T(8,128)S(1)}, f32[2,256,512]{2,1,0:T(8,128)}, u32[]{:S(2)}) copy-start(f32[2,256,512]{2,1,0:T(8,128)} %get-tuple-element.105.refs_2_) | copy-start | bytes 3145732
  66.1 13.6 %collective-permute-start.14 = (f32[256,512]{1,0:T(8,128)}, f32[256,512]{1,0:T(8,128)S(1)}, u32[]{:S(2)}, u32[]{:S(2)}) collective-permute-start(f32[256,512]{1,0:T(8,128)} %get-tuple-element.101), channel_id=1, source_target_pairs={{0,1},{1,0},{2,3},{3,2},{4,5},{5,4},{6,7},{7,6},{8,9},{9,8},{10,11... | collective-permute-start | bytes 1572872 | tf_op jit(solution)/shard_map/row_grads_both/ppermute | solution.py:370
  66.1 19.8 %collective-permute-start.16 = (bf16[2,256,512]{2,1,0:T(8,128)(2,1)}, bf16[2,256,512]{2,1,0:T(8,128)(2,1)}, u32[]{:S(2)}, u32[]{:S(2)}) collective-permute-start(bf16[2,256,512]{2,1,0:T(8,128)(2,1)} %get-tuple-element.106), channel_id=1, source_target_pairs={{0,4},{4,0},{8,12},{12,8},{16,20},{20,16},{24,28},{28,24},{1,5},{5... | collective-permute-start | bytes 1572872 | tf_op jit(solution)/shard_map/grads_mate_1/ppermute | solution.py:370
  71.6 23.3 %copy-start = (f32[2,128,512]{2,1,0:T(8,128)S(1)}, f32[2,128,512]{2,1,0:T(8,128)}, u32[]{:S(2)}) copy-start(f32[2,128,512]{2,1,0:T(8,128)} %get-tuple-element.110.refs_0_) | copy-start | bytes 1572868
  71.6 8.0 %collective-permute-start.15 = (bf16[2,128,512]{2,1,0:T(8,128)(2,1)S(1)}, bf16[2,128,512]{2,1,0:T(8,128)(2,1)S(1)}, u32[]{:S(2)}, u32[]{:S(2)}) collective-permute-start(bf16[2,128,512]{2,1,0:T(8,128)(2,1)S(1)} %get-tuple-element.103), channel_id=1, source_target_pairs={{0,8},{4,12},{8,0},{12,4},{16,24},{20,28},{24,16},{28,20},{1,9},{5... | collective-permute-start | bytes 786440 | tf_op jit(solution)/shard_map/grads_cross_0_0/ppermute | solution.py:370
  73.0 31.7 %collective-permute-start.12 = (f32[256,512]{1,0:T(8,128)}, f32[256,512]{1,0:T(8,128)}, u32[]{:S(2)}, u32[]{:S(2)}) collective-permute-start(f32[256,512]{1,0:T(8,128)} %get-tuple-element.96), channel_id=1, source_target_pairs={{0,1},{1,0},{2,3},{3,2},{4,5},{5,4},{6,7},{7,6},{8,9},{9,8},{10,11... | collective-permute-start | bytes 1572872 | tf_op jit(solution)/shard_map/row_grads_core/ppermute | solution.py:370
  73.0 19.5 %collective-permute-start.18 = (bf16[2,128,512]{2,1,0:T(8,128)(2,1)}, bf16[2,128,512]{2,1,0:T(8,128)(2,1)S(1)}, u32[]{:S(2)}, u32[]{:S(2)}) collective-permute-start(bf16[2,128,512]{2,1,0:T(8,128)(2,1)} %get-tuple-element.111), channel_id=1, source_target_pairs={{0,8},{4,12},{8,0},{12,4},{16,24},{20,28},{24,16},{28,20},{1,9},{5... | collective-permute-start | bytes 786440 | tf_op jit(solution)/shard_map/grads_near_0/ppermute | solution.py:370
  81.3 13.0 %collective-permute-start.19 = (bf16[2,128,512]{2,1,0:T(8,128)(2,1)S(1)}, bf16[2,128,512]{2,1,0:T(8,128)(2,1)S(1)}, u32[]{:S(2)}, u32[]{:S(2)}) collective-permute-start(bf16[2,128,512]{2,1,0:T(8,128)(2,1)S(1)} %get-tuple-element.112), channel_id=1, source_target_pairs={{0,16},{4,20},{8,24},{12,28},{16,0},{20,4},{24,8},{28,12},{1,17},{... | collective-permute-start | bytes 786440 | tf_op jit(solution)/shard_map/grads_far_0/ppermute | solution.py:370
  88.9 15.8 %collective-permute-start.17 = (bf16[256,512]{1,0:T(8,128)(2,1)S(1)}, bf16[256,512]{1,0:T(8,128)(2,1)}, u32[]{:S(2)}, u32[]{:S(2)}) collective-permute-start(bf16[256,512]{1,0:T(8,128)(2,1)S(1)} %get-tuple-element.109), channel_id=1, source_target_pairs={{0,2},{1,3},{2,0},{3,1},{4,6},{5,7},{6,4},{7,5},{8,10},{9,11},{10,... | collective-permute-start | bytes 786440 | tf_op jit(solution)/shard_map/row_grads_chip/ppermute | solution.py:370
  90.5 8.1 %collective-permute-start.20 = (bf16[1,128,512]{2,1,0:T(8,128)(2,1)}, bf16[1,128,512]{2,1,0:T(8,128)(2,1)S(1)}, u32[]{:S(2)}, u32[]{:S(2)}) collective-permute-start(bf16[1,128,512]{2,1,0:T(8,128)(2,1)} %copy-done.11), channel_id=1, source_target_pairs={{0,8},{4,12},{8,0},{12,4},{16,24},{20,28},{24,16},{28,20},{1,9},{5... | collective-permute-start | bytes 393224 | tf_op jit(solution)/shard_map/grads_cross_1_0/ppermute | solution.py:370
  92.5 8.7 %collective-permute-start.21 = (bf16[1,128,512]{2,1,0:T(8,128)(2,1)}, bf16[1,128,512]{2,1,0:T(8,128)(2,1)S(1)}, u32[]{:S(2)}, u32[]{:S(2)}) collective-permute-start(bf16[1,128,512]{2,1,0:T(8,128)(2,1)} %copy-done.10), channel_id=1, source_target_pairs={{0,8},{4,12},{8,0},{12,4},{16,24},{20,28},{24,16},{28,20},{1,9},{5... | collective-permute-start | bytes 393224 | tf_op jit(solution)/shard_map/grads_cross_1_1/ppermute | solution.py:370
  94.3 15.0 %collective-permute-start.22 = (bf16[2,128,512]{2,1,0:T(8,128)(2,1)}, bf16[2,128,512]{2,1,0:T(8,128)(2,1)S(1)}, u32[]{:S(2)}, u32[]{:S(2)}) collective-permute-start(bf16[2,128,512]{2,1,0:T(8,128)(2,1)} %get-tuple-element.121), channel_id=1, source_target_pairs={{0,8},{4,12},{8,0},{12,4},{16,24},{20,28},{24,16},{28,20},{1,9},{5... | collective-permute-start | bytes 786440 | tf_op jit(solution)/shard_map/grads_near_1/ppermute | solution.py:370
  100.2 9.1 %collective-permute-start.23 = (bf16[1,128,512]{2,1,0:T(8,128)(2,1)S(1)}, bf16[1,128,512]{2,1,0:T(8,128)(2,1)S(1)}, u32[]{:S(2)}, u32[]{:S(2)}) collective-permute-start(bf16[1,128,512]{2,1,0:T(8,128)(2,1)S(1)} %get-tuple-element.122), channel_id=1, source_target_pairs={{0,16},{4,20},{8,24},{12,28},{16,0},{20,4},{24,8},{28,12},{1,17},{... | collective-permute-start | bytes 393224 | tf_op jit(solution)/shard_map/grads_far_1_0/ppermute | solution.py:370
  102.7 6.7 %collective-permute-start.24 = (bf16[1,128,512]{2,1,0:T(8,128)(2,1)S(1)}, bf16[1,128,512]{2,1,0:T(8,128)(2,1)S(1)}, u32[]{:S(2)}, u32[]{:S(2)}) collective-permute-start(bf16[1,128,512]{2,1,0:T(8,128)(2,1)S(1)} %get-tuple-element.123), channel_id=1, source_target_pairs={{0,16},{4,20},{8,24},{12,28},{16,0},{20,4},{24,8},{28,12},{1,17},{... | collective-permute-start | bytes 393224 | tf_op jit(solution)/shard_map/grads_far_1_1/ppermute | solution.py:370
  (9 other events, 75.5 us)
